TPU v7x, 32 devices: a whole 2x2x4 slice. The times are simulated.
32 devices in a mesh: groups: 2 (over y), seq: 4 (over z), head: 2 (over x), prompt: 2 (over core).
Axes of the slice: x: 2, y: 2, z: 4, core: 2. Of those that a mesh axis runs over, the one named last changes fastest.
Arguments:
- prompt_queries: bfloat16 [4, 512, 2048], P(('groups', 'prompt'), 'seq', 'head'), parts along dimension 0, may hold values from -6 to 6
- prompt_keys: bfloat16 [4, 512, 2048], P(('groups', 'prompt'), 'seq', 'head'), parts along dimension 0, may hold values from -20 to 20
- prompt_values: bfloat16 [4, 512, 4096], P(('groups', 'prompt'), 'seq', 'head'), parts along dimension 0, may hold values from -6 to 6
- prompt_beta: float32 [4, 32, 512], P(('groups', 'prompt'), 'head', 'seq'), parts along dimension 0, may hold values from 0.005 to 0.15
- prompt_decay: float32 [4, 32, 512], P(('groups', 'prompt'), 'head', 'seq'), parts along dimension 0, may hold values from -0.7 to 0
- suffix_queries: bfloat16 [32, 256, 2048], P(('groups', 'seq', 'prompt'), None, 'head'), parts along dimension 0, may hold values from -6 to 6
- suffix_keys: bfloat16 [32, 256, 2048], P(('groups', 'seq', 'prompt'), None, 'head'), parts along dimension 0, may hold values from -20 to 20
- suffix_values: bfloat16 [32, 256, 4096], P(('groups', 'seq', 'prompt'), None, 'head'), parts along dimension 0, may hold values from -6 to 6
- suffix_beta: float32 [32, 32, 256], P(('groups', 'seq', 'prompt'), 'head'), parts along dimension 0, may hold values from 0.005 to 0.15
- suffix_decay: float32 [32, 32, 256], P(('groups', 'seq', 'prompt'), 'head'), parts along dimension 0, may hold values from -0.2 to 0
- norm_gain: float32 [128], replicated, may hold values from 0.25 to 1.75
- slot_branch: int32 [32], P('groups'), parts along dimension 0, may hold values from 0 to 15, each once
- branch_length: int32 [32], P('groups'), parts along dimension 0, may hold values from 1 to 256, 2048 in all
- branch_prompt: int32 [32], P('groups'), parts along dimension 0, may hold values from 0 to 1
Outputs:
- prompt_out: bfloat16 [4, 512, 4096], P(('groups', 'prompt'), 'seq', 'head'), parts along dimension 0
- suffix_out: bfloat16 [32, 256, 4096], P(('groups', 'seq', 'prompt'), None, 'head'), parts along dimension 0
There are 2 independent parts, one for each index of `groups`. A program takes and returns all parts, laid end to end along the dimension named above; an argument that names none is the same for every part. Nothing has to cross between parts.
Inputs may be any that keep to these rules, and one draw needn't show every extreme that they name: slot_branch names every branch exactly once. `branch_length`: the lengths sum to 2048 and one of them is exactly 256.
All inputs are finite; a program needn't handle non-finite values.
Results may differ from a plain program's by a relative error of at most 0.0067.
Values sent between devices are 32-bit elements; how exact they have to be, the bound alone decides.
No kernel may reach another device: no remote copies, remote signals or barrier semaphores. Data moves between devices by JAX's collectives and lax.ppermute only.
A program may use at most 128 MiB of HBM per device.

v0:
```python
import functools

import jax
import jax.numpy as jnp
from jax import lax
from jax.experimental import pallas as pl
from jax.experimental.pallas import tpu as pltpu
from jax.sharding import PartitionSpec as P

DK = 128
DV = 128
CH = 128
W2 = 2 * DV
EPS_NORM = 1e-06
HIGH = lax.Precision.HIGHEST
VMEM = 56 * 1024 * 1024


def mm(left, right):
    return lax.dot_general(left, right, (((1,), (0,)), ((), ())), preferred_element_type=jnp.float32)


def diag2(pair):
    zero = jnp.zeros((pair.shape[0], DV), pair.dtype)
    top = jnp.concatenate([pair[:, :DV], zero], axis=1)
    low = jnp.concatenate([zero, pair[:, DV:]], axis=1)
    return jnp.concatenate([top, low], axis=0)


def low16(value):
    return value.astype(jnp.bfloat16)


def lanes2(col_a, col_b):
    shape = (col_a.shape[0], DV)
    return jnp.concatenate(
        [jnp.broadcast_to(col_a, shape), jnp.broadcast_to(col_b, shape)], axis=1
    )


def unit_rows(vectors):
    wide = vectors.astype(jnp.float32)
    factor = lax.rsqrt(jnp.sum(wide * wide, axis=-1, keepdims=True) + EPS_NORM)
    return low16(wide * factor)


def apply_pair(transfer, state, offset):
    t_hi = low16(transfer)
    t_lo = low16(transfer - t_hi.astype(jnp.float32))
    s_hi = low16(state)
    s_lo = low16(state - s_hi.astype(jnp.float32))
    hi = diag2(s_hi)
    return mm(t_hi, hi) + mm(t_lo, hi) + mm(t_hi, diag2(s_lo)) + offset


def gate_tables(beta, decay):
    rows = lax.broadcasted_iota(jnp.int32, (CH, CH), 0)
    cols = lax.broadcasted_iota(jnp.int32, (CH, CH), 1)
    upper = jnp.where(rows <= cols, 1.0, 0.0).astype(jnp.float32)
    cum = lax.dot_general(
        decay, upper, (((1,), (0,)), ((), ())), precision=HIGH, preferred_element_type=jnp.float32
    )
    return beta.T, cum, cum.T


def chunk_terms(chains):
    rows = lax.broadcasted_iota(jnp.int32, (CH, W2), 0)
    cols = jnp.bitwise_and(lax.broadcasted_iota(jnp.int32, (CH, W2), 1), CH - 1)
    causal = rows >= cols
    strict = rows > cols
    eye = jnp.where(rows == cols, 1.0, 0.0).astype(jnp.float32)
    apart = jnp.bitwise_xor(rows, cols)
    near = strict & (apart < 8)

    state = []
    for q, k, v, beta_c, cum_r, cum_c in chains:
        qn = unit_rows(q)
        kn = unit_rows(k)
        kf = kn.astype(jnp.float32)
        kt = kf.T
        state.append((qn, kn, kf, kt))
    grams = [mm(jnp.concatenate([kn, qn], axis=0), low16(kt)) for qn, kn, kf, kt in state]
    lows, attns = [], []
    for (q, k, v, beta_c, cum_r, cum_c), gram in zip(chains, grams):
        kk = gram[:CH]
        qk = gram[CH:]
        row = jnp.concatenate([cum_r[0:1], cum_r[1:2]], axis=1)
        ratio = jnp.exp(jnp.where(causal, lanes2(cum_c[:, 0:1], cum_c[:, 1:2]) - row, -1e30))
        scaled = lanes2(beta_c[:, 0:1], beta_c[:, 1:2]) * ratio
        lows.append(jnp.where(strict, scaled * jnp.concatenate([kk, kk], axis=1), 0.0))
        attns.append(low16(ratio * jnp.concatenate([qk, qk], axis=1)))
    lows16 = [low16(low) for low in lows]
    nil = [jnp.where(near, -low, 0.0) for low in lows]
    nil16 = [low16(n) for n in nil]
    sq = [low16(mm(n, diag2(n))) for n in nil16]
    base = [eye + n for n in nil]
    both = [mm(jnp.concatenate([s, low16(b)], axis=0), diag2(s)) for s, b in zip(sq, base)]
    base = [b + x[CH:] for b, x in zip(base, both)]
    inv = [b + mm(low16(b), diag2(low16(x[:CH]))) for b, x in zip(base, both)]
    for level in (3, 4, 5, 6):
        here = lax.shift_right_logical(apart, level) == 1
        inv16 = [low16(i) for i in inv]
        mid = [
            low16(mm(jnp.where(here, low, jnp.zeros_like(low)), diag2(i)))
            for low, i in zip(lows16, inv16)
        ]
        inv = [i - mm(i16, diag2(m)) for i, i16, m in zip(inv, inv16, mid)]
    out = []
    stage = []
    for (q, k, v, beta_c, cum_r, cum_c), (qn, kn, kf, kt), i in zip(chains, state, inv):
        grow = jnp.exp(cum_c)
        bg = beta_c * grow
        i16 = low16(i)
        kf2 = jnp.concatenate([kf, kf], axis=1)
        w = mm(i16, diag2(low16(kf2 * lanes2(bg[:, 0:1], bg[:, 1:2]))))
        u = mm(i16, diag2(low16(v.astype(jnp.float32) * lanes2(beta_c[:, 0:1], beta_c[:, 1:2]))))
        stage.append((grow, low16(w), low16(u)))
    for (q, k, v, beta_c, cum_r, cum_c), (qn, kn, kf, kt), attn, (grow, w, u) in zip(
        chains, state, attns, stage
    ):
        last = cum_r[:, CH - 1 : CH]
        tail = jnp.exp(last - cum_r)
        tail_k = low16(
            jnp.concatenate([kt, kt], axis=1) * jnp.concatenate([tail[0:1], tail[1:2]], axis=1)
        )
        left = jnp.concatenate([attn, tail_k], axis=0)
        by_w = mm(left, diag2(w))
        by_u = mm(left, diag2(u))
        qf = qn.astype(jnp.float32)
        a = jnp.concatenate([qf, qf], axis=1) * lanes2(grow[:, 0:1], grow[:, 1:2]) - by_w[:CH]
        end = jnp.exp(last)
        shrink = jnp.concatenate(
            [jnp.broadcast_to(end[0:1], (1, DV)), jnp.broadcast_to(end[1:2], (1, DV))], axis=1
        )
        out.append((a, by_u[:CH], eye * shrink - by_w[CH:], by_u[CH:]))
    return out


def prompt_kernel(first, pairs, q_ref, k_ref, v_ref, beta_ref, decay_ref, to_ref, a_ref, b_ref):
    heads = slice(2 * first, 2 * (first + pairs))
    beta_c, cum_r, cum_c = gate_tables(beta_ref[0, heads, :], decay_ref[0, heads, :])
    chains = []
    for p in range(pairs):
        chains.append(
            (
                q_ref[0, :, p * DK : (p + 1) * DK],
                k_ref[0, :, p * DK : (p + 1) * DK],
                v_ref[0, :, p * W2 : (p + 1) * W2],
                beta_c[:, 2 * p : 2 * p + 2],
                cum_r[2 * p : 2 * p + 2],
                cum_c[:, 2 * p : 2 * p + 2],
            )
        )
    for p, (a, b, transfer, offset) in enumerate(chunk_terms(chains)):
        a_ref[:, p * W2 : (p + 1) * W2] = low16(a)
        b_ref[:, p * W2 : (p + 1) * W2] = b
        to_ref[0, p] = transfer
        to_ref[1, p] = offset


def prompt_terms(first, pairs, q, k, v, beta, decay):
    at = first // pairs
    return pl.pallas_call(
        functools.partial(prompt_kernel, first, pairs),
        grid=(1,),
        in_specs=[
            pl.BlockSpec((1, CH, pairs * DK), lambda i: (0, 0, at)),
            pl.BlockSpec((1, CH, pairs * DK), lambda i: (0, 0, at)),
            pl.BlockSpec((1, CH, pairs * W2), lambda i: (0, 0, at)),
            pl.BlockSpec(beta.shape, lambda i: (0, 0, 0)),
            pl.BlockSpec(decay.shape, lambda i: (0, 0, 0)),
        ],
        out_specs=[
            pl.BlockSpec((2, pairs, DK, W2), lambda i: (0, 0, 0, 0)),
            pl.BlockSpec((CH, pairs * W2), lambda i: (0, 0)),
            pl.BlockSpec((CH, pairs * W2), lambda i: (0, 0)),
        ],
        out_shape=[
            jax.ShapeDtypeStruct((2, pairs, DK, W2), jnp.float32),
            jax.ShapeDtypeStruct((CH, pairs * W2), jnp.bfloat16),
            jax.ShapeDtypeStruct((CH, pairs * W2), jnp.float32),
        ],
        compiler_params=pltpu.CompilerParams(vmem_limit_bytes=VMEM),
        name="prompt_terms",
    )(q, k, v, beta, decay)


def suffix_kernel(first, unit, q_ref, k_ref, v_ref, beta_ref, decay_ref, a_ref, b_ref):
    spans = q_ref.shape[1] // CH
    heads = slice(2 * first, 2 * (first + unit))
    chains = []
    for s in range(spans):
        at = slice(s * CH, (s + 1) * CH)
        beta_c, cum_r, cum_c = gate_tables(beta_ref[0, heads, at], decay_ref[0, heads, at])
        for p in range(unit):
            chains.append(
                (
                    q_ref[0, at, p * DK : (p + 1) * DK],
                    k_ref[0, at, p * DK : (p + 1) * DK],
                    v_ref[0, at, p * W2 : (p + 1) * W2],
                    beta_c[:, 2 * p : 2 * p + 2],
                    cum_r[2 * p : 2 * p + 2],
                    cum_c[:, 2 * p : 2 * p + 2],
                )
            )
    terms = chunk_terms(chains)
    for p in range(unit):
        lanes = slice(p * W2, (p + 1) * W2)
        a, b, transfer, offset = terms[p]
        a_ref[0, 0:CH, lanes] = low16(a)
        b_ref[0, 0:CH, lanes] = b
        for s in range(1, spans):
            a, b, t_next, o_next = terms[s * unit + p]
            a16 = low16(a)
            at = slice(s * CH, (s + 1) * CH)
            d_t = diag2(low16(transfer))
            d_o = diag2(low16(offset))
            a_ref[0, at, lanes] = low16(mm(a16, d_t))
            b_ref[0, at, lanes] = mm(a16, d_o) + b
            if s + 1 < spans:
                t16 = low16(t_next)
                transfer, offset = mm(t16, d_t), mm(t16, d_o) + o_next


def suffix_terms(first, pairs, unit, q, k, v, beta, decay):
    slots, tokens = q.shape[0], q.shape[1]
    calls = []
    for part in range(0, pairs, unit):
        at = (first + part) // unit
        calls.append(
            pl.pallas_call(
                functools.partial(suffix_kernel, first + part, unit),
                grid=(slots,),
                in_specs=[
                    pl.BlockSpec((1, tokens, unit * DK), lambda i, at=at: (i, 0, at)),
                    pl.BlockSpec((1, tokens, unit * DK), lambda i, at=at: (i, 0, at)),
                    pl.BlockSpec((1, tokens, unit * W2), lambda i, at=at: (i, 0, at)),
                    pl.BlockSpec((1,) + beta.shape[1:], lambda i: (i, 0, 0)),
                    pl.BlockSpec((1,) + decay.shape[1:], lambda i: (i, 0, 0)),
                ],
                out_specs=[
                    pl.BlockSpec((1, tokens, unit * W2), lambda i: (i, 0, 0)),
                    pl.BlockSpec((1, tokens, unit * W2), lambda i: (i, 0, 0)),
                ],
                out_shape=[
                    jax.ShapeDtypeStruct((slots, tokens, unit * W2), jnp.bfloat16),
                    jax.ShapeDtypeStruct((slots, tokens, unit * W2), jnp.float32),
                ],
                compiler_params=pltpu.CompilerParams(vmem_limit_bytes=VMEM),
                name="suffix_terms",
            )(q, k, v, beta, decay)
        )
    return calls


def step_kernel(pairs, to_ref, s_ref, out_ref):
    for p in range(pairs):
        out_ref[p] = apply_pair(to_ref[0, p], s_ref[p], to_ref[1, p])


def step(to, state):
    pairs = state.shape[0]
    return pl.pallas_call(
        functools.partial(step_kernel, pairs),
        out_shape=jax.ShapeDtypeStruct(state.shape, jnp.float32),
        compiler_params=pltpu.CompilerParams(vmem_limit_bytes=VMEM),
        name="state_step",
    )(to, state)


def step2_kernel(pairs, to_ref, far_ref, s_ref, out_ref, final_ref):
    for p in range(pairs):
        state = apply_pair(to_ref[0, p], s_ref[p], to_ref[1, p])
        out_ref[p] = state
        final_ref[p] = apply_pair(far_ref[0, p], state, far_ref[1, p])


def step2(to, far, state):
    pairs = state.shape[0]
    shape = jax.ShapeDtypeStruct(state.shape, jnp.float32)
    return pl.pallas_call(
        functools.partial(step2_kernel, pairs),
        out_shape=[shape, shape],
        compiler_params=pltpu.CompilerParams(vmem_limit_bytes=VMEM),
        name="state_step_twice",
    )(to, far, state)


def finish(a, state, b, gain2):
    raw = mm(a, diag2(low16(state))) + b
    sq = raw * raw
    parts = []
    for h in range(2):
        lanes = slice(h * DV, (h + 1) * DV)
        inv = lax.rsqrt(jnp.mean(sq[:, lanes], axis=-1, keepdims=True) + EPS_NORM)
        parts.append(raw[:, lanes] * inv)
    return jnp.concatenate(parts, axis=1) * gain2


def suffix_out_kernel(unit, slots, n_prompt, *refs):
    sb_ref, bl_ref, bp_ref, own_ref, other_ref, a_ref, b_ref, gain_ref = refs[:8]
    out_ref = refs[-1]
    me = lax.axis_index("prompt")
    rank = lax.axis_index("seq") * n_prompt + me
    branch = sb_ref[rank * slots + pl.program_id(0)]
    length = bl_ref[branch]
    mine = bp_ref[branch] == me
    gain = gain_ref[...]
    gain2 = jnp.concatenate([gain, gain], axis=1)
    tokens = a_ref.shape[1]
    live = lax.broadcasted_iota(jnp.int32, (tokens, W2), 0) < length
    for p in range(unit):
        lanes = slice(p * W2, (p + 1) * W2)
        state = jnp.where(mine, own_ref[p], other_ref[p])
        out = finish(a_ref[0, :, lanes], state, b_ref[0, :, lanes], gain2)
        out_ref[0, :, lanes] = low16(jnp.where(live, out, 0.0))


def suffix_outputs(first, index, tables, own, other, a, b, gain, so_far, width):
    slots, tokens, lanes = a.shape
    unit = lanes // W2
    at = first // unit
    smem = pl.BlockSpec(memory_space=pltpu.SMEM)
    in_specs = [
        smem,
        smem,
        smem,
        pl.BlockSpec((unit, DK, W2), lambda i: (index, 0, 0)),
        pl.BlockSpec((unit, DK, W2), lambda i: (index, 0, 0)),
        pl.BlockSpec((1, tokens, lanes), lambda i: (i, 0, 0)),
        pl.BlockSpec((1, tokens, lanes), lambda i: (i, 0, 0)),
        pl.BlockSpec((1, DV), lambda i: (0, 0)),
    ]
    args = list(tables) + [own, other, a, b, gain]
    aliases = {}
    if so_far is not None:
        in_specs.append(pl.BlockSpec(memory_space=pl.ANY))
        args.append(so_far)
        aliases = {8: 0}
    return pl.pallas_call(
        functools.partial(suffix_out_kernel, unit, slots, lax.axis_size("prompt")),
        grid=(slots,),
        in_specs=in_specs,
        out_specs=pl.BlockSpec((1, tokens, lanes), lambda i: (i, 0, at)),
        out_shape=jax.ShapeDtypeStruct((slots, tokens, width), jnp.bfloat16),
        input_output_aliases=aliases,
        compiler_params=pltpu.CompilerParams(vmem_limit_bytes=VMEM),
        name="suffix_out",
    )(*args)


def prompt_out_kernel(pairs, s_ref, a_ref, b_ref, gain_ref, *refs):
    out_ref = refs[-1]
    gain = gain_ref[...]
    gain2 = jnp.concatenate([gain, gain], axis=1)
    for p in range(pairs):
        lanes = slice(p * W2, (p + 1) * W2)
        out_ref[0, :, lanes] = low16(finish(a_ref[:, lanes], s_ref[p], b_ref[:, lanes], gain2))


def prompt_outputs(first, state, a, b, gain, so_far, width):
    pairs = state.shape[0]
    at = first // pairs
    in_specs = [
        pl.BlockSpec(state.shape, lambda i: (0, 0, 0)),
        pl.BlockSpec(a.shape, lambda i: (0, 0)),
        pl.BlockSpec(b.shape, lambda i: (0, 0)),
        pl.BlockSpec((1, DV), lambda i: (0, 0)),
    ]
    args = [state, a, b, gain]
    aliases = {}
    if so_far is not None:
        in_specs.append(pl.BlockSpec(memory_space=pl.ANY))
        args.append(so_far)
        aliases = {4: 0}
    return pl.pallas_call(
        functools.partial(prompt_out_kernel, pairs),
        grid=(1,),
        in_specs=in_specs,
        out_specs=pl.BlockSpec((1, CH, pairs * W2), lambda i: (0, 0, at)),
        out_shape=jax.ShapeDtypeStruct((1, CH, width), jnp.bfloat16),
        input_output_aliases=aliases,
        compiler_params=pltpu.CompilerParams(vmem_limit_bytes=VMEM),
        name="prompt_out",
    )(*args)


def pair_product(left, right):
    pairs = left.shape[0]
    left = left.reshape(pairs, DK, 2, DK)
    right = right.reshape(pairs, DK, 2, DV)
    return jnp.einsum("pihj,pjhv->pihv", left, right, precision=HIGH).reshape(pairs, DK, W2)


def exchange(to):
    count = lax.axis_size("seq")
    half = count // 2
    here = lax.axis_index("seq")
    sending = to
    far = None
    for j in range(half - 1):
        arrived = lax.ppermute(sending, "seq", [(j, j + 1), (count - 1 - j, count - 2 - j)])
        far = arrived if far is None else far + arrived
        prefix = step(to, arrived[1])
        if j + 2 < half:
            joined = jnp.stack(
                [pair_product(arrived[0], to[0]), pair_product(arrived[0], to[1]) + arrived[1]]
            )
            sending = jnp.where(here < half, jnp.stack([prefix, prefix]), joined)
    middle = lax.ppermute(prefix, "seq", [(half - 1, half)])
    state_out, final_mid = step2(to, far, middle)
    back = lax.ppermute(final_mid, "seq", [(half, half - 1)])
    incoming = jnp.where(here == half, middle, jnp.where(here < half, far[1], 0.0))
    final = jnp.where(here == half, final_mid, back)
    left_out = back
    for j in range(half - 1):
        arrived = lax.ppermute(
            jnp.where(here < half, left_out, state_out),
            "seq",
            [(half - 1 - j, half - 2 - j), (half + j, half + j + 1)],
        )
        state_out = step(to, arrived)
        left_out = arrived
        right = here == half + j + 1
        if j + 2 < half:
            right_final = pair_product(far[0], state_out) + far[1]
        else:
            right_final = state_out
        incoming = jnp.where(right, arrived, incoming)
        final = jnp.where(right, right_final, jnp.where(here == half - 2 - j, arrived, final))
    return incoming, final


def split_pairs(pairs):
    half = max(1, pairs // 2)
    return (half,) * (pairs // half)


def local(
    prompt_queries,
    prompt_keys,
    prompt_values,
    prompt_beta,
    prompt_decay,
    suffix_queries,
    suffix_keys,
    suffix_values,
    suffix_beta,
    suffix_decay,
    norm_gain,
    slot_branch,
    branch_length,
    branch_prompt,
):
    gain = norm_gain.reshape(1, DV)
    tables = (slot_branch, branch_length, branch_prompt)
    prompts = lax.axis_size("prompt")
    groups = split_pairs(prompt_values.shape[2] // W2)
    terms = []
    first = 0
    for pairs in groups:
        terms.append(
            prompt_terms(
                first, pairs, prompt_queries, prompt_keys, prompt_values, prompt_beta, prompt_decay
            )
        )
        first += pairs
    states = [exchange(to) for to, a, b in terms]
    prompt_out, suffix_out = None, None
    first = 0
    for pairs, (to, a, b), (incoming, final) in zip(groups, terms, states):
        other = lax.ppermute(final, "prompt", [(i, (i + 1) % prompts) for i in range(prompts)])
        unit = min(2, pairs)
        calls = suffix_terms(
            first,
            pairs,
            unit,
            suffix_queries,
            suffix_keys,
            suffix_values,
            suffix_beta,
            suffix_decay,
        )
        prompt_out = prompt_outputs(
            first, incoming, a, b, gain, prompt_out, prompt_values.shape[2]
        )
        for index, (a, b) in enumerate(calls):
            suffix_out = suffix_outputs(
                first + index * unit,
                index,
                tables,
                final,
                other,
                a,
                b,
                gain,
                suffix_out,
                suffix_values.shape[2],
            )
        first += pairs
    return (prompt_out, suffix_out)


def solution(mesh):
    return jax.shard_map(
        local,
        mesh=mesh,
        in_specs=(
            P(("groups", "prompt"), "seq", "head"),
            P(("groups", "prompt"), "seq", "head"),
            P(("groups", "prompt"), "seq", "head"),
            P(("groups", "prompt"), "head", "seq"),
            P(("groups", "prompt"), "head", "seq"),
            P(("groups", "seq", "prompt"), None, "head"),
            P(("groups", "seq", "prompt"), None, "head"),
            P(("groups", "seq", "prompt"), None, "head"),
            P(("groups", "seq", "prompt"), "head", None),
            P(("groups", "seq", "prompt"), "head", None),
            P(),
            P("groups"),
            P("groups"),
            P("groups"),
        ),
        out_specs=(
            P(("groups", "prompt"), "seq", "head"),
            P(("groups", "seq", "prompt"), None, "head"),
        ),
        check_vma=False,
    )
```

profile of v0, /device:TPU:0, one launch (start us, length us, event | category | flops | bytes accessed | tf_op | source)
XLA Modules:
  0.0 167.3 jit_solution(7856355328732046530)
XLA Ops:
  0.6 5.7 %prompt_terms.3 = (f32[2,4,128,256]{3,2,1,0:T(8,128)}, bf16[128,1024]{1,0:T(8,128)(2,1)}, f32[128,1024]{1,0:T(8,128)}) custom-call(bf16[1,128,1024]{2,1,0:T(8,128)(2,1)} %q_ref.7, bf16[1,128,1024]{2,1,0:T(8,128)(2,1)} %k_ref.7, bf16[1,128,2048]{2,1,0:T(8,128)(2,1)} %v_ref.7, f32[1,16,128]{2,1,0:T(8,128)} %beta_ref.7, f32[1,16,128]{2,1,0:T(8,128)} %decay_ref.7), custom_call_target="tpu_custom_call" | custom-call | tf_op jit(solution)/shard_map/prompt_terms/pallas_call | solution.py:163
  6.3 5.0 %collective-permute-start.4 = (f32[2,4,128,256]{3,2,1,0:T(8,128)}, f32[2,4,128,256]{3,2,1,0:T(8,128)S(1)}, u32[]{:S(2)}, u32[]{:S(2)}) collective-permute-start(f32[2,4,128,256]{3,2,1,0:T(8,128)} %get-tuple-element.25.to_ref), channel_id=1, source_target_pairs={{0,4},{12,8},{1,5},{13,9},{2,6},{14,10},{3,7},{15,11},{16,20},{28,... | collective-permute-start | bytes 3145736 | tf_op jit(solution)/shard_map/ppermute | solution.py:402
  11.3 5.7 %prompt_terms.2 = (f32[2,4,128,256]{3,2,1,0:T(8,128)}, bf16[128,1024]{1,0:T(8,128)(2,1)}, f32[128,1024]{1,0:T(8,128)}) custom-call(bf16[1,128,1024]{2,1,0:T(8,128)(2,1)} %q_ref.7, bf16[1,128,1024]{2,1,0:T(8,128)(2,1)} %k_ref.7, bf16[1,128,2048]{2,1,0:T(8,128)(2,1)} %v_ref.7, f32[1,16,128]{2,1,0:T(8,128)} %beta_ref.7, f32[1,16,128]{2,1,0:T(8,128)} %decay_ref.7), custom_call_target="tpu_custom_call" | custom-call | tf_op jit(solution)/shard_map/prompt_terms/pallas_call | solution.py:163
  17.0 1.3 collective-permute-start
  18.3 16.8 %collective-permute-done.4.far_ref = f32[2,4,128,256]{3,2,1,0:T(8,128)S(1)} collective-permute-done((f32[2,4,128,256]{3,2,1,0:T(8,128)}, f32[2,4,128,256]{3,2,1,0:T(8,128)S(1)}, u32[]{:S(2)}, u32[]{:S(2)}) %collective-permute-start.4) | collective-permute-done | bytes 1048608 | tf_op jit(solution)/shard_map/ppermute | solution.py:402
  35.1 0.0 copy-start.4
  35.1 0.9 slice_bitcast_fusion.s_ref
  36.0 2.5 %state_step.5 = f32[4,128,256]{2,1,0:T(8,128)} custom-call(f32[2,4,128,256]{3,2,1,0:T(8,128)} %get-tuple-element.25.to_ref, f32[4,128,256]{2,1,0:T(8,128)} %slice_bitcast_fusion.s_ref), custom_call_target="tpu_custom_call" | custom-call | tf_op jit(solution)/shard_map/state_step/pallas_call | solution.py:263
  38.6 0.7 collective-permute-start.5
  39.2 17.2 %collective-permute-done.far_ref = f32[2,4,128,256]{3,2,1,0:T(8,128)S(1)} collective-permute-done((f32[2,4,128,256]{3,2,1,0:T(8,128)}, f32[2,4,128,256]{3,2,1,0:T(8,128)S(1)}, u32[]{:S(2)}, u32[]{:S(2)}) %collective-permute-start) | collective-permute-done | bytes 1048608 | tf_op jit(solution)/shard_map/ppermute | solution.py:402
  56.4 0.9 slice_bitcast_fusion.1.s_ref
  57.3 2.5 %state_step.4 = f32[4,128,256]{2,1,0:T(8,128)} custom-call(f32[2,4,128,256]{3,2,1,0:T(8,128)} %get-tuple-element.20.to_ref, f32[4,128,256]{2,1,0:T(8,128)} %slice_bitcast_fusion.1.s_ref), custom_call_target="tpu_custom_call" | custom-call | tf_op jit(solution)/shard_map/state_step/pallas_call | solution.py:263
  59.8 0.0 copy-done.4
  59.8 0.7 collective-permute-start.1
  60.5 0.0 collective-permute-done.5.s_ref
  60.6 0.0 copy-start.10
  60.6 0.8 copy-done.10
  61.4 3.3 %state_step_twice.3 = (f32[4,128,256]{2,1,0:T(8,128)}, f32[4,128,256]{2,1,0:T(8,128)}) custom-call(f32[2,4,128,256]{3,2,1,0:T(8,128)} %get-tuple-element.25.to_ref, f32[2,4,128,256]{3,2,1,0:T(8,128)} %copy-done.4, f32[4,128,256]{2,1,0:T(8,128)} %copy-done.10), custom_call_target="tpu_custom_call" | custom-call | tf_op jit(solution)/shard_map/state_step_twice/pallas_call | solution.py:281
  64.6 0.0 copy-done.2
  64.6 0.8 collective-permute-start.6
  65.4 0.0 collective-permute-done.1.s_ref
  65.4 0.0 copy-start.8
  65.5 0.8 copy-done.8
  66.2 3.3 %state_step_twice.2 = (f32[4,128,256]{2,1,0:T(8,128)}, f32[4,128,256]{2,1,0:T(8,128)}) custom-call(f32[2,4,128,256]{3,2,1,0:T(8,128)} %get-tuple-element.20.to_ref, f32[2,4,128,256]{3,2,1,0:T(8,128)} %copy-done.2, f32[4,128,256]{2,1,0:T(8,128)} %copy-done.8), custom_call_target="tpu_custom_call" | custom-call | tf_op jit(solution)/shard_map/state_step_twice/pallas_call | solution.py:281
  69.5 0.7 collective-permute-start.2
  70.2 0.0 collective-permute-done.6
  70.2 0.0 copy-done.13
  70.2 0.9 broadcast_select_fusion
  71.1 1.4 collective-permute-start.7
  72.5 0.0 collective-permute-done.2
  72.6 0.9 broadcast_select_fusion.1
  73.4 1.5 collective-permute-start.3
  74.9 0.0 copy-start.15
  74.9 22.1 %collective-permute-done.7.s_ref = f32[4,128,256]{2,1,0:T(8,128)} collective-permute-done((f32[4,128,256]{2,1,0:T(8,128)}, f32[4,128,256]{2,1,0:T(8,128)}, u32[]{:S(2)}, u32[]{:S(2)}) %collective-permute-start.7) | collective-permute-done | bytes 524320 | tf_op jit(solution)/shard_map/ppermute | solution.py:417
  97.0 2.6 %state_step.7 = f32[4,128,256]{2,1,0:T(8,128)} custom-call(f32[2,4,128,256]{3,2,1,0:T(8,128)} %get-tuple-element.25.to_ref, f32[4,128,256]{2,1,0:T(8,128)} %collective-permute-done.7.s_ref), custom_call_target="tpu_custom_call" | custom-call | tf_op jit(solution)/shard_map/state_step/pallas_call | solution.py:263
  99.6 0.0 copy-done.5
  99.6 0.0 copy-done.11
  99.6 0.0 copy-done.15
  99.6 2.1 %select_select_fusion = (f32[4,128,256]{2,1,0:T(8,128)S(1)}, f32[4,128,256]{2,1,0:T(8,128)}) fusion(f32[4,128,256]{2,1,0:T(8,128)} %state_step.7, f32[4,128,256]{2,1,0:T(8,128)} %collective-permute-done.7.s_ref, f32[4,128,256]{2,1,0:T(8,128)S(1)} %copy-done.15, f32[4,128,256]{2,1,0:T(8,128)S(1)} %collective-permute-done.6, pred[]{:T(512)S(6)} %eq.16, ...), kind=kLoop, calls=%fused_computation.2 | loop fusion | flops 786432 | bytes 4194308 | tf_op jit(solution)/shard_map/jit(_where)/select_n | solution.py:430
  101.7 0.1 collective-permute-start.9
  101.8 7.0 %collective-permute-done.3.s_ref = f32[4,128,256]{2,1,0:T(8,128)S(1)} collective-permute-done((f32[4,128,256]{2,1,0:T(8,128)}, f32[4,128,256]{2,1,0:T(8,128)S(1)}, u32[]{:S(2)}, u32[]{:S(2)}) %collective-permute-start.3) | collective-permute-done | bytes 524320 | tf_op jit(solution)/shard_map/ppermute | solution.py:417
  108.8 0.8 copy-done.12
  109.6 2.5 %state_step.6 = f32[4,128,256]{2,1,0:T(8,128)} custom-call(f32[2,4,128,256]{3,2,1,0:T(8,128)} %get-tuple-element.20.to_ref, f32[4,128,256]{2,1,0:T(8,128)} %copy-done.12), custom_call_target="tpu_custom_call" | custom-call | tf_op jit(solution)/shard_map/state_step/pallas_call | solution.py:263
  112.1 0.0 copy-done.3
  112.1 0.0 copy-done.9
  112.1 0.0 copy-done.14
  112.1 2.1 %select_select_fusion.1 = (f32[4,128,256]{2,1,0:T(8,128)S(1)}, f32[4,128,256]{2,1,0:T(8,128)}) fusion(f32[4,128,256]{2,1,0:T(8,128)} %state_step.6, f32[4,128,256]{2,1,0:T(8,128)} %copy-done.12, f32[4,128,256]{2,1,0:T(8,128)S(1)} %copy-done.14, f32[4,128,256]{2,1,0:T(8,128)S(1)} %collective-permute-done.2, pred[]{:T(512)S(6)} %eq.16, pred[]{:T(512)S(6)} %eq.7, ...), kind=kLoop, calls=%fused_computation.3 | loop fusion | flops 786432 | bytes 4194308 | tf_op jit(solution)/shard_map/jit(_where)/select_n | solution.py:430
  114.2 0.0 copy-done
  114.2 0.0 collective-permute-start.8
  114.2 8.9 %suffix_terms.7 = (bf16[2,256,512]{2,1,0:T(8,128)(2,1)}, f32[2,256,512]{2,1,0:T(8,128)}) custom-call(bf16[2,256,1024]{2,1,0:T(8,128)(2,1)} %q_ref.11, bf16[2,256,1024]{2,1,0:T(8,128)(2,1)} %k_ref.11, bf16[2,256,2048]{2,1,0:T(8,128)(2,1)} %v_ref.11, f32[2,16,256]{2,1,0:T(8,128)} %beta_ref.11, f32[2,16,256]{2,1,0:T(8,128)} %decay_ref.11), custom_call_target="tpu_custom_call" | custom-call | tf_op jit(solution)/shard_map/suffix_terms/pallas_call | solution.py:231
  123.1 0.0 copy-done.1
  123.1 8.7 %suffix_terms.6 = (bf16[2,256,512]{2,1,0:T(8,128)(2,1)}, f32[2,256,512]{2,1,0:T(8,128)}) custom-call(bf16[2,256,1024]{2,1,0:T(8,128)(2,1)} %q_ref.11, bf16[2,256,1024]{2,1,0:T(8,128)(2,1)} %k_ref.11, bf16[2,256,2048]{2,1,0:T(8,128)(2,1)} %v_ref.11, f32[2,16,256]{2,1,0:T(8,128)} %beta_ref.11, f32[2,16,256]{2,1,0:T(8,128)} %decay_ref.11), custom_call_target="tpu_custom_call" | custom-call | tf_op jit(solution)/shard_map/suffix_terms/pallas_call | solution.py:231
  131.8 8.7 %suffix_terms.5 = (bf16[2,256,512]{2,1,0:T(8,128)(2,1)}, f32[2,256,512]{2,1,0:T(8,128)}) custom-call(bf16[2,256,1024]{2,1,0:T(8,128)(2,1)} %q_ref.11, bf16[2,256,1024]{2,1,0:T(8,128)(2,1)} %k_ref.11, bf16[2,256,2048]{2,1,0:T(8,128)(2,1)} %v_ref.11, f32[2,16,256]{2,1,0:T(8,128)} %beta_ref.11, f32[2,16,256]{2,1,0:T(8,128)} %decay_ref.11), custom_call_target="tpu_custom_call" | custom-call | tf_op jit(solution)/shard_map/suffix_terms/pallas_call | solution.py:231
  140.6 9.0 %suffix_terms.4 = (bf16[2,256,512]{2,1,0:T(8,128)(2,1)}, f32[2,256,512]{2,1,0:T(8,128)}) custom-call(bf16[2,256,1024]{2,1,0:T(8,128)(2,1)} %q_ref.11, bf16[2,256,1024]{2,1,0:T(8,128)(2,1)} %k_ref.11, bf16[2,256,2048]{2,1,0:T(8,128)(2,1)} %v_ref.11, f32[2,16,256]{2,1,0:T(8,128)} %beta_ref.11, f32[2,16,256]{2,1,0:T(8,128)} %decay_ref.11), custom_call_target="tpu_custom_call" | custom-call | tf_op jit(solution)/shard_map/suffix_terms/pallas_call | solution.py:231
  149.5 2.4 %prompt_out.2.refs_0_ = bf16[1,128,2048]{2,1,0:T(8,128)(2,1)} custom-call(f32[4,128,256]{2,1,0:T(8,128)} %get-tuple-element.39.s_ref, bf16[128,1024]{1,0:T(8,128)(2,1)} %get-tuple-element.28.a_ref, f32[128,1024]{1,0:T(8,128)} %get-tuple-element.29.b_ref, f32[1,128]{1,0:T(1,128)} %bitcast.9), custom_call_target="tpu_custom_call" | custom-call | tf_op jit(solution)/shard_map/prompt_out/pallas_call | solution.py:376
  151.9 2.4 %prompt_out.3 = bf16[1,128,2048]{2,1,0:T(8,128)(2,1)} custom-call(f32[4,128,256]{2,1,0:T(8,128)} %get-tuple-element.41.s_ref, bf16[128,1024]{1,0:T(8,128)(2,1)} %get-tuple-element.23.a_ref, f32[128,1024]{1,0:T(8,128)} %get-tuple-element.24.b_ref, f32[1,128]{1,0:T(1,128)} %bitcast.10, ...), custom_call_target="tpu_custom_call", output_to_operand_aliasing={{}: (4, {})} | custom-call | tf_op jit(solution)/shard_map/prompt_out/pallas_call | solution.py:376
  154.3 0.0 collective-permute-done.9.refs_4_
  154.3 0.8 copy-done.6
  155.1 2.8 %suffix_out.4.refs_8_ = bf16[2,256,2048]{2,1,0:T(8,128)(2,1)} custom-call(s32[16]{0:T(128)} %refs_0_.7, s32[16]{0:T(128)} %refs_1_.7, s32[16]{0:T(128)} %refs_2_.7, f32[4,128,256]{2,1,0:T(8,128)} %copy-done, f32[4,128,256]{2,1,0:T(8,128)} %copy-done.6, bf16[2,256,512]{2,1,0:T(8,128)(2,1)} %get-tuple-element.36.refs_5_, ...), custom_call_target="tpu_custom_call" | custom-call | tf_op jit(solution)/shard_map/suffix_out/pallas_call | solution.py:340
  157.9 2.9 %suffix_out.5.refs_8_ = bf16[2,256,2048]{2,1,0:T(8,128)(2,1)} custom-call(s32[16]{0:T(128)} %refs_0_.7, s32[16]{0:T(128)} %refs_1_.7, s32[16]{0:T(128)} %refs_2_.7, f32[4,128,256]{2,1,0:T(8,128)} %copy-done, f32[4,128,256]{2,1,0:T(8,128)} %copy-done.6, bf16[2,256,512]{2,1,0:T(8,128)(2,1)} %get-tuple-element.34.refs_5_, ...), custom_call_target="tpu_custom_call", output_to_operand_aliasing={{}: (8, {})} | custom-call | tf_op jit(solution)/shard_map/suffix_out/pallas_call | solution.py:340
  160.8 0.0 collective-permute-done.8.refs_4_
  160.8 0.8 copy-done.7
  161.6 2.8 %suffix_out.6.refs_8_ = bf16[2,256,2048]{2,1,0:T(8,128)(2,1)} custom-call(s32[16]{0:T(128)} %refs_0_.7, s32[16]{0:T(128)} %refs_1_.7, s32[16]{0:T(128)} %refs_2_.7, f32[4,128,256]{2,1,0:T(8,128)} %copy-done.1, f32[4,128,256]{2,1,0:T(8,128)} %copy-done.7, bf16[2,256,512]{2,1,0:T(8,128)(2,1)} %get-tuple-element.32.refs_5_, ...), custom_call_target="tpu_custom_call", output_to_operand_aliasing={{}: (8, {})} | custom-call | tf_op jit(solution)/shard_map/suffix_out/pallas_call | solution.py:340
  164.5 2.9 %suffix_out.7 = bf16[2,256,2048]{2,1,0:T(8,128)(2,1)} custom-call(s32[16]{0:T(128)} %refs_0_.7, s32[16]{0:T(128)} %refs_1_.7, s32[16]{0:T(128)} %refs_2_.7, f32[4,128,256]{2,1,0:T(8,128)} %copy-done.1, f32[4,128,256]{2,1,0:T(8,128)} %copy-done.7, bf16[2,256,512]{2,1,0:T(8,128)(2,1)} %get-tuple-element.30.refs_5_, ...), custom_call_target="tpu_custom_call", output_to_operand_aliasing={{}: (8, {})} | custom-call | tf_op jit(solution)/shard_map/suffix_out/pallas_call | solution.py:340
  (12 shorter events, 0.0 us)
Async XLA Ops:
  6.3 28.8 %collective-permute-start.4 = (f32[2,4,128,256]{3,2,1,0:T(8,128)}, f32[2,4,128,256]{3,2,1,0:T(8,128)S(1)}, u32[]{:S(2)}, u32[]{:S(2)}) collective-permute-start(f32[2,4,128,256]{3,2,1,0:T(8,128)} %get-tuple-element.25.to_ref), channel_id=1, source_target_pairs={{0,4},{12,8},{1,5},{13,9},{2,6},{14,10},{3,7},{15,11},{16,20},{28,... | collective-permute-start | bytes 3145736 | tf_op jit(solution)/shard_map/ppermute | solution.py:402
  17.0 39.4 %collective-permute-start = (f32[2,4,128,256]{3,2,1,0:T(8,128)}, f32[2,4,128,256]{3,2,1,0:T(8,128)S(1)}, u32[]{:S(2)}, u32[]{:S(2)}) collective-permute-start(f32[2,4,128,256]{3,2,1,0:T(8,128)} %get-tuple-element.20.to_ref), channel_id=1, source_target_pairs={{0,4},{12,8},{1,5},{13,9},{2,6},{14,10},{3,7},{15,11},{16,20},{28,... | collective-permute-start | bytes 3145736 | tf_op jit(solution)/shard_map/ppermute | solution.py:402
  35.1 24.7 %copy-start.4 = (f32[2,4,128,256]{3,2,1,0:T(8,128)}, f32[2,4,128,256]{3,2,1,0:T(8,128)S(1)}, u32[]{:S(2)}) copy-start(f32[2,4,128,256]{3,2,1,0:T(8,128)S(1)} %collective-permute-done.4.far_ref) | copy-start | bytes 3145732
  38.6 22.0 %collective-permute-start.5 = (f32[4,128,256]{2,1,0:T(8,128)}, f32[4,128,256]{2,1,0:T(8,128)S(1)}, u32[]{:S(2)}, u32[]{:S(2)}) collective-permute-start(f32[4,128,256]{2,1,0:T(8,128)} %state_step.5), channel_id=1, source_target_pairs={{4,8},{5,9},{6,10},{7,11},{20,24},{21,25},{22,26},{23,27}} | collective-permute-start | bytes 1572872 | tf_op jit(solution)/shard_map/ppermute | solution.py:410
  56.4 8.2 %copy-start.2 = (f32[2,4,128,256]{3,2,1,0:T(8,128)}, f32[2,4,128,256]{3,2,1,0:T(8,128)S(1)}, u32[]{:S(2)}) copy-start(f32[2,4,128,256]{3,2,1,0:T(8,128)S(1)} %collective-permute-done.far_ref) | copy-start | bytes 3145732
  59.8 5.6 %collective-permute-start.1 = (f32[4,128,256]{2,1,0:T(8,128)}, f32[4,128,256]{2,1,0:T(8,128)S(1)}, u32[]{:S(2)}, u32[]{:S(2)}) collective-permute-start(f32[4,128,256]{2,1,0:T(8,128)} %state_step.4), channel_id=1, source_target_pairs={{4,8},{5,9},{6,10},{7,11},{20,24},{21,25},{22,26},{23,27}} | collective-permute-start | bytes 1572872 | tf_op jit(solution)/shard_map/ppermute | solution.py:410
  60.6 0.8 copy-start.10
  64.6 5.6 %copy-start.13 = (f32[4,128,256]{2,1,0:T(8,128)S(1)}, f32[4,128,256]{2,1,0:T(8,128)}, u32[]{:S(2)}) copy-start(f32[4,128,256]{2,1,0:T(8,128)} %get-tuple-element.27) | copy-start | bytes 1572868
  64.6 5.6 %collective-permute-start.6 = (f32[4,128,256]{2,1,0:T(8,128)}, f32[4,128,256]{2,1,0:T(8,128)S(1)}, u32[]{:S(2)}, u32[]{:S(2)}) collective-permute-start(f32[4,128,256]{2,1,0:T(8,128)} %get-tuple-element.26), channel_id=1, source_target_pairs={{8,4},{9,5},{10,6},{11,7},{24,20},{25,21},{26,22},{27,23}} | collective-permute-start | bytes 1572872 | tf_op jit(solution)/shard_map/ppermute | solution.py:412
  65.4 0.8 copy-start.8
  69.5 3.0 %collective-permute-start.2 = (f32[4,128,256]{2,1,0:T(8,128)}, f32[4,128,256]{2,1,0:T(8,128)S(1)}, u32[]{:S(2)}, u32[]{:S(2)}) collective-permute-start(f32[4,128,256]{2,1,0:T(8,128)} %get-tuple-element.21), channel_id=1, source_target_pairs={{8,4},{9,5},{10,6},{11,7},{24,20},{25,21},{26,22},{27,23}} | collective-permute-start | bytes 1572872 | tf_op jit(solution)/shard_map/ppermute | solution.py:412
  71.1 28.5 %copy-start.5 = (f32[2,4,128,256]{3,2,1,0:T(8,128)S(1)}, f32[2,4,128,256]{3,2,1,0:T(8,128)}, u32[]{:S(2)}) copy-start(f32[2,4,128,256]{3,2,1,0:T(8,128)} %copy-done.4) | copy-start | bytes 3145732
  71.1 28.5 %copy-start.11 = (f32[4,128,256]{2,1,0:T(8,128)S(1)}, f32[4,128,256]{2,1,0:T(8,128)}, u32[]{:S(2)}) copy-start(f32[4,128,256]{2,1,0:T(8,128)} %copy-done.10) | copy-start | bytes 1572868
  71.1 25.9 %collective-permute-start.7 = (f32[4,128,256]{2,1,0:T(8,128)}, f32[4,128,256]{2,1,0:T(8,128)}, u32[]{:S(2)}, u32[]{:S(2)}) collective-permute-start(f32[4,128,256]{2,1,0:T(8,128)} %broadcast_select_fusion), channel_id=1, source_target_pairs={{4,0},{8,12},{5,1},{9,13},{6,2},{10,14},{7,3},{11,15},{20,16},{24,... | collective-permute-start | bytes 1572872 | tf_op jit(solution)/shard_map/ppermute | solution.py:417
  73.4 35.4 %collective-permute-start.3 = (f32[4,128,256]{2,1,0:T(8,128)}, f32[4,128,256]{2,1,0:T(8,128)S(1)}, u32[]{:S(2)}, u32[]{:S(2)}) collective-permute-start(f32[4,128,256]{2,1,0:T(8,128)} %broadcast_select_fusion.1), channel_id=1, source_target_pairs={{4,0},{8,12},{5,1},{9,13},{6,2},{10,14},{7,3},{11,15},{20,16},{24,... | collective-permute-start | bytes 1572872 | tf_op jit(solution)/shard_map/ppermute | solution.py:417
  74.9 24.7 %copy-start.15 = (f32[4,128,256]{2,1,0:T(8,128)S(1)}, f32[4,128,256]{2,1,0:T(8,128)}, u32[]{:S(2)}) copy-start(f32[4,128,256]{2,1,0:T(8,128)} %get-tuple-element.26) | copy-start | bytes 1572868
  101.7 12.5 %copy-start = (f32[4,128,256]{2,1,0:T(8,128)}, f32[4,128,256]{2,1,0:T(8,128)S(1)}, u32[]{:S(2)}) copy-start(f32[4,128,256]{2,1,0:T(8,128)S(1)} %get-tuple-element.38.refs_3_) | copy-start | bytes 1572868
  101.7 10.4 %copy-start.3 = (f32[2,4,128,256]{3,2,1,0:T(8,128)S(1)}, f32[2,4,128,256]{3,2,1,0:T(8,128)}, u32[]{:S(2)}) copy-start(f32[2,4,128,256]{3,2,1,0:T(8,128)} %copy-done.2) | copy-start | bytes 3145732
  101.7 10.4 %copy-start.9 = (f32[4,128,256]{2,1,0:T(8,128)S(1)}, f32[4,128,256]{2,1,0:T(8,128)}, u32[]{:S(2)}) copy-start(f32[4,128,256]{2,1,0:T(8,128)} %copy-done.8) | copy-start | bytes 1572868
  101.7 10.4 %copy-start.14 = (f32[4,128,256]{2,1,0:T(8,128)S(1)}, f32[4,128,256]{2,1,0:T(8,128)}, u32[]{:S(2)}) copy-start(f32[4,128,256]{2,1,0:T(8,128)} %get-tuple-element.21) | copy-start | bytes 1572868
  101.7 52.5 %collective-permute-start.9 = (f32[4,128,256]{2,1,0:T(8,128)S(1)}, f32[4,128,256]{2,1,0:T(8,128)S(1)}, u32[]{:S(2)}, u32[]{:S(2)}) collective-permute-start(f32[4,128,256]{2,1,0:T(8,128)S(1)} %get-tuple-element.38.refs_3_), channel_id=1, source_target_pairs={{0,1},{1,0},{2,3},{3,2},{4,5},{5,4},{6,7},{7,6},{8,9},{9,8},{10,11... | collective-permute-start | bytes 1572872 | tf_op jit(solution)/shard_map/ppermute | solution.py:472
  108.8 0.8 copy-start.12
  114.2 8.9 %copy-start.1 = (f32[4,128,256]{2,1,0:T(8,128)}, f32[4,128,256]{2,1,0:T(8,128)S(1)}, u32[]{:S(2)}) copy-start(f32[4,128,256]{2,1,0:T(8,128)S(1)} %get-tuple-element.40.refs_3_) | copy-start | bytes 1572868
  114.2 46.6 %collective-permute-start.8 = (f32[4,128,256]{2,1,0:T(8,128)S(1)}, f32[4,128,256]{2,1,0:T(8,128)S(1)}, u32[]{:S(2)}, u32[]{:S(2)}) collective-permute-start(f32[4,128,256]{2,1,0:T(8,128)S(1)} %get-tuple-element.40.refs_3_), channel_id=1, source_target_pairs={{0,1},{1,0},{2,3},{3,2},{4,5},{5,4},{6,7},{7,6},{8,9},{9,8},{10,11... | collective-permute-start | bytes 1572872 | tf_op jit(solution)/shard_map/ppermute | solution.py:472
  154.3 0.8 copy-start.6
  160.8 0.8 copy-start.7
where the time goes:
time: 168 us; the launch traced here: 167 us
  Pallas kernels  79.5 us (47%)
  waiting for transfers between devices  63 us (38%)
  starting transfers between devices  12.1 us (7%)
  other arithmetic  5.94 us (4%)
  local copies, waits for them, and re-layouts  5.84 us (3%)
    pallas_call x4, Pallas kernels, suffix_terms(): pl.pallas_call(functools.partial(suffix_kernel, first + part, unit), grid...  35.3 us
    ppermute x2, waiting for transfers between devices, exchange(): lax.ppermute(sending, 'seq', [(j, j + 1), (count - 1 - j, count - 2 - j)])  33.9 us
    ppermute x2, waiting for transfers between devices, exchange(): lax.ppermute(jnp.where(here < half, left_out, state_out), 'seq', [(half -...  29.1 us
    pallas_call x2, Pallas kernels, prompt_terms(): pl.pallas_call(functools.partial(prompt_kernel, first, pairs), grid=(1,),...  11.4 us
    pallas_call x4, Pallas kernels, suffix_outputs(): pl.pallas_call(functools.partial(suffix_out_kernel, unit, slots, lax.axis...  11.4 us
    pallas_call x4, Pallas kernels, step(): pl.pallas_call(functools.partial(step_kernel, pairs), out_shape=jax.Shape...  10.2 us
    pallas_call x2, Pallas kernels, step2(): pl.pallas_call(functools.partial(step2_kernel, pairs), out_shape=[shape,...  6.51 us
    ppermute x2, starting transfers between devices, exchange(): lax.ppermute(sending, 'seq', [(j, j + 1), (count - 1 - j, count - 2 - j)])  6.32 us
  transfers between devices with their start and end apart: 10, of which 4 were waited for; matrix products, arithmetic and copies ran while one was open for 5% of the time, Pallas kernels for 41%

commit v1 on v0

v1 whole, which is shorter than its diff:
```python
import functools
import math

import jax
import jax.numpy as jnp
from jax import lax
from jax.experimental import pallas as pl
from jax.experimental.pallas import tpu as pltpu
from jax.sharding import PartitionSpec as P

DK = 128
DV = 128
CH = 128
W2 = 2 * DV
EPS_NORM = 1e-06
HIGH = lax.Precision.HIGHEST
VMEM = 56 * 1024 * 1024


def mm(left, right):
    return lax.dot_general(left, right, (((1,), (0,)), ((), ())), preferred_element_type=jnp.float32)


def diag2(pair):
    zero = jnp.zeros((pair.shape[0], DV), pair.dtype)
    top = jnp.concatenate([pair[:, :DV], zero], axis=1)
    low = jnp.concatenate([zero, pair[:, DV:]], axis=1)
    return jnp.concatenate([top, low], axis=0)


def low16(value):
    return value.astype(jnp.bfloat16)


def halves(value):
    high = low16(value)
    return high, low16(value - high.astype(jnp.float32))


def lanes2(col_a, col_b):
    shape = (col_a.shape[0], DV)
    return jnp.concatenate(
        [jnp.broadcast_to(col_a, shape), jnp.broadcast_to(col_b, shape)], axis=1
    )


def unit_rows(vectors):
    wide = vectors.astype(jnp.float32)
    factor = lax.rsqrt(jnp.sum(wide * wide, axis=-1, keepdims=True) + EPS_NORM)
    return low16(wide * factor)


def apply_pair(transfer, state, offset):
    t_hi, t_lo = halves(transfer)
    s_hi, s_lo = halves(state)
    hi = diag2(s_hi)
    return mm(t_hi, hi) + mm(t_lo, hi) + mm(t_hi, diag2(s_lo)) + offset


def gate_tables(decay):
    rows = lax.broadcasted_iota(jnp.int32, (CH, CH), 0)
    cols = lax.broadcasted_iota(jnp.int32, (CH, CH), 1)
    upper = jnp.where(rows <= cols, 1.0, 0.0).astype(jnp.float32)
    cum = lax.dot_general(
        decay, upper, (((1,), (0,)), ((), ())), precision=HIGH, preferred_element_type=jnp.float32
    )
    return cum, cum.T


def chunk_terms(chains):
    rows = lax.broadcasted_iota(jnp.int32, (CH, W2), 0)
    cols = jnp.bitwise_and(lax.broadcasted_iota(jnp.int32, (CH, W2), 1), CH - 1)
    causal = rows >= cols
    eye = jnp.where(rows == cols, 1.0, 0.0).astype(jnp.float32)
    eye16 = low16(eye)
    apart = jnp.bitwise_xor(rows, cols)
    strict = rows > cols
    masks = [
        low16(jnp.where(strict & (apart >= low) & (apart < high), -1.0, 0.0))
        for low, high in ((1, 8), (8, 32), (32, CH))
    ]

    heads = []
    for q, k, v, beta, cum_r, cum_c in chains:
        qn = unit_rows(q)
        kn = unit_rows(k)
        heads.append((qn, kn, low16(kn.astype(jnp.float32).T)))
    grams = [mm(jnp.concatenate([kn, qn], axis=0), kt) for qn, kn, kt in heads]
    lows, lefts, grows = [], [], []
    for (q, k, v, beta, cum_r, cum_c), (qn, kn, kt), gram in zip(chains, heads, grams):
        kk = gram[:CH]
        qk = gram[CH:]
        bcast = lanes2(cum_c[:, 0:1], cum_c[:, 1:2])
        row = jnp.concatenate([cum_r[0:1], cum_r[1:2]], axis=1)
        gate = jnp.concatenate([beta[0:1], beta[1:2]], axis=1)
        scaled = jnp.exp(jnp.where(causal, bcast - row, -1e30)) * gate
        lows.append(low16(scaled * jnp.concatenate([kk, kk], axis=1)))
        attn = scaled * jnp.concatenate([qk, qk], axis=1)
        last = jnp.concatenate([cum_r[0:1, CH - 1 :], cum_r[1:2, CH - 1 :]], axis=0)
        last = jnp.concatenate(
            [jnp.broadcast_to(last[0:1], (1, DV)), jnp.broadcast_to(last[1:2], (1, DV))], axis=1
        )
        tail = jnp.exp(last - row) * gate
        ktf = kt.astype(jnp.float32)
        lefts.append(halves(jnp.concatenate([attn, jnp.concatenate([ktf, ktf], axis=1) * tail], axis=0)))
        grows.append((jnp.exp(bcast), jnp.exp(row), jnp.exp(last)))
    nil = [low * masks[0] for low in lows]
    sq = [low16(mm(n, diag2(n))) for n in nil]
    fourth = [low16(mm(s, diag2(s))) for s in sq]
    inv = [low16(mm(eye16 + n, diag2(eye16 + s))) for n, s in zip(nil, sq)]
    inv = [low16(mm(i, diag2(eye16 + f))) for i, f in zip(inv, fourth)]
    for mask in masks[1:]:
        x = [low16(mm(i, diag2(low * mask))) for i, low in zip(inv, lows)]
        y = [low16(mm(eye16 + t, diag2(i))) for t, i in zip(x, inv)]
        z = [low16(mm(t, diag2(t))) for t in x]
        full = [mm(eye16 + t, diag2(i)) for t, i in zip(z, y)]
        inv = [low16(f) for f in full]
    ws = [
        low16(mm(low16(f * grow[1]), diag2(jnp.concatenate([kn, kn], axis=1))))
        for f, grow, (qn, kn, kt) in zip(full, grows, heads)
    ]
    us = [halves(mm(i, diag2(chain[2]))) for i, chain in zip(inv, chains)]
    by_w = [mm(left, diag2(w)) for (left, rest), w in zip(lefts, ws)]
    by_u = []
    for (left, rest), (u_hi, u_lo) in zip(lefts, us):
        hi = diag2(u_hi)
        by_u.append(mm(left, hi) + mm(rest, hi) + mm(left, diag2(u_lo)))
    out = []
    for (qn, kn, kt), grow, bw, bu in zip(heads, grows, by_w, by_u):
        qf = qn.astype(jnp.float32)
        a = jnp.concatenate([qf, qf], axis=1) * grow[0] - bw[:CH]
        out.append((a, bu[:CH], eye * grow[2] - bw[CH:], bu[CH:]))
    return out


def read_chains(pairs, heads, at, q_ref, k_ref, v_ref, beta_ref, decay_ref, slot):
    beta = beta_ref[slot, heads, at]
    cum_r, cum_c = gate_tables(decay_ref[slot, heads, at])
    return [
        (
            q_ref[slot, at, p * DK : (p + 1) * DK],
            k_ref[slot, at, p * DK : (p + 1) * DK],
            v_ref[slot, at, p * W2 : (p + 1) * W2],
            beta[2 * p : 2 * p + 2],
            cum_r[2 * p : 2 * p + 2],
            cum_c[:, 2 * p : 2 * p + 2],
        )
        for p in range(pairs)
    ]


def window(first, pairs):
    return math.gcd(first, pairs) if first else pairs


def lane_specs(arrays, first, pairs, width):
    wide = window(first, pairs)
    specs, args = [], []
    for part in range(first, first + pairs, wide):
        specs.append(
            pl.BlockSpec(arrays.shape[:2] + (wide * width,), lambda i, at=part // wide: (0, 0, at))
        )
        args.append(arrays)
    return specs, args, wide


ANY = pl.BlockSpec(memory_space=pl.ANY)


class Spans:
    def __init__(self, refs, wide, width):
        self.refs, self.size, self.width = refs, wide * width, width

    def __getitem__(self, key):
        lanes = key[-1]
        part, at = divmod(lanes.start, self.size)
        return self.refs[part][key[:-1] + (slice(at, at + lanes.stop - lanes.start),)]


def prompt_kernel(first, sizes, wide, count, *refs):
    pairs = sum(sizes)
    q_ref = Spans(refs[:count], wide, DK)
    k_ref = Spans(refs[count : 2 * count], wide, DK)
    v_ref = Spans(refs[2 * count : 3 * count], wide, W2)
    beta_ref, decay_ref = refs[3 * count : 3 * count + 2]
    outs = refs[len(refs) - 2 - len(sizes) :]
    heads = slice(2 * first, 2 * (first + pairs))
    chains = read_chains(
        pairs, heads, slice(0, CH), q_ref, k_ref, v_ref, beta_ref, decay_ref, 0
    )
    places = [(c, p) for c, size in enumerate(sizes) for p in range(size)]
    for p, (a, b, transfer, offset) in enumerate(chunk_terms(chains)):
        outs[-2][:, p * W2 : (p + 1) * W2] = low16(a)
        outs[-1][:, p * W2 : (p + 1) * W2] = low16(b)
        chunk, at = places[p]
        outs[chunk][0, at] = transfer
        outs[chunk][1, at] = offset


def prompt_terms(first, sizes, q, k, v, beta, decay, after=()):
    pairs = sum(sizes)
    q_specs, q_args, wide = lane_specs(q, first, pairs, DK)
    k_specs, k_args, wide = lane_specs(k, first, pairs, DK)
    v_specs, v_args, wide = lane_specs(v, first, pairs, W2)
    *tos, a, b = pl.pallas_call(
        functools.partial(prompt_kernel, first, sizes, wide, len(q_args)),
        grid=(1,),
        in_specs=q_specs
        + k_specs
        + v_specs
        + [
            pl.BlockSpec(beta.shape, lambda i: (0, 0, 0)),
            pl.BlockSpec(decay.shape, lambda i: (0, 0, 0)),
        ]
        + [ANY] * len(after),
        out_specs=[pl.BlockSpec((2, size, DK, W2), lambda i: (0, 0, 0, 0)) for size in sizes]
        + [pl.BlockSpec((CH, pairs * W2), lambda i: (0, 0))] * 2,
        out_shape=[jax.ShapeDtypeStruct((2, size, DK, W2), jnp.float32) for size in sizes]
        + [jax.ShapeDtypeStruct((CH, pairs * W2), jnp.bfloat16)] * 2,
        compiler_params=pltpu.CompilerParams(vmem_limit_bytes=VMEM),
        name="prompt_terms",
    )(*q_args, *k_args, *v_args, beta, decay, *after)
    return tos, a, b


def suffix_kernel(first, unit, q_ref, k_ref, v_ref, beta_ref, decay_ref, *refs):
    a_ref, b_ref = refs[-2:]
    slots, tokens = q_ref.shape[:2]
    spans = tokens // CH
    heads = slice(2 * first, 2 * (first + unit))
    chains = []
    for slot in range(slots):
        for s in range(spans):
            chains += read_chains(
                unit,
                heads,
                slice(s * CH, (s + 1) * CH),
                q_ref,
                k_ref,
                v_ref,
                beta_ref,
                decay_ref,
                slot,
            )
    terms = chunk_terms(chains)
    for slot in range(slots):
        for p in range(unit):
            lanes = slice(p * W2, (p + 1) * W2)
            a, b, transfer, offset = terms[slot * spans * unit + p]
            a_ref[slot, 0:CH, lanes] = low16(a)
            b_ref[slot, 0:CH, lanes] = low16(b)
            for s in range(1, spans):
                a, b, t_next, o_next = terms[(slot * spans + s) * unit + p]
                a16 = low16(a)
                at = slice(s * CH, (s + 1) * CH)
                d_t = diag2(low16(transfer))
                d_o = diag2(low16(offset))
                a_ref[slot, at, lanes] = low16(mm(a16, d_t))
                b_ref[slot, at, lanes] = low16(mm(a16, d_o) + b)
                if s + 1 < spans:
                    t16 = low16(t_next)
                    transfer, offset = mm(t16, d_t), mm(t16, d_o) + o_next


def suffix_terms(first, unit, q, k, v, beta, decay, after=()):
    slots, tokens = q.shape[0], q.shape[1]
    at = first // unit
    return pl.pallas_call(
        functools.partial(suffix_kernel, first, unit),
        grid=(1,),
        in_specs=[
            pl.BlockSpec((slots, tokens, unit * DK), lambda i: (0, 0, at)),
            pl.BlockSpec((slots, tokens, unit * DK), lambda i: (0, 0, at)),
            pl.BlockSpec((slots, tokens, unit * W2), lambda i: (0, 0, at)),
            pl.BlockSpec(beta.shape, lambda i: (0, 0, 0)),
            pl.BlockSpec(decay.shape, lambda i: (0, 0, 0)),
        ]
        + [ANY] * len(after),
        out_specs=[pl.BlockSpec((slots, tokens, unit * W2), lambda i: (0, 0, 0))] * 2,
        out_shape=[jax.ShapeDtypeStruct((slots, tokens, unit * W2), jnp.bfloat16)] * 2,
        compiler_params=pltpu.CompilerParams(vmem_limit_bytes=VMEM),
        name="suffix_terms",
    )(q, k, v, beta, decay, *after)


def step_kernel(kinds, half, *refs):
    here = lax.axis_index("seq")
    refs = list(refs)
    counts = {"step": 2, "twice": 3}
    inputs = []
    for kind in kinds:
        inputs.append([refs.pop(0) for _ in range(counts[kind])])
    outs = refs[len(refs) - sum(2 if kind == "twice" else 1 for kind in kinds) :]
    for kind, ins in zip(kinds, inputs):
        if kind == "step":
            out = outs.pop(0)

            @pl.when(here < half)
            def _(ins=ins, out=out):
                for p in range(out.shape[0]):
                    out[p] = apply_pair(ins[0][0, p], ins[1][1, p], ins[0][1, p])

        else:
            out, final = outs.pop(0), outs.pop(0)

            @pl.when(here == half)
            def _(ins=ins, out=out, final=final):
                for p in range(out.shape[0]):
                    state = apply_pair(ins[0][0, p], ins[2][p], ins[0][1, p])
                    out[p] = state
                    final[p] = apply_pair(ins[1][0, p], state, ins[1][1, p])


def run_steps(jobs, half, after=()):
    kinds = tuple(job[0] for job in jobs)
    args, shapes = [], []
    for kind, *ins in jobs:
        args += ins
        shape = jax.ShapeDtypeStruct(ins[0].shape[1:], jnp.float32)
        shapes += [shape] * (2 if kind == "twice" else 1)
    whole = pl.BlockSpec(memory_space=pltpu.VMEM)
    outs = pl.pallas_call(
        functools.partial(step_kernel, kinds, half),
        in_specs=[whole] * len(args) + [ANY] * len(after),
        out_specs=[whole] * len(shapes),
        out_shape=shapes,
        compiler_params=pltpu.CompilerParams(vmem_limit_bytes=VMEM),
        name="state_steps",
    )(*args, *after)
    outs = list(outs)
    results = []
    for kind in kinds:
        if kind == "twice":
            results.append((outs.pop(0), outs.pop(0)))
        else:
            results.append(outs.pop(0))
    return results


def settle_kernel(half, to_ref, right_ref, mid_ref, *refs):
    here = lax.axis_index("seq")
    out_ref = refs[-1]
    lefts = refs[:half]
    for d in range(half):

        @pl.when(here == d)
        def _(d=d):
            out_ref[...] = lefts[d][...]

    @pl.when(here == half)
    def _():
        out_ref[...] = mid_ref[...]

    @pl.when(here > half)
    def _():
        for p in range(out_ref.shape[0]):
            out_ref[p] = apply_pair(to_ref[0, p], right_ref[p], to_ref[1, p])


def settle(to, right, mid, lefts, after=()):
    half = len(lefts)
    whole = pl.BlockSpec(memory_space=pltpu.VMEM)
    return pl.pallas_call(
        functools.partial(settle_kernel, half),
        in_specs=[whole] * (3 + half) + [ANY] * len(after),
        out_specs=whole,
        out_shape=jax.ShapeDtypeStruct(mid.shape, jnp.float32),
        compiler_params=pltpu.CompilerParams(vmem_limit_bytes=VMEM),
        name="settle",
    )(to, right, mid, *lefts, *after)


def finish(a, state, b, gain2):
    raw = mm(a, diag2(low16(state))) + b.astype(jnp.float32)
    sq = raw * raw
    parts = []
    for h in range(2):
        lanes = slice(h * DV, (h + 1) * DV)
        inv = lax.rsqrt(jnp.mean(sq[:, lanes], axis=-1, keepdims=True) + EPS_NORM)
        parts.append(raw[:, lanes] * inv)
    return jnp.concatenate(parts, axis=1) * gain2


def suffix_out_kernel(unit, slots, n_prompt, *refs):
    sb_ref, bl_ref, bp_ref, own_ref, other_ref, a_ref, b_ref, gain_ref = refs[:8]
    out_ref = refs[-1]
    me = lax.axis_index("prompt")
    rank = lax.axis_index("seq") * n_prompt + me
    branch = sb_ref[rank * slots + pl.program_id(0)]
    length = bl_ref[branch]
    mine = bp_ref[branch] == me
    gain = gain_ref[...]
    gain2 = jnp.concatenate([gain, gain], axis=1)
    tokens = a_ref.shape[1]
    live = lax.broadcasted_iota(jnp.int32, (tokens, W2), 0) < length
    for p in range(unit):
        lanes = slice(p * W2, (p + 1) * W2)
        state = jnp.where(mine, own_ref[p], other_ref[p])
        out = finish(a_ref[0, :, lanes], state, b_ref[0, :, lanes], gain2)
        out_ref[0, :, lanes] = low16(jnp.where(live, out, 0.0))


def suffix_outputs(first, tables, own, other, a, b, gain, so_far, width, after=()):
    slots, tokens, lanes = a.shape
    unit = lanes // W2
    at = first // unit
    smem = pl.BlockSpec(memory_space=pltpu.SMEM)
    in_specs = [
        smem,
        smem,
        smem,
        pl.BlockSpec((unit, DK, W2), lambda i: (0, 0, 0)),
        pl.BlockSpec((unit, DK, W2), lambda i: (0, 0, 0)),
        pl.BlockSpec((1, tokens, lanes), lambda i: (i, 0, 0)),
        pl.BlockSpec((1, tokens, lanes), lambda i: (i, 0, 0)),
        pl.BlockSpec((1, DV), lambda i: (0, 0)),
    ]
    args = list(tables) + [own, other, a, b, gain]
    aliases = {}
    if so_far is not None:
        in_specs.append(ANY)
        args.append(so_far)
        aliases = {8: 0}
    return pl.pallas_call(
        functools.partial(suffix_out_kernel, unit, slots, lax.axis_size("prompt")),
        grid=(slots,),
        in_specs=in_specs + [ANY] * len(after),
        out_specs=pl.BlockSpec((1, tokens, lanes), lambda i: (i, 0, at)),
        out_shape=jax.ShapeDtypeStruct((slots, tokens, width), jnp.bfloat16),
        input_output_aliases=aliases,
        compiler_params=pltpu.CompilerParams(vmem_limit_bytes=VMEM),
        name="suffix_out",
    )(*args, *after)


def prompt_out_kernel(half, skip, far_ref, mid_ref, right_ref, a_ref, b_ref, gain_ref, *refs):
    here = lax.axis_index("seq")
    out_ref = refs[-1]
    gain = gain_ref[...]
    gain2 = jnp.concatenate([gain, gain], axis=1)

    def write(state_of):
        for p in range(mid_ref.shape[0]):
            lanes = slice(p * W2, (p + 1) * W2)
            near = slice((skip + p) * W2, (skip + p + 1) * W2)
            out_ref[0, :, lanes] = low16(finish(a_ref[:, near], state_of(p), b_ref[:, near], gain2))

    @pl.when(here < half)
    def _():
        write(lambda p: far_ref[1, p])

    @pl.when(here == half)
    def _():
        write(lambda p: mid_ref[p])

    @pl.when(here > half)
    def _():
        write(lambda p: right_ref[p])


def prompt_outputs(first, skip, half, far, mid, right, a, b, gain, so_far, width, after=()):
    pairs = mid.shape[0]
    at = first // pairs
    zero3 = lambda i: (0, 0, 0)
    in_specs = [
        pl.BlockSpec(far.shape, lambda i: (0, 0, 0, 0)),
        pl.BlockSpec(mid.shape, zero3),
        pl.BlockSpec(right.shape, zero3),
        pl.BlockSpec(a.shape, lambda i: (0, 0)),
        pl.BlockSpec(b.shape, lambda i: (0, 0)),
        pl.BlockSpec((1, DV), lambda i: (0, 0)),
    ]
    args = [far, mid, right, a, b, gain]
    aliases = {}
    if so_far is not None:
        in_specs.append(ANY)
        args.append(so_far)
        aliases = {6: 0}
    return pl.pallas_call(
        functools.partial(prompt_out_kernel, half, skip),
        grid=(1,),
        in_specs=in_specs + [ANY] * len(after),
        out_specs=pl.BlockSpec((1, CH, pairs * W2), lambda i: (0, 0, at)),
        out_shape=jax.ShapeDtypeStruct((1, CH, width), jnp.bfloat16),
        input_output_aliases=aliases,
        compiler_params=pltpu.CompilerParams(vmem_limit_bytes=VMEM),
        name="prompt_out",
    )(*args, *after)


def pair_product(left, right):
    pairs = left.shape[0]
    left = left.reshape(pairs, DK, 2, DK)
    right = right.reshape(pairs, DK, 2, DV)
    return jnp.einsum("pihj,pjhv->pihv", left, right, precision=HIGH).reshape(pairs, DK, W2)


class Relay:
    def __init__(self, to):
        self.to = to
        self.count = lax.axis_size("seq")
        self.half = self.count // 2
        self.here = lax.axis_index("seq")

    def open(self):
        count, half = self.count, self.half
        sending, far = self.to, None
        for j in range(half - 1):
            arrived = lax.ppermute(sending, "seq", [(j, j + 1), (count - 1 - j, count - 2 - j)])
            far = arrived if far is None else far + arrived
            if j + 2 < half:
                prefix = pair_product(self.to[0], arrived[1]) + self.to[1]
                joined = jnp.stack(
                    [
                        pair_product(arrived[0], self.to[0]),
                        pair_product(arrived[0], self.to[1]) + arrived[1],
                    ]
                )
                sending = jnp.where(self.here < half, jnp.stack([prefix, prefix]), joined)
        self.far = far

    def prefix_job(self):
        return ("step", self.to, self.far)

    def cross(self, prefix):
        self.mid = lax.ppermute(prefix, "seq", [(self.half - 1, self.half)])

    def final_job(self):
        return ("twice", self.to, self.far, self.mid)

    def spread(self, result):
        state, self.final_mid = result
        half, count = self.half, self.count
        self.lefts = [lax.ppermute(self.final_mid, "seq", [(half, d)]) for d in range(half)]
        right = None
        for j in range(half - 1):
            arrived = lax.ppermute(state, "seq", [(half + j, half + j + 1)])
            right = arrived if right is None else right + arrived
            if j + 2 < half:
                state = pair_product(self.to[0], arrived) + self.to[1]
        self.right = right

    def settle(self, after=()):
        self.final = settle(self.to, self.right, self.final_mid, self.lefts, after)
        if self.half > 2:
            inner = (self.here > self.half) & (self.here < self.count - 1)
            done = pair_product(self.far[0], self.final) + self.far[1]
            self.final = jnp.where(inner, done, self.final)
        prompts = lax.axis_size("prompt")
        self.other = lax.ppermute(
            self.final, "prompt", [(i, (i + 1) % prompts) for i in range(prompts)]
        )


def plan_of(pairs):
    if pairs % 4:
        return [[1]] * pairs
    unit = pairs // 4
    return [[unit], [unit, unit, unit]]


def local(
    prompt_queries,
    prompt_keys,
    prompt_values,
    prompt_beta,
    prompt_decay,
    suffix_queries,
    suffix_keys,
    suffix_values,
    suffix_beta,
    suffix_decay,
    norm_gain,
    slot_branch,
    branch_length,
    branch_prompt,
):
    gain = norm_gain.reshape(1, DV)
    tables = (slot_branch, branch_length, branch_prompt)
    width = prompt_values.shape[2]
    prompt_in = (prompt_queries, prompt_keys, prompt_values, prompt_beta, prompt_decay)
    suffix_in = (suffix_queries, suffix_keys, suffix_values, suffix_beta, suffix_decay)
    half = lax.axis_size("seq") // 2

    runs = []
    first = 0
    last = ()
    for sizes in plan_of(width // W2):
        tos, a, b = prompt_terms(first, sizes, *prompt_in, after=last)
        last = (a,)
        skip = 0
        for to, size in zip(tos, sizes):
            relay = Relay(to)
            relay.open()
            runs.append((first + skip, skip, size, a, b, relay))
            skip += size
        first += skip
    total = len(runs)
    made = {}

    def make(index, after):
        if index < total:
            made[index] = suffix_terms(runs[index][0], runs[index][2], *suffix_in, after=after)
            return (made[index][0],)
        return after

    prompt_out, suffix_out = None, None

    def write_prompt(index, after):
        nonlocal prompt_out
        start, skip, size, a, b, relay = runs[index]
        prompt_out = prompt_outputs(
            start, skip, half, relay.far, relay.mid, relay.right, a, b, gain, prompt_out, width, after
        )
        return (prompt_out,)

    def write_suffix(index, after):
        nonlocal suffix_out
        start, skip, size, a, b, relay = runs[index]
        suffix_out = suffix_outputs(
            start, tables, relay.final, relay.other, *made[index], gain, suffix_out, width, after
        )
        return (suffix_out,)

    last = make(0, last)
    last = make(1, last)
    for index in range(total + 1):
        jobs = []
        if index < total:
            jobs.append(runs[index][5].prefix_job())
        if index:
            jobs.append(runs[index - 1][5].final_job())
        results = run_steps(jobs, half, last)
        if index < total:
            prefix = results.pop(0)
            runs[index][5].cross(prefix)
            last = (prefix,)
        if index:
            last = (results[0][0],)
            runs[index - 1][5].spread(results.pop(0))
        last = make(index + 2, last)
        if index >= 2:
            relay = runs[index - 2][5]
            relay.settle(last)
            last = write_prompt(index - 2, (relay.final,))
            last = write_suffix(index - 2, last)
    relay = runs[total - 1][5]
    relay.settle(last)
    last = write_prompt(total - 1, (relay.final,))
    write_suffix(total - 1, last)
    return (prompt_out, suffix_out)


def solution(mesh):
    return jax.shard_map(
        local,
        mesh=mesh,
        in_specs=(
            P(("groups", "prompt"), "seq", "head"),
            P(("groups", "prompt"), "seq", "head"),
            P(("groups", "prompt"), "seq", "head"),
            P(("groups", "prompt"), "head", "seq"),
            P(("groups", "prompt"), "head", "seq"),
            P(("groups", "seq", "prompt"), None, "head"),
            P(("groups", "seq", "prompt"), None, "head"),
            P(("groups", "seq", "prompt"), None, "head"),
            P(("groups", "seq", "prompt"), "head", None),
            P(("groups", "seq", "prompt"), "head", None),
            P(),
            P("groups"),
            P("groups"),
            P("groups"),
        ),
        out_specs=(
            P(("groups", "prompt"), "seq", "head"),
            P(("groups", "seq", "prompt"), None, "head"),
        ),
        check_vma=False,
    )
```

time: 168 us -> 138 us (0.82)
  the two profiles are of different devices: /device:TPU:0 before, /device:TPU:11 now
where the time goes in v1:
time: 138 us; the launch traced here: 137 us
  Pallas kernels  78.7 us (57%)
  starting transfers between devices  35.3 us (26%)
  waiting for transfers between devices  12 us (9%)
  local copies, waits for them, and re-layouts  9.56 us (7%)
    pallas_call x4, Pallas kernels, suffix_terms(): pl.pallas_call(functools.partial(suffix_kernel, first, unit), grid=(1,),...  27 us
    ppermute x4, starting transfers between devices, cross(): self.mid = lax.ppermute(prefix, 'seq', [(self.half - 1, self.half)])  14.9 us
    pallas_call x5, Pallas kernels, run_steps(): pl.pallas_call(functools.partial(step_kernel, kinds, half), in_specs=[who...  12.5 us
    ppermute x8, waiting for transfers between devices, spread(): lax.ppermute(self.final_mid, 'seq', [(half, d)])  11.9 us
    pallas_call x4, Pallas kernels, suffix_outputs(): pl.pallas_call(functools.partial(suffix_out_kernel, unit, slots, lax.axis...  11.1 us
    pallas_call x2, Pallas kernels, prompt_terms(): pl.pallas_call(functools.partial(prompt_kernel, first, sizes, wide, len(q...  10 us
    pallas_call x4, Pallas kernels, prompt_outputs(): pl.pallas_call(functools.partial(prompt_out_kernel, half, skip), grid=(1,...  9.76 us
    unnamed x68, local copies, waits for them, and re-layouts  9.56 us
  transfers between devices with their start and end apart: 24, of which 4 were waited for; matrix products, arithmetic and copies ran while one was open for 0% of the time, Pallas kernels for 48%

profile of v1, /device:TPU:11, one launch (start us, length us, event | category | flops | bytes accessed | tf_op | source)
XLA Modules:
  0.0 136.5 jit_solution(7442369789732421202)
XLA Ops:
  0.6 4.2 %prompt_terms.2 = (f32[2,2,128,256]{3,2,1,0:T(8,128)}, bf16[128,512]{1,0:T(8,128)(2,1)}, bf16[128,512]{1,0:T(8,128)(2,1)}) custom-call(bf16[1,128,1024]{2,1,0:T(8,128)(2,1)} %refs_2_.7, bf16[1,128,1024]{2,1,0:T(8,128)(2,1)} %refs_5_.1, bf16[1,128,2048]{2,1,0:T(8,128)(2,1)} %refs_8_.1, f32[1,16,128]{2,1,0:T(8,128)} %refs_9_.1, f32[1,16,128]{2,1,0:T(8,128)} %refs_10_.1), custom_call_target="tpu_custom_call" | custom-call | tf_op jit(solution)/shard_map/prompt_terms/pallas_call | solution.py:205
  4.8 1.3 collective-permute-start.3
  6.1 5.8 %prompt_terms.3 = (f32[2,2,128,256]{3,2,1,0:T(8,128)}, f32[2,2,128,256]{3,2,1,0:T(8,128)}, f32[2,2,128,256]{3,2,1,0:T(8,128)}, bf16[128,1536]{1,0:T(8,128)(2,1)}, bf16[128,1536]{1,0:T(8,128)(2,1)}) custom-call(bf16[1,128,1024]{2,1,0:T(8,128)(2,1)} %refs_2_.7, bf16[1,128,1024]{2,1,0:T(8,128)(2,1)} %refs_2_.7, bf16[1,128,1024]{2,1,0:T(8,128)(2,1)} %refs_2_.7, ...), custom_call_target="tpu_custom_call" | custom-call | tf_op jit(solution)/shard_map/prompt_terms/pallas_call | solution.py:205
  11.9 1.5 %collective-permute-start.2 = (f32[2,2,128,256]{3,2,1,0:T(8,128)}, f32[2,2,128,256]{3,2,1,0:T(8,128)S(1)}, u32[]{:S(2)}, u32[]{:S(2)}) collective-permute-start(f32[2,2,128,256]{3,2,1,0:T(8,128)} %get-tuple-element.32.refs_0_.refs_2_.to_ref), channel_id=1, source_target_pairs={{0,4},{12,8},{1,5},{13,9},{2,6},{14,10},{3,7},{15,11},{16,20},{28,... | collective-permute-start | bytes 1572872 | tf_op jit(solution)/shard_map/ppermute | solution.py:509
  13.4 6.7 %suffix_terms.4 = (bf16[2,256,512]{2,1,0:T(8,128)(2,1)}, bf16[2,256,512]{2,1,0:T(8,128)(2,1)}) custom-call(bf16[2,256,1024]{2,1,0:T(8,128)(2,1)} %q_ref.7, bf16[2,256,1024]{2,1,0:T(8,128)(2,1)} %k_ref.7, bf16[2,256,2048]{2,1,0:T(8,128)(2,1)} %v_ref.7, f32[2,16,256]{2,1,0:T(8,128)} %beta_ref.7, f32[2,16,256]{2,1,0:T(8,128)} %decay_ref.7, ...), custom_call_target="tpu_custom_call" | custom-call | tf_op jit(solution)/shard_map/suffix_terms/pallas_call | solution.py:268
  20.1 6.8 %suffix_terms.5 = (bf16[2,256,512]{2,1,0:T(8,128)(2,1)}, bf16[2,256,512]{2,1,0:T(8,128)(2,1)}) custom-call(bf16[2,256,1024]{2,1,0:T(8,128)(2,1)} %q_ref.7, bf16[2,256,1024]{2,1,0:T(8,128)(2,1)} %k_ref.7, bf16[2,256,2048]{2,1,0:T(8,128)(2,1)} %v_ref.7, f32[2,16,256]{2,1,0:T(8,128)} %beta_ref.7, f32[2,16,256]{2,1,0:T(8,128)} %decay_ref.7, ...), custom_call_target="tpu_custom_call" | custom-call | tf_op jit(solution)/shard_map/suffix_terms/pallas_call | solution.py:268
  26.9 0.8 copy-done.1
  27.7 2.2 %state_steps.5.refs_0_ = f32[2,128,256]{2,1,0:T(8,128)} custom-call(f32[2,2,128,256]{3,2,1,0:T(8,128)} %get-tuple-element.33.refs_0_.refs_2_.to_ref, f32[2,2,128,256]{3,2,1,0:T(8,128)} %copy-done.1, bf16[2,256,512]{2,1,0:T(8,128)(2,1)} %get-tuple-element.36.refs_2_.refs_5_), custom_call_target="tpu_custom_call" | custom-call | tf_op jit(solution)/shard_map/state_steps/pallas_call | solution.py:322
  29.9 2.9 %collective-permute-start.4 = (f32[2,128,256]{2,1,0:T(8,128)}, f32[2,128,256]{2,1,0:T(8,128)S(1)}, u32[]{:S(2)}, u32[]{:S(2)}) collective-permute-start(f32[2,128,256]{2,1,0:T(8,128)} %state_steps.5.refs_0_), channel_id=1, source_target_pairs={{4,8},{5,9},{6,10},{7,11},{20,24},{21,25},{22,26},{23,27}} | collective-permute-start | bytes 786440 | tf_op jit(solution)/shard_map/ppermute | solution.py:526
  32.9 1.5 %collective-permute-start.1 = (f32[2,2,128,256]{3,2,1,0:T(8,128)S(1)}, f32[2,2,128,256]{3,2,1,0:T(8,128)S(1)}, u32[]{:S(2)}, u32[]{:S(2)}) collective-permute-start(f32[2,2,128,256]{3,2,1,0:T(8,128)S(1)} %copy-done.2), channel_id=1, source_target_pairs={{0,4},{12,8},{1,5},{13,9},{2,6},{14,10},{3,7},{15,11},{16,20},{28,... | collective-permute-start | bytes 1572872 | tf_op jit(solution)/shard_map/ppermute | solution.py:509
  34.4 6.7 %suffix_terms.6 = (bf16[2,256,512]{2,1,0:T(8,128)(2,1)}, bf16[2,256,512]{2,1,0:T(8,128)(2,1)}) custom-call(bf16[2,256,1024]{2,1,0:T(8,128)(2,1)} %q_ref.7, bf16[2,256,1024]{2,1,0:T(8,128)(2,1)} %k_ref.7, bf16[2,256,2048]{2,1,0:T(8,128)(2,1)} %v_ref.7, f32[2,16,256]{2,1,0:T(8,128)} %beta_ref.7, f32[2,16,256]{2,1,0:T(8,128)} %decay_ref.7, ...), custom_call_target="tpu_custom_call" | custom-call | tf_op jit(solution)/shard_map/suffix_terms/pallas_call | solution.py:268
  41.1 0.8 copy-done.5
  42.0 2.7 %state_steps.6 = (f32[2,128,256]{2,1,0:T(8,128)}, f32[2,128,256]{2,1,0:T(8,128)}, f32[2,128,256]{2,1,0:T(8,128)}) custom-call(f32[2,2,128,256]{3,2,1,0:T(8,128)} %get-tuple-element.32.refs_0_.refs_2_.to_ref, f32[2,2,128,256]{3,2,1,0:T(8,128)} %copy-done.5, f32[2,2,128,256]{3,2,1,0:T(8,128)} %get-tuple-element.33.refs_0_.refs_2_.to_ref, ...), custom_call_target="tpu_custom_call" | custom-call | tf_op jit(solution)/shard_map/state_steps/pallas_call | solution.py:322
  44.7 1.6 %collective-permute-start.5 = (f32[2,128,256]{2,1,0:T(8,128)}, f32[2,128,256]{2,1,0:T(8,128)S(1)}, u32[]{:S(2)}, u32[]{:S(2)}) collective-permute-start(f32[2,128,256]{2,1,0:T(8,128)} %get-tuple-element.38), channel_id=1, source_target_pairs={{4,8},{5,9},{6,10},{7,11},{20,24},{21,25},{22,26},{23,27}} | collective-permute-start | bytes 786440 | tf_op jit(solution)/shard_map/ppermute | solution.py:526
  46.3 0.7 collective-permute-start.7
  47.0 0.8 collective-permute-start.8
  47.9 1.3 collective-permute-start.9
  49.2 6.7 %suffix_terms.7 = (bf16[2,256,512]{2,1,0:T(8,128)(2,1)}, bf16[2,256,512]{2,1,0:T(8,128)(2,1)}) custom-call(bf16[2,256,1024]{2,1,0:T(8,128)(2,1)} %q_ref.7, bf16[2,256,1024]{2,1,0:T(8,128)(2,1)} %k_ref.7, bf16[2,256,2048]{2,1,0:T(8,128)(2,1)} %v_ref.7, f32[2,16,256]{2,1,0:T(8,128)} %beta_ref.7, f32[2,16,256]{2,1,0:T(8,128)} %decay_ref.7, ...), custom_call_target="tpu_custom_call" | custom-call | tf_op jit(solution)/shard_map/suffix_terms/pallas_call | solution.py:268
  55.9 1.3 collective-permute-start
  57.2 0.7 copy-done.9
  57.9 2.7 %state_steps.7 = (f32[2,128,256]{2,1,0:T(8,128)}, f32[2,128,256]{2,1,0:T(8,128)}, f32[2,128,256]{2,1,0:T(8,128)}) custom-call(f32[2,2,128,256]{3,2,1,0:T(8,128)} %get-tuple-element.31.refs_0_.refs_2_.to_ref, f32[2,2,128,256]{3,2,1,0:T(8,128)} %copy-done.3, f32[2,2,128,256]{3,2,1,0:T(8,128)} %get-tuple-element.32.refs_0_.refs_2_.to_ref, ...), custom_call_target="tpu_custom_call" | custom-call | tf_op jit(solution)/shard_map/state_steps/pallas_call | solution.py:322
  60.7 1.7 %collective-permute-done.9.refs_1_ = f32[2,128,256]{2,1,0:T(8,128)S(1)} collective-permute-done((f32[2,128,256]{2,1,0:T(8,128)}, f32[2,128,256]{2,1,0:T(8,128)S(1)}, u32[]{:S(2)}, u32[]{:S(2)}) %collective-permute-start.9) | collective-permute-done | bytes 262176 | tf_op jit(solution)/shard_map/ppermute | solution.py:534
  62.4 0.7 copy-done.27
  63.1 2.1 %settle.4.refs_0_.refs_3_ = f32[2,128,256]{2,1,0:T(8,128)} custom-call(f32[2,2,128,256]{3,2,1,0:T(8,128)} %get-tuple-element.33.refs_0_.refs_2_.to_ref, f32[2,128,256]{2,1,0:T(8,128)} %copy-done.8, f32[2,128,256]{2,1,0:T(8,128)} %get-tuple-element.42.mid_ref, f32[2,128,256]{2,1,0:T(8,128)} %copy-done.26, f32[2,128,256]{2,1,0:T(8,128)} %copy-done.27, ...), custom_call_target="tpu_custom_call" | custom-call | tf_op jit(solution)/shard_map/settle/pallas_call | solution.py:363
  65.1 2.2 %collective-permute-start.10 = (f32[2,128,256]{2,1,0:T(8,128)}, f32[2,128,256]{2,1,0:T(8,128)S(1)}, u32[]{:S(2)}, u32[]{:S(2)}) collective-permute-start(f32[2,128,256]{2,1,0:T(8,128)} %settle.4.refs_0_.refs_3_), channel_id=1, source_target_pairs={{0,1},{1,0},{2,3},{3,2},{4,5},{5,4},{6,7},{7,6},{8,9},{9,8},{10,11... | collective-permute-start | bytes 786440 | tf_op jit(solution)/shard_map/ppermute | solution.py:550
  67.3 0.7 collective-permute-start.12
  68.0 7.0 %collective-permute-start.6 = (f32[2,128,256]{2,1,0:T(8,128)S(1)}, f32[2,128,256]{2,1,0:T(8,128)S(1)}, u32[]{:S(2)}, u32[]{:S(2)}) collective-permute-start(f32[2,128,256]{2,1,0:T(8,128)S(1)} %copy-done.32), channel_id=1, source_target_pairs={{4,8},{5,9},{6,10},{7,11},{20,24},{21,25},{22,26},{23,27}} | collective-permute-start | bytes 786440 | tf_op jit(solution)/shard_map/ppermute | solution.py:526
  75.0 0.7 collective-permute-start.13
  75.7 1.3 collective-permute-start.14
  77.0 2.5 %prompt_out.4.refs_8_.refs_0_ = bf16[1,128,2048]{2,1,0:T(8,128)(2,1)} custom-call(f32[2,2,128,256]{3,2,1,0:T(8,128)} %copy-done.1, f32[2,128,256]{2,1,0:T(8,128)} %copy-done.7, f32[2,128,256]{2,1,0:T(8,128)} %copy-done.8, bf16[128,512]{1,0:T(8,128)(2,1)} %get-tuple-element.29.refs_11_.a_ref, bf16[128,512]{1,0:T(8,128)(2,1)} %get-tuple-element.45.b_ref, ...), custom_call_target="tpu_custom_call" | custom-call | tf_op jit(solution)/shard_map/prompt_out/pallas_call | solution.py:479
  79.5 2.8 %suffix_out.4.refs_5_.refs_8_ = bf16[2,256,2048]{2,1,0:T(8,128)(2,1)} custom-call(s32[16]{0:T(128)} %refs_0_.11, s32[16]{0:T(128)} %refs_1_.11, s32[16]{0:T(128)} %refs_2_.11, f32[2,128,256]{2,1,0:T(8,128)} %settle.4.refs_0_.refs_3_, f32[2,128,256]{2,1,0:T(8,128)} %copy-done.29, bf16[2,256,512]{2,1,0:T(8,128)(2,1)} %get-tuple-element.35.refs_0_.refs_5_, ...), custom_call_target="tpu_custom_call" | custom-call | tf_op jit(solution)/shard_map/suffix_out/pallas_call | solution.py:424
  82.3 0.8 copy-done.4
  83.1 0.7 copy-done.6
  83.8 2.8 %state_steps.8 = (f32[2,128,256]{2,1,0:T(8,128)}, f32[2,128,256]{2,1,0:T(8,128)}, f32[2,128,256]{2,1,0:T(8,128)}) custom-call(f32[2,2,128,256]{3,2,1,0:T(8,128)} %get-tuple-element.30.refs_0_.to_ref, f32[2,2,128,256]{3,2,1,0:T(8,128)} %copy-done.4, f32[2,2,128,256]{3,2,1,0:T(8,128)} %get-tuple-element.31.refs_0_.refs_2_.to_ref, ...), custom_call_target="tpu_custom_call" | custom-call | tf_op jit(solution)/shard_map/state_steps/pallas_call | solution.py:322
  86.6 1.1 collective-permute-done.14.refs_1_
  87.7 0.7 copy-done.24
  88.4 2.1 %settle.5.refs_1_.refs_3_ = f32[2,128,256]{2,1,0:T(8,128)} custom-call(f32[2,2,128,256]{3,2,1,0:T(8,128)} %get-tuple-element.32.refs_0_.refs_2_.to_ref, f32[2,128,256]{2,1,0:T(8,128)} %copy-done.11, f32[2,128,256]{2,1,0:T(8,128)} %get-tuple-element.47.mid_ref, f32[2,128,256]{2,1,0:T(8,128)} %copy-done.22, f32[2,128,256]{2,1,0:T(8,128)} %copy-done.24, ...), custom_call_target="tpu_custom_call" | custom-call | tf_op jit(solution)/shard_map/settle/pallas_call | solution.py:363
  90.5 0.8 collective-permute-start.15
  91.3 3.4 %collective-permute-start.11 = (f32[2,128,256]{2,1,0:T(8,128)S(1)}, f32[2,128,256]{2,1,0:T(8,128)S(1)}, u32[]{:S(2)}, u32[]{:S(2)}) collective-permute-start(f32[2,128,256]{2,1,0:T(8,128)S(1)} %copy-done.33), channel_id=1, source_target_pairs={{4,8},{5,9},{6,10},{7,11},{20,24},{21,25},{22,26},{23,27}} | collective-permute-start | bytes 786440 | tf_op jit(solution)/shard_map/ppermute | solution.py:526
  94.7 0.7 collective-permute-start.17
  95.4 0.7 collective-permute-start.18
  96.1 1.3 collective-permute-start.19
  97.4 2.4 %prompt_out.5.refs_9_.refs_0_ = bf16[1,128,2048]{2,1,0:T(8,128)(2,1)} custom-call(f32[2,2,128,256]{3,2,1,0:T(8,128)} %copy-done.5, f32[2,128,256]{2,1,0:T(8,128)} %copy-done.9, f32[2,128,256]{2,1,0:T(8,128)} %copy-done.11, bf16[128,1536]{1,0:T(8,128)(2,1)} %get-tuple-element.34.refs_0_.a_ref, ...), custom_call_target="tpu_custom_call", output_to_operand_aliasing={{}: (6, {})} | custom-call | tf_op jit(solution)/shard_map/prompt_out/pallas_call | solution.py:479
  99.8 0.7 copy-done.14
  100.5 2.8 %suffix_out.5.refs_3_.refs_8_ = bf16[2,256,2048]{2,1,0:T(8,128)(2,1)} custom-call(s32[16]{0:T(128)} %refs_0_.11, s32[16]{0:T(128)} %refs_1_.11, s32[16]{0:T(128)} %refs_2_.11, f32[2,128,256]{2,1,0:T(8,128)} %settle.5.refs_1_.refs_3_, f32[2,128,256]{2,1,0:T(8,128)} %copy-done.14, ...), custom_call_target="tpu_custom_call", output_to_operand_aliasing={{}: (8, {})} | custom-call | tf_op jit(solution)/shard_map/suffix_out/pallas_call | solution.py:424
  103.3 0.7 copy-done.10
  104.0 2.1 %state_steps.9 = (f32[2,128,256]{2,1,0:T(8,128)}, f32[2,128,256]{2,1,0:T(8,128)}) custom-call(f32[2,2,128,256]{3,2,1,0:T(8,128)} %get-tuple-element.30.refs_0_.to_ref, f32[2,2,128,256]{3,2,1,0:T(8,128)} %copy-done.4, f32[2,128,256]{2,1,0:T(8,128)} %copy-done.10, bf16[2,256,2048]{2,1,0:T(8,128)(2,1)} %suffix_out.5.refs_3_.refs_8_), custom_call_target="tpu_custom_call" | custom-call | tf_op jit(solution)/shard_map/state_steps/pallas_call | solution.py:322
  106.2 2.8 %collective-permute-done.19.refs_1_ = f32[2,128,256]{2,1,0:T(8,128)S(1)} collective-permute-done((f32[2,128,256]{2,1,0:T(8,128)S(1)}, f32[2,128,256]{2,1,0:T(8,128)S(1)}, u32[]{:S(2)}, u32[]{:S(2)}) %collective-permute-start.19) | collective-permute-done | bytes 262176 | tf_op jit(solution)/shard_map/ppermute | solution.py:534
  109.0 0.7 copy-done.25
  109.7 2.1 %settle.6.refs_1_.refs_3_ = f32[2,128,256]{2,1,0:T(8,128)} custom-call(f32[2,2,128,256]{3,2,1,0:T(8,128)} %get-tuple-element.31.refs_0_.refs_2_.to_ref, f32[2,128,256]{2,1,0:T(8,128)} %copy-done.12, f32[2,128,256]{2,1,0:T(8,128)} %get-tuple-element.52.mid_ref, f32[2,128,256]{2,1,0:T(8,128)} %copy-done.23, f32[2,128,256]{2,1,0:T(8,128)} %copy-done.25, ...), custom_call_target="tpu_custom_call" | custom-call | tf_op jit(solution)/shard_map/settle/pallas_call | solution.py:363
  111.8 0.6 collective-permute-start.22
  112.4 0.7 collective-permute-start.16
  113.1 0.7 collective-permute-start.20
  113.7 1.3 collective-permute-start.21
  115.0 2.4 %prompt_out.6.refs_9_.refs_0_ = bf16[1,128,2048]{2,1,0:T(8,128)(2,1)} custom-call(f32[2,2,128,256]{3,2,1,0:T(8,128)} %copy-done.3, f32[2,128,256]{2,1,0:T(8,128)} %copy-done.6, f32[2,128,256]{2,1,0:T(8,128)} %copy-done.12, bf16[128,1536]{1,0:T(8,128)(2,1)} %get-tuple-element.34.refs_0_.a_ref, ...), custom_call_target="tpu_custom_call", output_to_operand_aliasing={{}: (6, {})} | custom-call | tf_op jit(solution)/shard_map/prompt_out/pallas_call | solution.py:479
  117.5 0.7 copy-done.15
  118.2 2.8 %suffix_out.6.refs_2_.refs_8_ = bf16[2,256,2048]{2,1,0:T(8,128)(2,1)} custom-call(s32[16]{0:T(128)} %refs_0_.11, s32[16]{0:T(128)} %refs_1_.11, s32[16]{0:T(128)} %refs_2_.11, f32[2,128,256]{2,1,0:T(8,128)} %settle.6.refs_1_.refs_3_, f32[2,128,256]{2,1,0:T(8,128)} %copy-done.15, ...), custom_call_target="tpu_custom_call", output_to_operand_aliasing={{}: (8, {})} | custom-call | tf_op jit(solution)/shard_map/suffix_out/pallas_call | solution.py:424
  121.0 6.3 %collective-permute-done.21.refs_1_ = f32[2,128,256]{2,1,0:T(8,128)S(1)} collective-permute-done((f32[2,128,256]{2,1,0:T(8,128)S(1)}, f32[2,128,256]{2,1,0:T(8,128)S(1)}, u32[]{:S(2)}, u32[]{:S(2)}) %collective-permute-start.21) | collective-permute-done | bytes 262176 | tf_op jit(solution)/shard_map/ppermute | solution.py:534
  127.3 0.7 copy-done.31
  128.0 2.1 %settle.7.refs_1_.refs_3_ = f32[2,128,256]{2,1,0:T(8,128)} custom-call(f32[2,2,128,256]{3,2,1,0:T(8,128)} %get-tuple-element.30.refs_0_.to_ref, f32[2,128,256]{2,1,0:T(8,128)} %copy-done.13, f32[2,128,256]{2,1,0:T(8,128)} %get-tuple-element.53.mid_ref, f32[2,128,256]{2,1,0:T(8,128)} %copy-done.30, f32[2,128,256]{2,1,0:T(8,128)} %copy-done.31, ...), custom_call_target="tpu_custom_call" | custom-call | tf_op jit(solution)/shard_map/settle/pallas_call | solution.py:363
  130.1 0.6 collective-permute-start.23
  130.7 2.4 %prompt_out.7.refs_9_ = bf16[1,128,2048]{2,1,0:T(8,128)(2,1)} custom-call(f32[2,2,128,256]{3,2,1,0:T(8,128)} %copy-done.4, f32[2,128,256]{2,1,0:T(8,128)} %copy-done.10, f32[2,128,256]{2,1,0:T(8,128)} %copy-done.13, bf16[128,1536]{1,0:T(8,128)(2,1)} %get-tuple-element.34.refs_0_.a_ref, ...), custom_call_target="tpu_custom_call", output_to_operand_aliasing={{}: (6, {})} | custom-call | tf_op jit(solution)/shard_map/prompt_out/pallas_call | solution.py:479
  133.1 0.7 copy-done.16
  133.8 2.8 %suffix_out.7 = bf16[2,256,2048]{2,1,0:T(8,128)(2,1)} custom-call(s32[16]{0:T(128)} %refs_0_.11, s32[16]{0:T(128)} %refs_1_.11, s32[16]{0:T(128)} %refs_2_.11, f32[2,128,256]{2,1,0:T(8,128)} %settle.7.refs_1_.refs_3_, f32[2,128,256]{2,1,0:T(8,128)} %copy-done.16, bf16[2,256,512]{2,1,0:T(8,128)(2,1)} %get-tuple-element.40.refs_5_, ...), custom_call_target="tpu_custom_call", output_to_operand_aliasing={{}: (8, {})} | custom-call | tf_op jit(solution)/shard_map/suffix_out/pallas_call | solution.py:424
  (75 shorter events, 0.3 us)
Async XLA Ops:
  4.8 22.1 %collective-permute-start.3 = (f32[2,2,128,256]{3,2,1,0:T(8,128)}, f32[2,2,128,256]{3,2,1,0:T(8,128)S(1)}, u32[]{:S(2)}, u32[]{:S(2)}) collective-permute-start(f32[2,2,128,256]{3,2,1,0:T(8,128)} %get-tuple-element.33.refs_0_.refs_2_.to_ref), channel_id=1, source_target_pairs={{0,4},{12,8},{1,5},{13,9},{2,6},{14,10},{3,7},{15,11},{16,20},{28,... | collective-permute-start | bytes 1572872 | tf_op jit(solution)/shard_map/ppermute | solution.py:509
  11.9 29.2 %collective-permute-start.2 = (f32[2,2,128,256]{3,2,1,0:T(8,128)}, f32[2,2,128,256]{3,2,1,0:T(8,128)S(1)}, u32[]{:S(2)}, u32[]{:S(2)}) collective-permute-start(f32[2,2,128,256]{3,2,1,0:T(8,128)} %get-tuple-element.32.refs_0_.refs_2_.to_ref), channel_id=1, source_target_pairs={{0,4},{12,8},{1,5},{13,9},{2,6},{14,10},{3,7},{15,11},{16,20},{28,... | collective-permute-start | bytes 1572872 | tf_op jit(solution)/shard_map/ppermute | solution.py:509
  20.1 12.7 %copy-start.2 = (f32[2,2,128,256]{3,2,1,0:T(8,128)S(1)}, f32[2,2,128,256]{3,2,1,0:T(8,128)}, u32[]{:S(2)}) copy-start(f32[2,2,128,256]{3,2,1,0:T(8,128)} %get-tuple-element.31.refs_0_.refs_2_.to_ref) | copy-start | bytes 1572868
  26.9 0.8 copy-start.1
  29.9 11.2 %collective-permute-start.4 = (f32[2,128,256]{2,1,0:T(8,128)}, f32[2,128,256]{2,1,0:T(8,128)S(1)}, u32[]{:S(2)}, u32[]{:S(2)}) collective-permute-start(f32[2,128,256]{2,1,0:T(8,128)} %state_steps.5.refs_0_), channel_id=1, source_target_pairs={{4,8},{5,9},{6,10},{7,11},{20,24},{21,25},{22,26},{23,27}} | collective-permute-start | bytes 786440 | tf_op jit(solution)/shard_map/ppermute | solution.py:526
  32.9 23.0 %collective-permute-start.1 = (f32[2,2,128,256]{3,2,1,0:T(8,128)S(1)}, f32[2,2,128,256]{3,2,1,0:T(8,128)S(1)}, u32[]{:S(2)}, u32[]{:S(2)}) collective-permute-start(f32[2,2,128,256]{3,2,1,0:T(8,128)S(1)} %copy-done.2), channel_id=1, source_target_pairs={{0,4},{12,8},{1,5},{13,9},{2,6},{14,10},{3,7},{15,11},{16,20},{28,... | collective-permute-start | bytes 1572872 | tf_op jit(solution)/shard_map/ppermute | solution.py:509
  41.1 0.8 copy-start.5
  41.1 0.9 copy-start.7
  44.7 12.4 %collective-permute-start.5 = (f32[2,128,256]{2,1,0:T(8,128)}, f32[2,128,256]{2,1,0:T(8,128)S(1)}, u32[]{:S(2)}, u32[]{:S(2)}) collective-permute-start(f32[2,128,256]{2,1,0:T(8,128)} %get-tuple-element.38), channel_id=1, source_target_pairs={{4,8},{5,9},{6,10},{7,11},{20,24},{21,25},{22,26},{23,27}} | collective-permute-start | bytes 786440 | tf_op jit(solution)/shard_map/ppermute | solution.py:526
  46.3 14.3 %collective-permute-start.7 = (f32[2,128,256]{2,1,0:T(8,128)}, f32[2,128,256]{2,1,0:T(8,128)S(1)}, u32[]{:S(2)}, u32[]{:S(2)}) collective-permute-start(f32[2,128,256]{2,1,0:T(8,128)} %get-tuple-element.39.refs_0_), channel_id=1, source_target_pairs={{8,12},{9,13},{10,14},{11,15},{24,28},{25,29},{26,30},{27,31}} | collective-permute-start | bytes 786440 | tf_op jit(solution)/shard_map/ppermute | solution.py:537
  47.0 8.8 %copy-start = (f32[2,2,128,256]{3,2,1,0:T(8,128)S(1)}, f32[2,2,128,256]{3,2,1,0:T(8,128)}, u32[]{:S(2)}) copy-start(f32[2,2,128,256]{3,2,1,0:T(8,128)} %get-tuple-element.30.refs_0_.to_ref) | copy-start | bytes 1572868
  47.0 13.6 %collective-permute-start.8 = (f32[2,128,256]{2,1,0:T(8,128)}, f32[2,128,256]{2,1,0:T(8,128)S(1)}, u32[]{:S(2)}, u32[]{:S(2)}) collective-permute-start(f32[2,128,256]{2,1,0:T(8,128)} %get-tuple-element.42.mid_ref), channel_id=1, source_target_pairs={{8,0},{9,1},{10,2},{11,3},{24,16},{25,17},{26,18},{27,19}} | collective-permute-start | bytes 786440 | tf_op jit(solution)/shard_map/ppermute | solution.py:534
  47.9 14.5 %collective-permute-start.9 = (f32[2,128,256]{2,1,0:T(8,128)}, f32[2,128,256]{2,1,0:T(8,128)S(1)}, u32[]{:S(2)}, u32[]{:S(2)}) collective-permute-start(f32[2,128,256]{2,1,0:T(8,128)} %get-tuple-element.42.mid_ref), channel_id=1, source_target_pairs={{8,4},{9,5},{10,6},{11,7},{24,20},{25,21},{26,22},{27,23}} | collective-permute-start | bytes 786440 | tf_op jit(solution)/shard_map/ppermute | solution.py:534
  55.9 1.3 copy-start.3
  55.9 26.4 %collective-permute-start = (f32[2,2,128,256]{3,2,1,0:T(8,128)S(1)}, f32[2,2,128,256]{3,2,1,0:T(8,128)S(1)}, u32[]{:S(2)}, u32[]{:S(2)}) collective-permute-start(f32[2,2,128,256]{3,2,1,0:T(8,128)S(1)} %copy-done), channel_id=1, source_target_pairs={{0,4},{12,8},{1,5},{13,9},{2,6},{14,10},{3,7},{15,11},{16,20},{28,... | collective-permute-start | bytes 1572872 | tf_op jit(solution)/shard_map/ppermute | solution.py:509
  57.2 0.7 copy-start.9
  60.6 6.7 %copy-start.19 = (f32[2,128,256]{2,1,0:T(8,128)S(1)}, f32[2,128,256]{2,1,0:T(8,128)}, u32[]{:S(2)}) copy-start(f32[2,128,256]{2,1,0:T(8,128)} %get-tuple-element.43.refs_2_) | copy-start | bytes 786436
  60.6 7.3 %copy-start.32 = (f32[2,128,256]{2,1,0:T(8,128)S(1)}, f32[2,128,256]{2,1,0:T(8,128)}, u32[]{:S(2)}) copy-start(f32[2,128,256]{2,1,0:T(8,128)} %get-tuple-element.41) | copy-start | bytes 786436
  60.6 14.3 %copy-start.17 = (f32[2,128,256]{2,1,0:T(8,128)S(1)}, f32[2,128,256]{2,1,0:T(8,128)}, u32[]{:S(2)}) copy-start(f32[2,128,256]{2,1,0:T(8,128)} %get-tuple-element.47.mid_ref) | copy-start | bytes 786436
  60.7 1.7 %copy-start.8 = (f32[2,128,256]{2,1,0:T(8,128)}, f32[2,128,256]{2,1,0:T(8,128)S(1)}, u32[]{:S(2)}) copy-start(f32[2,128,256]{2,1,0:T(8,128)S(1)} %collective-permute-done.7.right_ref) | copy-start | bytes 786436
  60.7 1.7 %copy-start.26 = (f32[2,128,256]{2,1,0:T(8,128)}, f32[2,128,256]{2,1,0:T(8,128)S(1)}, u32[]{:S(2)}) copy-start(f32[2,128,256]{2,1,0:T(8,128)S(1)} %collective-permute-done.8.refs_0_) | copy-start | bytes 786436
  62.4 0.7 copy-start.27
  65.1 10.5 %collective-permute-start.10 = (f32[2,128,256]{2,1,0:T(8,128)}, f32[2,128,256]{2,1,0:T(8,128)S(1)}, u32[]{:S(2)}, u32[]{:S(2)}) collective-permute-start(f32[2,128,256]{2,1,0:T(8,128)} %settle.4.refs_0_.refs_3_), channel_id=1, source_target_pairs={{0,1},{1,0},{2,3},{3,2},{4,5},{5,4},{6,7},{7,6},{8,9},{9,8},{10,11... | collective-permute-start | bytes 786440 | tf_op jit(solution)/shard_map/ppermute | solution.py:550
  67.3 19.3 %collective-permute-start.12 = (f32[2,128,256]{2,1,0:T(8,128)S(1)}, f32[2,128,256]{2,1,0:T(8,128)S(1)}, u32[]{:S(2)}, u32[]{:S(2)}) collective-permute-start(f32[2,128,256]{2,1,0:T(8,128)S(1)} %copy-done.19), channel_id=1, source_target_pairs={{8,12},{9,13},{10,14},{11,15},{24,28},{25,29},{26,30},{27,31}} | collective-permute-start | bytes 786440 | tf_op jit(solution)/shard_map/ppermute | solution.py:537
  68.0 14.3 %collective-permute-start.6 = (f32[2,128,256]{2,1,0:T(8,128)S(1)}, f32[2,128,256]{2,1,0:T(8,128)S(1)}, u32[]{:S(2)}, u32[]{:S(2)}) collective-permute-start(f32[2,128,256]{2,1,0:T(8,128)S(1)} %copy-done.32), channel_id=1, source_target_pairs={{4,8},{5,9},{6,10},{7,11},{20,24},{21,25},{22,26},{23,27}} | collective-permute-start | bytes 786440 | tf_op jit(solution)/shard_map/ppermute | solution.py:526
  75.0 11.6 %collective-permute-start.13 = (f32[2,128,256]{2,1,0:T(8,128)S(1)}, f32[2,128,256]{2,1,0:T(8,128)S(1)}, u32[]{:S(2)}, u32[]{:S(2)}) collective-permute-start(f32[2,128,256]{2,1,0:T(8,128)S(1)} %copy-done.17), channel_id=1, source_target_pairs={{8,0},{9,1},{10,2},{11,3},{24,16},{25,17},{26,18},{27,19}} | collective-permute-start | bytes 786440 | tf_op jit(solution)/shard_map/ppermute | solution.py:534
  75.7 3.8 %copy-start.29 = (f32[2,128,256]{2,1,0:T(8,128)}, f32[2,128,256]{2,1,0:T(8,128)S(1)}, u32[]{:S(2)}) copy-start(f32[2,128,256]{2,1,0:T(8,128)S(1)} %collective-permute-done.10.refs_4_) | copy-start | bytes 786436
  75.7 12.0 %collective-permute-start.14 = (f32[2,128,256]{2,1,0:T(8,128)S(1)}, f32[2,128,256]{2,1,0:T(8,128)S(1)}, u32[]{:S(2)}, u32[]{:S(2)}) collective-permute-start(f32[2,128,256]{2,1,0:T(8,128)S(1)} %copy-done.17), channel_id=1, source_target_pairs={{8,4},{9,5},{10,6},{11,7},{24,20},{25,21},{26,22},{27,23}} | collective-permute-start | bytes 786440 | tf_op jit(solution)/shard_map/ppermute | solution.py:534
  82.3 0.8 copy-start.4
  83.1 0.7 copy-start.6
  86.6 4.7 %copy-start.33 = (f32[2,128,256]{2,1,0:T(8,128)S(1)}, f32[2,128,256]{2,1,0:T(8,128)}, u32[]{:S(2)}) copy-start(f32[2,128,256]{2,1,0:T(8,128)} %get-tuple-element.46) | copy-start | bytes 786436
  86.6 8.1 %copy-start.20 = (f32[2,128,256]{2,1,0:T(8,128)S(1)}, f32[2,128,256]{2,1,0:T(8,128)}, u32[]{:S(2)}) copy-start(f32[2,128,256]{2,1,0:T(8,128)} %get-tuple-element.48.refs_2_) | copy-start | bytes 786436
  86.6 8.8 %copy-start.18 = (f32[2,128,256]{2,1,0:T(8,128)S(1)}, f32[2,128,256]{2,1,0:T(8,128)}, u32[]{:S(2)}) copy-start(f32[2,128,256]{2,1,0:T(8,128)} %get-tuple-element.52.mid_ref) | copy-start | bytes 786436
  86.6 1.1 copy-start.11
  86.6 1.1 copy-start.22
  87.7 0.7 copy-start.24
  90.5 9.3 %collective-permute-start.15 = (f32[2,128,256]{2,1,0:T(8,128)}, f32[2,128,256]{2,1,0:T(8,128)S(1)}, u32[]{:S(2)}, u32[]{:S(2)}) collective-permute-start(f32[2,128,256]{2,1,0:T(8,128)} %settle.5.refs_1_.refs_3_), channel_id=1, source_target_pairs={{0,1},{1,0},{2,3},{3,2},{4,5},{5,4},{6,7},{7,6},{8,9},{9,8},{10,11... | collective-permute-start | bytes 786440 | tf_op jit(solution)/shard_map/ppermute | solution.py:550
  91.3 12.0 %collective-permute-start.11 = (f32[2,128,256]{2,1,0:T(8,128)S(1)}, f32[2,128,256]{2,1,0:T(8,128)S(1)}, u32[]{:S(2)}, u32[]{:S(2)}) collective-permute-start(f32[2,128,256]{2,1,0:T(8,128)S(1)} %copy-done.33), channel_id=1, source_target_pairs={{4,8},{5,9},{6,10},{7,11},{20,24},{21,25},{22,26},{23,27}} | collective-permute-start | bytes 786440 | tf_op jit(solution)/shard_map/ppermute | solution.py:526
  94.7 11.4 %collective-permute-start.17 = (f32[2,128,256]{2,1,0:T(8,128)S(1)}, f32[2,128,256]{2,1,0:T(8,128)S(1)}, u32[]{:S(2)}, u32[]{:S(2)}) collective-permute-start(f32[2,128,256]{2,1,0:T(8,128)S(1)} %copy-done.20), channel_id=1, source_target_pairs={{8,12},{9,13},{10,14},{11,15},{24,28},{25,29},{26,30},{27,31}} | collective-permute-start | bytes 786440 | tf_op jit(solution)/shard_map/ppermute | solution.py:537
  95.4 10.7 %collective-permute-start.18 = (f32[2,128,256]{2,1,0:T(8,128)S(1)}, f32[2,128,256]{2,1,0:T(8,128)S(1)}, u32[]{:S(2)}, u32[]{:S(2)}) collective-permute-start(f32[2,128,256]{2,1,0:T(8,128)S(1)} %copy-done.18), channel_id=1, source_target_pairs={{8,0},{9,1},{10,2},{11,3},{24,16},{25,17},{26,18},{27,19}} | collective-permute-start | bytes 786440 | tf_op jit(solution)/shard_map/ppermute | solution.py:534
  96.1 12.9 %collective-permute-start.19 = (f32[2,128,256]{2,1,0:T(8,128)S(1)}, f32[2,128,256]{2,1,0:T(8,128)S(1)}, u32[]{:S(2)}, u32[]{:S(2)}) collective-permute-start(f32[2,128,256]{2,1,0:T(8,128)S(1)} %copy-done.18), channel_id=1, source_target_pairs={{8,4},{9,5},{10,6},{11,7},{24,20},{25,21},{26,22},{27,23}} | collective-permute-start | bytes 786440 | tf_op jit(solution)/shard_map/ppermute | solution.py:534
  99.8 0.7 copy-start.14
  103.3 0.7 copy-start.10
  106.1 6.3 %copy-start.21 = (f32[2,128,256]{2,1,0:T(8,128)S(1)}, f32[2,128,256]{2,1,0:T(8,128)}, u32[]{:S(2)}) copy-start(f32[2,128,256]{2,1,0:T(8,128)} %get-tuple-element.51.refs_2_) | copy-start | bytes 786436
  106.1 6.9 %copy-start.28 = (f32[2,128,256]{2,1,0:T(8,128)S(1)}, f32[2,128,256]{2,1,0:T(8,128)}, u32[]{:S(2)}) copy-start(f32[2,128,256]{2,1,0:T(8,128)} %get-tuple-element.53.mid_ref) | copy-start | bytes 786436
  106.1 2.9 %copy-start.12 = (f32[2,128,256]{2,1,0:T(8,128)}, f32[2,128,256]{2,1,0:T(8,128)S(1)}, u32[]{:S(2)}) copy-start(f32[2,128,256]{2,1,0:T(8,128)S(1)} %collective-permute-done.17.right_ref) | copy-start | bytes 786436
  106.2 2.9 %copy-start.23 = (f32[2,128,256]{2,1,0:T(8,128)}, f32[2,128,256]{2,1,0:T(8,128)S(1)}, u32[]{:S(2)}) copy-start(f32[2,128,256]{2,1,0:T(8,128)S(1)} %collective-permute-done.18.refs_0_) | copy-start | bytes 786436
  109.0 0.7 copy-start.25
  111.8 5.7 %collective-permute-start.22 = (f32[2,128,256]{2,1,0:T(8,128)}, f32[2,128,256]{2,1,0:T(8,128)S(1)}, u32[]{:S(2)}, u32[]{:S(2)}) collective-permute-start(f32[2,128,256]{2,1,0:T(8,128)} %settle.6.refs_1_.refs_3_), channel_id=1, source_target_pairs={{0,1},{1,0},{2,3},{3,2},{4,5},{5,4},{6,7},{7,6},{8,9},{9,8},{10,11... | collective-permute-start | bytes 786440 | tf_op jit(solution)/shard_map/ppermute | solution.py:550
  112.4 8.6 %collective-permute-start.16 = (f32[2,128,256]{2,1,0:T(8,128)S(1)}, f32[2,128,256]{2,1,0:T(8,128)S(1)}, u32[]{:S(2)}, u32[]{:S(2)}) collective-permute-start(f32[2,128,256]{2,1,0:T(8,128)S(1)} %copy-done.21), channel_id=1, source_target_pairs={{8,12},{9,13},{10,14},{11,15},{24,28},{25,29},{26,30},{27,31}} | collective-permute-start | bytes 786440 | tf_op jit(solution)/shard_map/ppermute | solution.py:537
  113.1 7.9 %collective-permute-start.20 = (f32[2,128,256]{2,1,0:T(8,128)S(1)}, f32[2,128,256]{2,1,0:T(8,128)S(1)}, u32[]{:S(2)}, u32[]{:S(2)}) collective-permute-start(f32[2,128,256]{2,1,0:T(8,128)S(1)} %copy-done.28), channel_id=1, source_target_pairs={{8,0},{9,1},{10,2},{11,3},{24,16},{25,17},{26,18},{27,19}} | collective-permute-start | bytes 786440 | tf_op jit(solution)/shard_map/ppermute | solution.py:534
  113.7 13.5 %collective-permute-start.21 = (f32[2,128,256]{2,1,0:T(8,128)S(1)}, f32[2,128,256]{2,1,0:T(8,128)S(1)}, u32[]{:S(2)}, u32[]{:S(2)}) collective-permute-start(f32[2,128,256]{2,1,0:T(8,128)S(1)} %copy-done.28), channel_id=1, source_target_pairs={{8,4},{9,5},{10,6},{11,7},{24,20},{25,21},{26,22},{27,23}} | collective-permute-start | bytes 786440 | tf_op jit(solution)/shard_map/ppermute | solution.py:534
  117.5 0.7 copy-start.15
  120.9 6.3 %copy-start.13 = (f32[2,128,256]{2,1,0:T(8,128)}, f32[2,128,256]{2,1,0:T(8,128)S(1)}, u32[]{:S(2)}) copy-start(f32[2,128,256]{2,1,0:T(8,128)S(1)} %collective-permute-done.16.right_ref) | copy-start | bytes 786436
  121.0 6.3 %copy-start.30 = (f32[2,128,256]{2,1,0:T(8,128)}, f32[2,128,256]{2,1,0:T(8,128)S(1)}, u32[]{:S(2)}) copy-start(f32[2,128,256]{2,1,0:T(8,128)S(1)} %collective-permute-done.20.refs_0_) | copy-start | bytes 786436
  127.3 0.7 copy-start.31
  130.1 3.0 %collective-permute-start.23 = (f32[2,128,256]{2,1,0:T(8,128)}, f32[2,128,256]{2,1,0:T(8,128)S(1)}, u32[]{:S(2)}, u32[]{:S(2)}) collective-permute-start(f32[2,128,256]{2,1,0:T(8,128)} %settle.7.refs_1_.refs_3_), channel_id=1, source_target_pairs={{0,1},{1,0},{2,3},{3,2},{4,5},{5,4},{6,7},{7,6},{8,9},{9,8},{10,11... | collective-permute-start | bytes 786440 | tf_op jit(solution)/shard_map/ppermute | solution.py:550
  133.1 0.7 copy-start.16

commit v2 on v1

--- a/solution.py
+++ b/solution.py
@@ -14,7 +14,7 @@
 W2 = 2 * DV
 EPS_NORM = 1e-06
 HIGH = lax.Precision.HIGHEST
-VMEM = 56 * 1024 * 1024
+SCOPED = 24 * 1024 * 1024
 
 
 def mm(left, right):
@@ -133,14 +133,14 @@
     return out
 
 
-def read_chains(pairs, heads, at, q_ref, k_ref, v_ref, beta_ref, decay_ref, slot):
+def read_chains(pairs, heads, at, q_ref, k_ref, v_ref, beta_ref, decay_ref, slot, skip=0):
     beta = beta_ref[slot, heads, at]
     cum_r, cum_c = gate_tables(decay_ref[slot, heads, at])
     return [
         (
-            q_ref[slot, at, p * DK : (p + 1) * DK],
-            k_ref[slot, at, p * DK : (p + 1) * DK],
-            v_ref[slot, at, p * W2 : (p + 1) * W2],
+            q_ref[slot, at, (skip + p) * DK : (skip + p + 1) * DK],
+            k_ref[slot, at, (skip + p) * DK : (skip + p + 1) * DK],
+            v_ref[slot, at, (skip + p) * W2 : (skip + p + 1) * W2],
             beta[2 * p : 2 * p + 2],
             cum_r[2 * p : 2 * p + 2],
             cum_c[:, 2 * p : 2 * p + 2],
@@ -165,6 +165,18 @@
 
 
 ANY = pl.BlockSpec(memory_space=pl.ANY)
+WHOLE = pl.BlockSpec(memory_space=pltpu.VMEM)
+
+
+SHORT = pl.CostEstimate(flops=1, transcendentals=0, bytes_accessed=1)
+
+
+def near(value):
+    return pltpu.with_memory_space_constraint(value, pltpu.VMEM)
+
+
+def away(value):
+    return pltpu.with_memory_space_constraint(value, pltpu.HBM)
 
 
 class Spans:
@@ -175,6 +187,10 @@
         lanes = key[-1]
         part, at = divmod(lanes.start, self.size)
         return self.refs[part][key[:-1] + (slice(at, at + lanes.stop - lanes.start),)]
+
+
+def places_of(sizes):
+    return [(run, at) for run, size in enumerate(sizes) for at in range(size)]
 
 
 def prompt_kernel(first, sizes, wide, count, *refs):
@@ -188,7 +204,7 @@
     chains = read_chains(
         pairs, heads, slice(0, CH), q_ref, k_ref, v_ref, beta_ref, decay_ref, 0
     )
-    places = [(c, p) for c, size in enumerate(sizes) for p in range(size)]
+    places = places_of(sizes)
     for p, (a, b, transfer, offset) in enumerate(chunk_terms(chains)):
         outs[-2][:, p * W2 : (p + 1) * W2] = low16(a)
         outs[-1][:, p * W2 : (p + 1) * W2] = low16(b)
@@ -213,13 +229,13 @@
             pl.BlockSpec(decay.shape, lambda i: (0, 0, 0)),
         ]
         + [ANY] * len(after),
-        out_specs=[pl.BlockSpec((2, size, DK, W2), lambda i: (0, 0, 0, 0)) for size in sizes]
-        + [pl.BlockSpec((CH, pairs * W2), lambda i: (0, 0))] * 2,
-        out_shape=[jax.ShapeDtypeStruct((2, size, DK, W2), jnp.float32) for size in sizes]
-        + [jax.ShapeDtypeStruct((CH, pairs * W2), jnp.bfloat16)] * 2,
-        compiler_params=pltpu.CompilerParams(vmem_limit_bytes=VMEM),
+        out_specs=[WHOLE] * (len(sizes) + 2),
+        out_shape=[pltpu.VMEM((2, size, DK, W2), jnp.float32) for size in sizes]
+        + [pltpu.VMEM((CH, pairs * W2), jnp.bfloat16)] * 2,
+        compiler_params=pltpu.CompilerParams(vmem_limit_bytes=SCOPED),
+        cost_estimate=SHORT,
         name="prompt_terms",
-    )(*q_args, *k_args, *v_args, beta, decay, *after)
+    )(*[away(value) for value in (*q_args, *k_args, *v_args, beta, decay)], *after)
     return tos, a, b
 
 
@@ -231,16 +247,9 @@
     chains = []
     for slot in range(slots):
         for s in range(spans):
+            at = slice(s * CH, (s + 1) * CH)
             chains += read_chains(
-                unit,
-                heads,
-                slice(s * CH, (s + 1) * CH),
-                q_ref,
-                k_ref,
-                v_ref,
-                beta_ref,
-                decay_ref,
-                slot,
+                unit, heads, at, q_ref, k_ref, v_ref, beta_ref, decay_ref, slot, first
             )
     terms = chunk_terms(chains)
     for slot in range(slots):
@@ -264,23 +273,15 @@
 
 def suffix_terms(first, unit, q, k, v, beta, decay, after=()):
     slots, tokens = q.shape[0], q.shape[1]
-    at = first // unit
     return pl.pallas_call(
         functools.partial(suffix_kernel, first, unit),
-        grid=(1,),
-        in_specs=[
-            pl.BlockSpec((slots, tokens, unit * DK), lambda i: (0, 0, at)),
-            pl.BlockSpec((slots, tokens, unit * DK), lambda i: (0, 0, at)),
-            pl.BlockSpec((slots, tokens, unit * W2), lambda i: (0, 0, at)),
-            pl.BlockSpec(beta.shape, lambda i: (0, 0, 0)),
-            pl.BlockSpec(decay.shape, lambda i: (0, 0, 0)),
-        ]
-        + [ANY] * len(after),
-        out_specs=[pl.BlockSpec((slots, tokens, unit * W2), lambda i: (0, 0, 0))] * 2,
-        out_shape=[jax.ShapeDtypeStruct((slots, tokens, unit * W2), jnp.bfloat16)] * 2,
-        compiler_params=pltpu.CompilerParams(vmem_limit_bytes=VMEM),
+        in_specs=[WHOLE] * 5 + [ANY] * len(after),
+        out_specs=[WHOLE] * 2,
+        out_shape=[pltpu.VMEM((slots, tokens, unit * W2), jnp.bfloat16)] * 2,
+        compiler_params=pltpu.CompilerParams(vmem_limit_bytes=SCOPED),
+        cost_estimate=SHORT,
         name="suffix_terms",
-    )(q, k, v, beta, decay, *after)
+    )(near(q), near(k), near(v), near(beta), near(decay), *after)
 
 
 def step_kernel(kinds, half, *refs):
@@ -315,16 +316,16 @@
     kinds = tuple(job[0] for job in jobs)
     args, shapes = [], []
     for kind, *ins in jobs:
-        args += ins
-        shape = jax.ShapeDtypeStruct(ins[0].shape[1:], jnp.float32)
+        args += [near(value) for value in ins]
+        shape = pltpu.VMEM(ins[0].shape[1:], jnp.float32)
         shapes += [shape] * (2 if kind == "twice" else 1)
-    whole = pl.BlockSpec(memory_space=pltpu.VMEM)
     outs = pl.pallas_call(
         functools.partial(step_kernel, kinds, half),
-        in_specs=[whole] * len(args) + [ANY] * len(after),
-        out_specs=[whole] * len(shapes),
+        in_specs=[WHOLE] * len(args) + [ANY] * len(after),
+        out_specs=[WHOLE] * len(shapes),
         out_shape=shapes,
-        compiler_params=pltpu.CompilerParams(vmem_limit_bytes=VMEM),
+        compiler_params=pltpu.CompilerParams(vmem_limit_bytes=SCOPED),
+        cost_estimate=SHORT,
         name="state_steps",
     )(*args, *after)
     outs = list(outs)
@@ -337,155 +338,140 @@
     return results
 
 
-def settle_kernel(half, to_ref, right_ref, mid_ref, *refs):
+def settle_kernel(half, sizes, *refs):
     here = lax.axis_index("seq")
     out_ref = refs[-1]
-    lefts = refs[:half]
-    for d in range(half):
-
-        @pl.when(here == d)
-        def _(d=d):
-            out_ref[...] = lefts[d][...]
-
-    @pl.when(here == half)
-    def _():
-        out_ref[...] = mid_ref[...]
-
-    @pl.when(here > half)
-    def _():
-        for p in range(out_ref.shape[0]):
-            out_ref[p] = apply_pair(to_ref[0, p], right_ref[p], to_ref[1, p])
-
-
-def settle(to, right, mid, lefts, after=()):
-    half = len(lefts)
-    whole = pl.BlockSpec(memory_space=pltpu.VMEM)
+    at = 0
+    for run, size in enumerate(sizes):
+        to_ref, right_ref, *finals = refs[run * (half + 3) : (run + 1) * (half + 3)]
+        for d in range(half + 1):
+
+            @pl.when(here == d)
+            def _(at=at, size=size, source=finals[d]):
+                out_ref[at : at + size] = source[...]
+
+        @pl.when(here > half)
+        def _(at=at, size=size, to_ref=to_ref, right_ref=right_ref):
+            for p in range(size):
+                out_ref[at + p] = apply_pair(to_ref[0, p], right_ref[p], to_ref[1, p])
+
+        at += size
+
+
+def settle(runs, half, after=()):
+    sizes = [to.shape[1] for to, right, lefts, mid in runs]
+    args = [x for to, right, lefts, mid in runs for x in (to, right, *lefts, mid)]
     return pl.pallas_call(
-        functools.partial(settle_kernel, half),
-        in_specs=[whole] * (3 + half) + [ANY] * len(after),
-        out_specs=whole,
-        out_shape=jax.ShapeDtypeStruct(mid.shape, jnp.float32),
-        compiler_params=pltpu.CompilerParams(vmem_limit_bytes=VMEM),
+        functools.partial(settle_kernel, half, sizes),
+        in_specs=[WHOLE] * len(args) + [ANY] * len(after),
+        out_specs=WHOLE,
+        out_shape=pltpu.VMEM((sum(sizes), DK, W2), jnp.float32),
+        compiler_params=pltpu.CompilerParams(vmem_limit_bytes=SCOPED),
+        cost_estimate=SHORT,
         name="settle",
-    )(to, right, mid, *lefts, *after)
+    )(*[near(value) for value in args], *after)
 
 
 def finish(a, state, b, gain2):
     raw = mm(a, diag2(low16(state))) + b.astype(jnp.float32)
-    sq = raw * raw
-    parts = []
-    for h in range(2):
-        lanes = slice(h * DV, (h + 1) * DV)
-        inv = lax.rsqrt(jnp.mean(sq[:, lanes], axis=-1, keepdims=True) + EPS_NORM)
-        parts.append(raw[:, lanes] * inv)
-    return jnp.concatenate(parts, axis=1) * gain2
-
-
-def suffix_out_kernel(unit, slots, n_prompt, *refs):
-    sb_ref, bl_ref, bp_ref, own_ref, other_ref, a_ref, b_ref, gain_ref = refs[:8]
+    share = diag2(jnp.full((DV, W2), 1.0 / DV, jnp.bfloat16))
+    return raw * lax.rsqrt(mm(low16(raw * raw), share) + EPS_NORM) * gain2
+
+
+def suffix_out_kernel(sizes, slots, n_prompt, *refs):
+    sb_ref, bl_ref, bp_ref, own_ref, other_ref, gain_ref = refs[:6]
     out_ref = refs[-1]
     me = lax.axis_index("prompt")
     rank = lax.axis_index("seq") * n_prompt + me
-    branch = sb_ref[rank * slots + pl.program_id(0)]
+    slot = pl.program_id(0)
+    branch = sb_ref[rank * slots + slot]
     length = bl_ref[branch]
     mine = bp_ref[branch] == me
     gain = gain_ref[...]
     gain2 = jnp.concatenate([gain, gain], axis=1)
-    tokens = a_ref.shape[1]
+    tokens = out_ref.shape[1]
     live = lax.broadcasted_iota(jnp.int32, (tokens, W2), 0) < length
-    for p in range(unit):
-        lanes = slice(p * W2, (p + 1) * W2)
+    for p, (run, at) in enumerate(places_of(sizes)):
+        source = slice(at * W2, (at + 1) * W2)
+        a_ref, b_ref = refs[6 + 2 * run : 8 + 2 * run]
         state = jnp.where(mine, own_ref[p], other_ref[p])
-        out = finish(a_ref[0, :, lanes], state, b_ref[0, :, lanes], gain2)
-        out_ref[0, :, lanes] = low16(jnp.where(live, out, 0.0))
-
-
-def suffix_outputs(first, tables, own, other, a, b, gain, so_far, width, after=()):
-    slots, tokens, lanes = a.shape
-    unit = lanes // W2
-    at = first // unit
-    smem = pl.BlockSpec(memory_space=pltpu.SMEM)
-    in_specs = [
-        smem,
-        smem,
-        smem,
-        pl.BlockSpec((unit, DK, W2), lambda i: (0, 0, 0)),
-        pl.BlockSpec((unit, DK, W2), lambda i: (0, 0, 0)),
-        pl.BlockSpec((1, tokens, lanes), lambda i: (i, 0, 0)),
-        pl.BlockSpec((1, tokens, lanes), lambda i: (i, 0, 0)),
-        pl.BlockSpec((1, DV), lambda i: (0, 0)),
-    ]
-    args = list(tables) + [own, other, a, b, gain]
+        out = finish(a_ref[slot, :, source], state, b_ref[slot, :, source], gain2)
+        out_ref[0, :, p * W2 : (p + 1) * W2] = low16(jnp.where(live, out, 0.0))
+
+
+def suffix_outputs(first, tables, own, other, terms, gain, so_far, width, after=()):
+    slots, tokens, _ = terms[0][0].shape
+    sizes = [a.shape[2] // W2 for a, b in terms]
+    pairs = sum(sizes)
+    at = first // pairs
+    args = [own, other, gain] + [x for pair in terms for x in pair]
+    in_specs = [pl.BlockSpec(memory_space=pltpu.SMEM)] * 3 + [WHOLE] * len(args)
+    args = list(tables) + [near(value) for value in args]
     aliases = {}
     if so_far is not None:
+        aliases = {len(args): 0}
         in_specs.append(ANY)
-        args.append(so_far)
-        aliases = {8: 0}
+        args.append(away(so_far))
     return pl.pallas_call(
-        functools.partial(suffix_out_kernel, unit, slots, lax.axis_size("prompt")),
+        functools.partial(suffix_out_kernel, sizes, slots, lax.axis_size("prompt")),
         grid=(slots,),
         in_specs=in_specs + [ANY] * len(after),
-        out_specs=pl.BlockSpec((1, tokens, lanes), lambda i: (i, 0, at)),
-        out_shape=jax.ShapeDtypeStruct((slots, tokens, width), jnp.bfloat16),
+        out_specs=pl.BlockSpec((1, tokens, pairs * W2), lambda i: (i, 0, at)),
+        out_shape=pltpu.HBM((slots, tokens, width), jnp.bfloat16),
         input_output_aliases=aliases,
-        compiler_params=pltpu.CompilerParams(vmem_limit_bytes=VMEM),
+        compiler_params=pltpu.CompilerParams(vmem_limit_bytes=SCOPED),
+        cost_estimate=SHORT,
         name="suffix_out",
     )(*args, *after)
 
 
-def prompt_out_kernel(half, skip, far_ref, mid_ref, right_ref, a_ref, b_ref, gain_ref, *refs):
+def prompt_out_kernel(half, calls, sizes, *refs):
     here = lax.axis_index("seq")
-    out_ref = refs[-1]
+    came = refs[: 3 * len(sizes)]
+    terms = refs[len(came) : len(came) + 2 * len(calls)]
+    gain_ref = refs[len(came) + len(terms)]
+    out_ref, state_ref = refs[-2:]
+    at = 0
+    for run, size in enumerate(sizes):
+        far_ref, mid_ref, right_ref = came[3 * run : 3 * run + 3]
+
+        @pl.when(here < half)
+        def _(at=at, size=size, far_ref=far_ref):
+            state_ref[at : at + size] = far_ref[1]
+
+        @pl.when(here == half)
+        def _(at=at, size=size, mid_ref=mid_ref):
+            state_ref[at : at + size] = mid_ref[...]
+
+        @pl.when(here > half)
+        def _(at=at, size=size, right_ref=right_ref):
+            state_ref[at : at + size] = right_ref[...]
+
+        at += size
     gain = gain_ref[...]
     gain2 = jnp.concatenate([gain, gain], axis=1)
-
-    def write(state_of):
-        for p in range(mid_ref.shape[0]):
-            lanes = slice(p * W2, (p + 1) * W2)
-            near = slice((skip + p) * W2, (skip + p + 1) * W2)
-            out_ref[0, :, lanes] = low16(finish(a_ref[:, near], state_of(p), b_ref[:, near], gain2))
-
-    @pl.when(here < half)
-    def _():
-        write(lambda p: far_ref[1, p])
-
-    @pl.when(here == half)
-    def _():
-        write(lambda p: mid_ref[p])
-
-    @pl.when(here > half)
-    def _():
-        write(lambda p: right_ref[p])
-
-
-def prompt_outputs(first, skip, half, far, mid, right, a, b, gain, so_far, width, after=()):
-    pairs = mid.shape[0]
-    at = first // pairs
-    zero3 = lambda i: (0, 0, 0)
-    in_specs = [
-        pl.BlockSpec(far.shape, lambda i: (0, 0, 0, 0)),
-        pl.BlockSpec(mid.shape, zero3),
-        pl.BlockSpec(right.shape, zero3),
-        pl.BlockSpec(a.shape, lambda i: (0, 0)),
-        pl.BlockSpec(b.shape, lambda i: (0, 0)),
-        pl.BlockSpec((1, DV), lambda i: (0, 0)),
-    ]
-    args = [far, mid, right, a, b, gain]
-    aliases = {}
-    if so_far is not None:
-        in_specs.append(ANY)
-        args.append(so_far)
-        aliases = {6: 0}
+    for p, (call, at) in enumerate(places_of(calls)):
+        source = slice(at * W2, (at + 1) * W2)
+        a, b = terms[2 * call][:, source], terms[2 * call + 1][:, source]
+        out_ref[0, :, p * W2 : (p + 1) * W2] = low16(finish(a, state_ref[p], b, gain2))
+
+
+def prompt_outputs(half, came, terms, gain, width, after=()):
+    pairs = width // W2
+    calls = [a.shape[1] // W2 for a, b in terms]
+    sizes = [mid.shape[0] for far, mid, right in came]
+    args = [x for run in came for x in run] + [x for pair in terms for x in pair] + [gain]
     return pl.pallas_call(
-        functools.partial(prompt_out_kernel, half, skip),
+        functools.partial(prompt_out_kernel, half, calls, sizes),
         grid=(1,),
-        in_specs=in_specs + [ANY] * len(after),
-        out_specs=pl.BlockSpec((1, CH, pairs * W2), lambda i: (0, 0, at)),
-        out_shape=jax.ShapeDtypeStruct((1, CH, width), jnp.bfloat16),
-        input_output_aliases=aliases,
-        compiler_params=pltpu.CompilerParams(vmem_limit_bytes=VMEM),
+        in_specs=[WHOLE] * len(args) + [ANY] * len(after),
+        out_specs=pl.BlockSpec((1, CH, width), lambda i: (0, 0, 0)),
+        out_shape=pltpu.HBM((1, CH, width), jnp.bfloat16),
+        scratch_shapes=[pltpu.VMEM((pairs, DK, W2), jnp.float32)],
+        compiler_params=pltpu.CompilerParams(vmem_limit_bytes=SCOPED),
+        cost_estimate=SHORT,
         name="prompt_out",
-    )(*args, *after)
+    )(*[near(value) for value in args], *after)
 
 
 def pair_product(left, right):
@@ -531,7 +517,10 @@
     def spread(self, result):
         state, self.final_mid = result
         half, count = self.half, self.count
-        self.lefts = [lax.ppermute(self.final_mid, "seq", [(half, d)]) for d in range(half)]
+        self.lefts, passed = [], self.final_mid
+        for d in range(half - 1, -1, -1):
+            passed = lax.ppermute(passed, "seq", [(d + 1, d)])
+            self.lefts.insert(0, passed)
         right = None
         for j in range(half - 1):
             arrived = lax.ppermute(state, "seq", [(half + j, half + j + 1)])
@@ -540,23 +529,24 @@
                 state = pair_product(self.to[0], arrived) + self.to[1]
         self.right = right
 
-    def settle(self, after=()):
-        self.final = settle(self.to, self.right, self.final_mid, self.lefts, after)
-        if self.half > 2:
-            inner = (self.here > self.half) & (self.here < self.count - 1)
-            done = pair_product(self.far[0], self.final) + self.far[1]
-            self.final = jnp.where(inner, done, self.final)
-        prompts = lax.axis_size("prompt")
-        self.other = lax.ppermute(
-            self.final, "prompt", [(i, (i + 1) % prompts) for i in range(prompts)]
-        )
+
+def settle_runs(relays, after):
+    half, count, here = relays[0].half, relays[0].count, relays[0].here
+    final = settle([(r.to, r.right, r.lefts, r.final_mid) for r in relays], half, after)
+    if half > 2:
+        inner = (here > half) & (here < count - 1)
+        far = jnp.concatenate([r.far for r in relays], axis=1)
+        final = jnp.where(inner, pair_product(far[0], final) + far[1], final)
+    prompts = lax.axis_size("prompt")
+    other = lax.ppermute(final, "prompt", [(i, (i + 1) % prompts) for i in range(prompts)])
+    return final, other
 
 
 def plan_of(pairs):
     if pairs % 4:
-        return [[1]] * pairs
+        return [[1]] * pairs, [1] * pairs
     unit = pairs // 4
-    return [[unit], [unit, unit, unit]]
+    return [[unit], [unit, unit, unit]], [3, 1]
 
 
 def local(
@@ -582,72 +572,60 @@
     suffix_in = (suffix_queries, suffix_keys, suffix_values, suffix_beta, suffix_decay)
     half = lax.axis_size("seq") // 2
 
-    runs = []
-    first = 0
-    last = ()
-    for sizes in plan_of(width // W2):
+    calls, ends = plan_of(width // W2)
+    relays, firsts, terms = [], [], []
+    first, last = 0, ()
+    for sizes in calls:
         tos, a, b = prompt_terms(first, sizes, *prompt_in, after=last)
-        last = (a,)
-        skip = 0
+        last = (near(a),)
+        terms.append((a, b))
         for to, size in zip(tos, sizes):
             relay = Relay(to)
             relay.open()
-            runs.append((first + skip, skip, size, a, b, relay))
-            skip += size
-        first += skip
-    total = len(runs)
-    made = {}
-
-    def make(index, after):
+            relays.append(relay)
+            firsts.append(first)
+            first += size
+    total = len(relays)
+    made = []
+
+    def make(after):
+        if len(made) == total:
+            return after
+        index = len(made)
+        size = relays[index].to.shape[1]
+        made.append(suffix_terms(firsts[index], size, *suffix_in, after=after))
+        return (near(made[index][0]),)
+
+    def landed(index):
+        return tuple(
+            near(relays[index - 2 - j].lefts[half - 1 - j])
+            for j in range(half)
+            if 0 <= index - 2 - j < total
+        )
+
+    last = make(make(last))
+    for index in range(total + 2):
         if index < total:
-            made[index] = suffix_terms(runs[index][0], runs[index][2], *suffix_in, after=after)
-            return (made[index][0],)
-        return after
-
-    prompt_out, suffix_out = None, None
-
-    def write_prompt(index, after):
-        nonlocal prompt_out
-        start, skip, size, a, b, relay = runs[index]
-        prompt_out = prompt_outputs(
-            start, skip, half, relay.far, relay.mid, relay.right, a, b, gain, prompt_out, width, after
+            (prefix,) = run_steps([relays[index].prefix_job()], half, last)
+            relays[index].cross(prefix)
+            last = (near(prefix),)
+        if 0 < index <= total:
+            (result,) = run_steps([relays[index - 1].final_job()], half, last)
+            relays[index - 1].spread(result)
+            last = (near(result[0]),)
+        last = make(last) + landed(index)
+    came = [(relay.far, relay.mid, relay.right) for relay in relays]
+    prompt_out = prompt_outputs(half, came, terms, gain, width, last)
+    last = (away(prompt_out),)
+    suffix_out = None
+    index = 0
+    for runs in ends:
+        own, other = settle_runs(relays[index : index + runs], last)
+        suffix_out = suffix_outputs(
+            firsts[index], tables, own, other, made[index : index + runs], gain, suffix_out, width
         )
-        return (prompt_out,)
-
-    def write_suffix(index, after):
-        nonlocal suffix_out
-        start, skip, size, a, b, relay = runs[index]
-        suffix_out = suffix_outputs(
-            start, tables, relay.final, relay.other, *made[index], gain, suffix_out, width, after
-        )
-        return (suffix_out,)
-
-    last = make(0, last)
-    last = make(1, last)
-    for index in range(total + 1):
-        jobs = []
-        if index < total:
-            jobs.append(runs[index][5].prefix_job())
-        if index:
-            jobs.append(runs[index - 1][5].final_job())
-        results = run_steps(jobs, half, last)
-        if index < total:
-            prefix = results.pop(0)
-            runs[index][5].cross(prefix)
-            last = (prefix,)
-        if index:
-            last = (results[0][0],)
-            runs[index - 1][5].spread(results.pop(0))
-        last = make(index + 2, last)
-        if index >= 2:
-            relay = runs[index - 2][5]
-            relay.settle(last)
-            last = write_prompt(index - 2, (relay.final,))
-            last = write_suffix(index - 2, last)
-    relay = runs[total - 1][5]
-    relay.settle(last)
-    last = write_prompt(total - 1, (relay.final,))
-    write_suffix(total - 1, last)
+        last = (away(suffix_out),)
+        index += runs
     return (prompt_out, suffix_out)
 
 

time: 138 us -> 93.3 us (0.68)
  the two profiles are of different devices: /device:TPU:11 before, /device:TPU:0 now
where the time goes in v2:
time: 93.3 us; the launch traced here: 92.9 us
  Pallas kernels  34.7 us (37%)
  waiting for transfers between devices  31.7 us (34%)
  starting transfers between devices  25.2 us (27%)
  between operations  1.12 us (1%)
    ppermute x8, waiting for transfers between devices, spread(): passed = lax.ppermute(passed, 'seq', [(d + 1, d)])  20 us
    pallas_call x4, Pallas kernels, suffix_terms(): pl.pallas_call(functools.partial(suffix_kernel, first, unit), in_specs=[W...  18.1 us
    ppermute x4, starting transfers between devices, open(): lax.ppermute(sending, 'seq', [(j, j + 1), (count - 1 - j, count - 2 - j)])  11.8 us
    ppermute x4, waiting for transfers between devices, open(): lax.ppermute(sending, 'seq', [(j, j + 1), (count - 1 - j, count - 2 - j)])  9.26 us
    pallas_call x2, Pallas kernels, prompt_terms(): pl.pallas_call(functools.partial(prompt_kernel, first, sizes, wide, len(q...  8.34 us
    ppermute x8, starting transfers between devices, spread(): passed = lax.ppermute(passed, 'seq', [(d + 1, d)])  7.88 us
    pallas_call x2, Pallas kernels, suffix_outputs(): pl.pallas_call(functools.partial(suffix_out_kernel, sizes, slots, lax.axi...  5.23 us
    ppermute x4, starting transfers between devices, spread(): arrived = lax.ppermute(state, 'seq', [(half + j, half + j + 1)])  2.71 us
  transfers between devices with their start and end apart: 22, of which 7 were waited for; matrix products, arithmetic and copies ran while one was open for 0% of the time, Pallas kernels for 30%

profile of v2, /device:TPU:0, one launch (start us, length us, event | category | flops | bytes accessed | tf_op | source)
XLA Modules:
  0.0 92.9 jit_solution(10570549210159225817)
XLA Ops:
  0.6 0.0 copy-start.4
  0.6 0.0 copy-start.3
  0.7 0.0 copy-start
  0.7 0.0 copy-start.2
  0.7 3.5 %prompt_terms.2 = (f32[2,2,128,256]{3,2,1,0:T(8,128)S(1)}, bf16[128,512]{1,0:T(8,128)(2,1)S(1)}, bf16[128,512]{1,0:T(8,128)(2,1)S(1)}) custom-call(bf16[1,128,1024]{2,1,0:T(8,128)(2,1)} %refs_2_.5, bf16[1,128,1024]{2,1,0:T(8,128)(2,1)} %refs_5_.1, bf16[1,128,2048]{2,1,0:T(8,128)(2,1)} %refs_8_.1, f32[1,16,128]{2,1,0:T(8,128)} %refs_9_.1, f32[1,16,128]{2,1,0:T(8,128)} %refs_10_.1), custom_call_target="tpu_custom_call" | custom-call | flops 1 | bytes 1 | tf_op jit(solution)/shard_map/prompt_terms/pallas_call | solution.py:221
  4.2 5.0 %collective-permute-start = (f32[2,2,128,256]{3,2,1,0:T(8,128)S(1)}, f32[2,2,128,256]{3,2,1,0:T(8,128)S(1)}, u32[]{:S(2)}, u32[]{:S(2)}) collective-permute-start(f32[2,2,128,256]{3,2,1,0:T(8,128)S(1)} %get-tuple-element.26.refs_0_), channel_id=1, source_target_pairs={{0,4},{12,8},{1,5},{13,9},{2,6},{14,10},{3,7},{15,11},{16,20},{28,... | collective-permute-start | bytes 1572872 | tf_op jit(solution)/shard_map/ppermute | solution.py:495
  9.2 4.8 %prompt_terms.3 = (f32[2,2,128,256]{3,2,1,0:T(8,128)S(1)}, f32[2,2,128,256]{3,2,1,0:T(8,128)S(1)}, f32[2,2,128,256]{3,2,1,0:T(8,128)S(1)}, bf16[128,1536]{1,0:T(8,128)(2,1)S(1)}, bf16[128,1536]{1,0:T(8,128)(2,1)S(1)}) custom-call(bf16[1,128,1024]{2,1,0:T(8,128)(2,1)} %refs_2_.5, bf16[1,128,1024]{2,1,0:T(8,128)(2,1)} %refs_2_.5, ...), custom_call_target="tpu_custom_call" | custom-call | flops 1 | bytes 1 | tf_op jit(solution)/shard_map/prompt_terms/pallas_call | solution.py:221
  14.0 1.3 %collective-permute-start.2 = (f32[2,2,128,256]{3,2,1,0:T(8,128)S(1)}, f32[2,2,128,256]{3,2,1,0:T(8,128)S(1)}, u32[]{:S(2)}, u32[]{:S(2)}) collective-permute-start(f32[2,2,128,256]{3,2,1,0:T(8,128)S(1)} %get-tuple-element.31.refs_0_.refs_5_), channel_id=1, source_target_pairs={{0,4},{12,8},{1,5},{13,9},{2,6},{14,10},{3,7},{15,11},{16,20},{28,... | collective-permute-start | bytes 1572872 | tf_op jit(solution)/shard_map/ppermute | solution.py:495
  15.3 1.5 %collective-permute-start.5 = (f32[2,2,128,256]{3,2,1,0:T(8,128)S(1)}, f32[2,2,128,256]{3,2,1,0:T(8,128)S(1)}, u32[]{:S(2)}, u32[]{:S(2)}) collective-permute-start(f32[2,2,128,256]{3,2,1,0:T(8,128)S(1)} %get-tuple-element.34.refs_0_.refs_10_), channel_id=1, source_target_pairs={{0,4},{12,8},{1,5},{13,9},{2,6},{14,10},{3,7},{15,11},{16,20},{28,... | collective-permute-start | bytes 1572872 | tf_op jit(solution)/shard_map/ppermute | solution.py:495
  16.9 4.5 %suffix_terms.4 = (bf16[2,256,512]{2,1,0:T(8,128)(2,1)S(1)}, bf16[2,256,512]{2,1,0:T(8,128)(2,1)S(1)}) custom-call(bf16[2,256,1024]{2,1,0:T(8,128)(2,1)S(1)} %copy-done.1, bf16[2,256,1024]{2,1,0:T(8,128)(2,1)S(1)} %copy-done.2, bf16[2,256,2048]{2,1,0:T(8,128)(2,1)S(1)} %copy-done, f32[2,16,256]{2,1,0:T(8,128)S(1)} %copy-done.3, f32[2,16,256]{2,1,0:T(8,128)S(1)} %copy-done.4, ...), custom_call_target="tpu_custom_call" | custom-call | flops 1 | bytes 1 | tf_op jit(solution)/shard_map/suffix_terms/pallas_call | solution.py:276
  21.4 4.5 %suffix_terms.5 = (bf16[2,256,512]{2,1,0:T(8,128)(2,1)S(1)}, bf16[2,256,512]{2,1,0:T(8,128)(2,1)S(1)}) custom-call(bf16[2,256,1024]{2,1,0:T(8,128)(2,1)S(1)} %copy-done.1, bf16[2,256,1024]{2,1,0:T(8,128)(2,1)S(1)} %copy-done.2, bf16[2,256,2048]{2,1,0:T(8,128)(2,1)S(1)} %copy-done, f32[2,16,256]{2,1,0:T(8,128)S(1)} %copy-done.3, f32[2,16,256]{2,1,0:T(8,128)S(1)} %copy-done.4, ...), custom_call_target="tpu_custom_call" | custom-call | flops 1 | bytes 1 | tf_op jit(solution)/shard_map/suffix_terms/pallas_call | solution.py:276
  26.0 0.0 collective-permute-done.refs_1_.refs_0_
  26.0 0.3 state_steps.8.refs_0_
  26.3 0.7 collective-permute-start.1
  27.0 4.0 %collective-permute-start.8 = (f32[2,2,128,256]{3,2,1,0:T(8,128)S(1)}, f32[2,2,128,256]{3,2,1,0:T(8,128)S(1)}, u32[]{:S(2)}, u32[]{:S(2)}) collective-permute-start(f32[2,2,128,256]{3,2,1,0:T(8,128)S(1)} %get-tuple-element.37.refs_0_), channel_id=1, source_target_pairs={{0,4},{12,8},{1,5},{13,9},{2,6},{14,10},{3,7},{15,11},{16,20},{28,... | collective-permute-start | bytes 1572872 | tf_op jit(solution)/shard_map/ppermute | solution.py:495
  31.0 4.5 %suffix_terms.6 = (bf16[2,256,512]{2,1,0:T(8,128)(2,1)S(1)}, bf16[2,256,512]{2,1,0:T(8,128)(2,1)S(1)}) custom-call(bf16[2,256,1024]{2,1,0:T(8,128)(2,1)S(1)} %copy-done.1, bf16[2,256,1024]{2,1,0:T(8,128)(2,1)S(1)} %copy-done.2, bf16[2,256,2048]{2,1,0:T(8,128)(2,1)S(1)} %copy-done, f32[2,16,256]{2,1,0:T(8,128)S(1)} %copy-done.3, f32[2,16,256]{2,1,0:T(8,128)S(1)} %copy-done.4, ...), custom_call_target="tpu_custom_call" | custom-call | flops 1 | bytes 1 | tf_op jit(solution)/shard_map/suffix_terms/pallas_call | solution.py:276
  35.5 0.0 collective-permute-done.2.refs_1_.refs_3_
  35.5 0.3 state_steps.9.refs_3_
  35.8 0.7 collective-permute-start.4
  36.5 0.0 collective-permute-done.1.refs_2_.refs_1_
  36.5 0.7 collective-permute-start.9
  37.2 4.5 %suffix_terms.7 = (bf16[2,256,512]{2,1,0:T(8,128)(2,1)S(1)}, bf16[2,256,512]{2,1,0:T(8,128)(2,1)S(1)}) custom-call(bf16[2,256,1024]{2,1,0:T(8,128)(2,1)S(1)} %copy-done.1, bf16[2,256,1024]{2,1,0:T(8,128)(2,1)S(1)} %copy-done.2, bf16[2,256,2048]{2,1,0:T(8,128)(2,1)S(1)} %copy-done, f32[2,16,256]{2,1,0:T(8,128)S(1)} %copy-done.3, f32[2,16,256]{2,1,0:T(8,128)S(1)} %copy-done.4, ...), custom_call_target="tpu_custom_call" | custom-call | flops 1 | bytes 1 | tf_op jit(solution)/shard_map/suffix_terms/pallas_call | solution.py:276
  41.7 2.2 %collective-permute-done.5.refs_1_.refs_6_ = f32[2,2,128,256]{3,2,1,0:T(8,128)S(1)} collective-permute-done((f32[2,2,128,256]{3,2,1,0:T(8,128)S(1)}, f32[2,2,128,256]{3,2,1,0:T(8,128)S(1)}, u32[]{:S(2)}, u32[]{:S(2)}) %collective-permute-start.5) | collective-permute-done | bytes 524320 | tf_op jit(solution)/shard_map/ppermute | solution.py:495
  43.9 0.3 state_steps.11.refs_3_
  44.2 0.7 collective-permute-start.7
  44.9 0.0 collective-permute-done.4.refs_2_.refs_4_
  44.9 0.7 collective-permute-start.12
  45.6 0.0 collective-permute-done.9.refs_3_
  45.6 1.3 %collective-permute-start.13 = (f32[2,128,256]{2,1,0:T(8,128)S(1)}, f32[2,128,256]{2,1,0:T(8,128)S(1)}, u32[]{:S(2)}, u32[]{:S(2)}) collective-permute-start(f32[2,128,256]{2,1,0:T(8,128)S(1)} %collective-permute-done.9.refs_3_), channel_id=1, source_target_pairs={{4,0},{5,1},{6,2},{7,3},{20,16},{21,17},{22,18},{23,19}} | collective-permute-start | bytes 786440 | tf_op jit(solution)/shard_map/ppermute | solution.py:522
  46.9 7.1 %collective-permute-done.8.refs_1_.refs_9_ = f32[2,2,128,256]{3,2,1,0:T(8,128)S(1)} collective-permute-done((f32[2,2,128,256]{3,2,1,0:T(8,128)S(1)}, f32[2,2,128,256]{3,2,1,0:T(8,128)S(1)}, u32[]{:S(2)}, u32[]{:S(2)}) %collective-permute-start.8) | collective-permute-done | bytes 524320 | tf_op jit(solution)/shard_map/ppermute | solution.py:495
  54.0 0.3 state_steps.13.refs_3_
  54.3 0.0 copy-start.5
  54.3 0.7 collective-permute-start.11
  55.0 0.7 collective-permute-start.3
  55.7 0.0 collective-permute-done.7.refs_2_.refs_7_
  55.7 0.7 collective-permute-start.15
  56.4 0.0 collective-permute-done.12.refs_4_.refs_8_
  56.4 0.7 collective-permute-start.6
  57.1 0.0 collective-permute-done.13.refs_5_.refs_2_
  57.1 0.7 collective-permute-start.10
  57.8 0.0 collective-permute-done.11.refs_2_.refs_10_
  57.8 1.3 %collective-permute-start.16 = (f32[2,128,256]{2,1,0:T(8,128)S(1)}, f32[2,128,256]{2,1,0:T(8,128)S(1)}, u32[]{:S(2)}, u32[]{:S(2)}) collective-permute-start(f32[2,128,256]{2,1,0:T(8,128)S(1)} %collective-permute-done.12.refs_4_.refs_8_), channel_id=1, source_target_pairs={{4,0},{5,1},{6,2},{7,3},{20,16},{21,17},{22,18},{23,19}} | collective-permute-start | bytes 786440 | tf_op jit(solution)/shard_map/ppermute | solution.py:522
  59.1 0.3 state_steps.15
  59.4 0.0 collective-permute-done.3.refs_2_.refs_1_
  59.4 0.7 collective-permute-start.14
  60.1 0.0 collective-permute-done.15.refs_18_.refs_13_
  60.1 1.3 %collective-permute-start.18 = (f32[2,128,256]{2,1,0:T(8,128)S(1)}, f32[2,128,256]{2,1,0:T(8,128)S(1)}, u32[]{:S(2)}, u32[]{:S(2)}) collective-permute-start(f32[2,128,256]{2,1,0:T(8,128)S(1)} %collective-permute-done.15.refs_18_.refs_13_), channel_id=1, source_target_pairs={{4,0},{5,1},{6,2},{7,3},{20,16},{21,17},{22,18},{23,19}} | collective-permute-start | bytes 786440 | tf_op jit(solution)/shard_map/ppermute | solution.py:522
  61.4 0.0 collective-permute-done.6.refs_5_.refs_6_
  61.4 0.7 collective-permute-start.17
  62.1 9.5 %collective-permute-done.16.refs_19_.refs_7_ = f32[2,128,256]{2,1,0:T(8,128)S(1)} collective-permute-done((f32[2,128,256]{2,1,0:T(8,128)S(1)}, f32[2,128,256]{2,1,0:T(8,128)S(1)}, u32[]{:S(2)}, u32[]{:S(2)}) %collective-permute-start.16) | collective-permute-done | bytes 262176 | tf_op jit(solution)/shard_map/ppermute | solution.py:522
  71.5 0.0 collective-permute-done.10.refs_8_.refs_11_
  71.5 4.6 %collective-permute-done.18.refs_21_.refs_12_ = f32[2,128,256]{2,1,0:T(8,128)S(1)} collective-permute-done((f32[2,128,256]{2,1,0:T(8,128)S(1)}, f32[2,128,256]{2,1,0:T(8,128)S(1)}, u32[]{:S(2)}, u32[]{:S(2)}) %collective-permute-start.18) | collective-permute-done | bytes 262176 | tf_op jit(solution)/shard_map/ppermute | solution.py:522
  76.2 0.0 collective-permute-done.14.refs_11_.refs_1_
  76.2 0.0 collective-permute-done.17.refs_20_.refs_3_
  76.2 1.5 %prompt_out.1.refs_15_ = bf16[1,128,2048]{2,1,0:T(8,128)(2,1)} custom-call(f32[2,2,128,256]{3,2,1,0:T(8,128)S(1)} %collective-permute-done.refs_1_.refs_0_, f32[2,128,256]{2,1,0:T(8,128)S(1)} %collective-permute-done.1.refs_2_.refs_1_, f32[2,128,256]{2,1,0:T(8,128)S(1)} %collective-permute-done.3.refs_2_.refs_1_, ...), custom_call_target="tpu_custom_call" | custom-call | flops 1 | bytes 1 | tf_op jit(solution)/shard_map/prompt_out/pallas_call | solution.py:464
  77.7 0.1 settle.2.refs_3_
  77.8 0.1 collective-permute-start.20
  77.8 1.3 %collective-permute-start.19 = (f32[2,128,256]{2,1,0:T(8,128)S(1)}, f32[2,128,256]{2,1,0:T(8,128)S(1)}, u32[]{:S(2)}, u32[]{:S(2)}) collective-permute-start(f32[2,128,256]{2,1,0:T(8,128)S(1)} %collective-permute-done.17.refs_20_.refs_3_), channel_id=1, source_target_pairs={{4,0},{5,1},{6,2},{7,3},{20,16},{21,17},{22,18},{23,19}} | collective-permute-start | bytes 786440 | tf_op jit(solution)/shard_map/ppermute | solution.py:522
  79.1 1.0 %collective-permute-done.20.refs_4_ = f32[6,128,256]{2,1,0:T(8,128)S(1)} collective-permute-done((f32[6,128,256]{2,1,0:T(8,128)S(1)}, f32[6,128,256]{2,1,0:T(8,128)S(1)}, u32[]{:S(2)}, u32[]{:S(2)}) %collective-permute-start.20) | collective-permute-done | bytes 786464 | tf_op jit(solution)/shard_map/ppermute | solution.py:541
  80.1 3.1 %suffix_out.2.refs_5_.refs_8_ = bf16[2,256,2048]{2,1,0:T(8,128)(2,1)} custom-call(s32[16]{0:T(128)S(1)} %copy-done.6, s32[16]{0:T(128)S(1)} %copy-done.7, s32[16]{0:T(128)S(1)} %copy-done.8, f32[6,128,256]{2,1,0:T(8,128)S(1)} %settle.2.refs_3_, f32[6,128,256]{2,1,0:T(8,128)S(1)} %collective-permute-done.20.refs_4_, f32[1,128]{1,0:T(1,128)S(1)} %bitcast.2, ...), custom_call_target="tpu_custom_call" | custom-call | flops 1 | bytes 1 | tf_op jit(solution)/shard_map/suffix_out/pallas_call | solution.py:415
  83.2 5.9 %collective-permute-done.19.refs_2_ = f32[2,128,256]{2,1,0:T(8,128)S(1)} collective-permute-done((f32[2,128,256]{2,1,0:T(8,128)S(1)}, f32[2,128,256]{2,1,0:T(8,128)S(1)}, u32[]{:S(2)}, u32[]{:S(2)}) %collective-permute-start.19) | collective-permute-done | bytes 262176 | tf_op jit(solution)/shard_map/ppermute | solution.py:522
  89.1 0.1 collective-permute-start.21
  89.2 1.5 %collective-permute-done.21.refs_4_ = f32[2,128,256]{2,1,0:T(8,128)S(1)} collective-permute-done((f32[2,128,256]{2,1,0:T(8,128)S(1)}, f32[2,128,256]{2,1,0:T(8,128)S(1)}, u32[]{:S(2)}, u32[]{:S(2)}) %collective-permute-start.21) | collective-permute-done | bytes 262176 | tf_op jit(solution)/shard_map/ppermute | solution.py:541
  90.7 2.2 %suffix_out.3 = bf16[2,256,2048]{2,1,0:T(8,128)(2,1)} custom-call(s32[16]{0:T(128)S(1)} %copy-done.6, s32[16]{0:T(128)S(1)} %copy-done.7, s32[16]{0:T(128)S(1)} %copy-done.8, f32[2,128,256]{2,1,0:T(8,128)S(1)} %settle.3.refs_3_, f32[2,128,256]{2,1,0:T(8,128)S(1)} %collective-permute-done.21.refs_4_, ...), custom_call_target="tpu_custom_call", output_to_operand_aliasing={{}: (8, {})} | custom-call | flops 1 | bytes 1 | tf_op jit(solution)/shard_map/suffix_out/pallas_call | solution.py:415
  (17 shorter events, 0.1 us)
Async XLA Ops:
  0.6 16.2 %copy-start.4 = (f32[2,16,256]{2,1,0:T(8,128)S(1)}, f32[2,16,256]{2,1,0:T(8,128)}, u32[]{:S(2)}) copy-start(f32[2,16,256]{2,1,0:T(8,128)} %decay_ref.7) | copy-start | bytes 98308
  0.6 16.2 %copy-start.3 = (f32[2,16,256]{2,1,0:T(8,128)S(1)}, f32[2,16,256]{2,1,0:T(8,128)}, u32[]{:S(2)}) copy-start(f32[2,16,256]{2,1,0:T(8,128)} %beta_ref.7) | copy-start | bytes 98308
  0.7 16.2 %copy-start = (bf16[2,256,2048]{2,1,0:T(8,128)(2,1)S(1)}, bf16[2,256,2048]{2,1,0:T(8,128)(2,1)}, u32[]{:S(2)}) copy-start(bf16[2,256,2048]{2,1,0:T(8,128)(2,1)} %v_ref.7) | copy-start | bytes 6291460
  0.7 16.2 %copy-start.2 = (bf16[2,256,1024]{2,1,0:T(8,128)(2,1)S(1)}, bf16[2,256,1024]{2,1,0:T(8,128)(2,1)}, u32[]{:S(2)}) copy-start(bf16[2,256,1024]{2,1,0:T(8,128)(2,1)} %k_ref.7) | copy-start | bytes 3145732
  0.7 16.2 %copy-start.1 = (bf16[2,256,1024]{2,1,0:T(8,128)(2,1)S(1)}, bf16[2,256,1024]{2,1,0:T(8,128)(2,1)}, u32[]{:S(2)}) copy-start(bf16[2,256,1024]{2,1,0:T(8,128)(2,1)} %q_ref.7) | copy-start | bytes 3145732
  4.2 21.8 %collective-permute-start = (f32[2,2,128,256]{3,2,1,0:T(8,128)S(1)}, f32[2,2,128,256]{3,2,1,0:T(8,128)S(1)}, u32[]{:S(2)}, u32[]{:S(2)}) collective-permute-start(f32[2,2,128,256]{3,2,1,0:T(8,128)S(1)} %get-tuple-element.26.refs_0_), channel_id=1, source_target_pairs={{0,4},{12,8},{1,5},{13,9},{2,6},{14,10},{3,7},{15,11},{16,20},{28,... | collective-permute-start | bytes 1572872 | tf_op jit(solution)/shard_map/ppermute | solution.py:495
  14.0 21.5 %collective-permute-start.2 = (f32[2,2,128,256]{3,2,1,0:T(8,128)S(1)}, f32[2,2,128,256]{3,2,1,0:T(8,128)S(1)}, u32[]{:S(2)}, u32[]{:S(2)}) collective-permute-start(f32[2,2,128,256]{3,2,1,0:T(8,128)S(1)} %get-tuple-element.31.refs_0_.refs_5_), channel_id=1, source_target_pairs={{0,4},{12,8},{1,5},{13,9},{2,6},{14,10},{3,7},{15,11},{16,20},{28,... | collective-permute-start | bytes 1572872 | tf_op jit(solution)/shard_map/ppermute | solution.py:495
  15.3 28.6 %collective-permute-start.5 = (f32[2,2,128,256]{3,2,1,0:T(8,128)S(1)}, f32[2,2,128,256]{3,2,1,0:T(8,128)S(1)}, u32[]{:S(2)}, u32[]{:S(2)}) collective-permute-start(f32[2,2,128,256]{3,2,1,0:T(8,128)S(1)} %get-tuple-element.34.refs_0_.refs_10_), channel_id=1, source_target_pairs={{0,4},{12,8},{1,5},{13,9},{2,6},{14,10},{3,7},{15,11},{16,20},{28,... | collective-permute-start | bytes 1572872 | tf_op jit(solution)/shard_map/ppermute | solution.py:495
  26.3 10.2 %collective-permute-start.1 = (f32[2,128,256]{2,1,0:T(8,128)S(1)}, f32[2,128,256]{2,1,0:T(8,128)S(1)}, u32[]{:S(2)}, u32[]{:S(2)}) collective-permute-start(f32[2,128,256]{2,1,0:T(8,128)S(1)} %state_steps.8.refs_0_), channel_id=1, source_target_pairs={{4,8},{5,9},{6,10},{7,11},{20,24},{21,25},{22,26},{23,27}} | collective-permute-start | bytes 786440 | tf_op jit(solution)/shard_map/ppermute | solution.py:512
  27.0 27.0 %collective-permute-start.8 = (f32[2,2,128,256]{3,2,1,0:T(8,128)S(1)}, f32[2,2,128,256]{3,2,1,0:T(8,128)S(1)}, u32[]{:S(2)}, u32[]{:S(2)}) collective-permute-start(f32[2,2,128,256]{3,2,1,0:T(8,128)S(1)} %get-tuple-element.37.refs_0_), channel_id=1, source_target_pairs={{0,4},{12,8},{1,5},{13,9},{2,6},{14,10},{3,7},{15,11},{16,20},{28,... | collective-permute-start | bytes 1572872 | tf_op jit(solution)/shard_map/ppermute | solution.py:495
  35.8 9.1 %collective-permute-start.4 = (f32[2,128,256]{2,1,0:T(8,128)S(1)}, f32[2,128,256]{2,1,0:T(8,128)S(1)}, u32[]{:S(2)}, u32[]{:S(2)}) collective-permute-start(f32[2,128,256]{2,1,0:T(8,128)S(1)} %state_steps.9.refs_3_), channel_id=1, source_target_pairs={{4,8},{5,9},{6,10},{7,11},{20,24},{21,25},{22,26},{23,27}} | collective-permute-start | bytes 786440 | tf_op jit(solution)/shard_map/ppermute | solution.py:512
  36.5 9.1 %collective-permute-start.9 = (f32[2,128,256]{2,1,0:T(8,128)S(1)}, f32[2,128,256]{2,1,0:T(8,128)S(1)}, u32[]{:S(2)}, u32[]{:S(2)}) collective-permute-start(f32[2,128,256]{2,1,0:T(8,128)S(1)} %get-tuple-element.38.refs_4_), channel_id=1, source_target_pairs={{8,4},{9,5},{10,6},{11,7},{24,20},{25,21},{26,22},{27,23}} | collective-permute-start | bytes 786440 | tf_op jit(solution)/shard_map/ppermute | solution.py:522
  44.2 11.5 %collective-permute-start.7 = (f32[2,128,256]{2,1,0:T(8,128)S(1)}, f32[2,128,256]{2,1,0:T(8,128)S(1)}, u32[]{:S(2)}, u32[]{:S(2)}) collective-permute-start(f32[2,128,256]{2,1,0:T(8,128)S(1)} %state_steps.11.refs_3_), channel_id=1, source_target_pairs={{4,8},{5,9},{6,10},{7,11},{20,24},{21,25},{22,26},{23,27}} | collective-permute-start | bytes 786440 | tf_op jit(solution)/shard_map/ppermute | solution.py:512
  44.9 11.5 %collective-permute-start.12 = (f32[2,128,256]{2,1,0:T(8,128)S(1)}, f32[2,128,256]{2,1,0:T(8,128)S(1)}, u32[]{:S(2)}, u32[]{:S(2)}) collective-permute-start(f32[2,128,256]{2,1,0:T(8,128)S(1)} %get-tuple-element.40.refs_9_), channel_id=1, source_target_pairs={{8,4},{9,5},{10,6},{11,7},{24,20},{25,21},{26,22},{27,23}} | collective-permute-start | bytes 786440 | tf_op jit(solution)/shard_map/ppermute | solution.py:522
  45.6 11.5 %collective-permute-start.13 = (f32[2,128,256]{2,1,0:T(8,128)S(1)}, f32[2,128,256]{2,1,0:T(8,128)S(1)}, u32[]{:S(2)}, u32[]{:S(2)}) collective-permute-start(f32[2,128,256]{2,1,0:T(8,128)S(1)} %collective-permute-done.9.refs_3_), channel_id=1, source_target_pairs={{4,0},{5,1},{6,2},{7,3},{20,16},{21,17},{22,18},{23,19}} | collective-permute-start | bytes 786440 | tf_op jit(solution)/shard_map/ppermute | solution.py:522
  54.3 21.9 %copy-start.5 = (f32[128]{0:T(128)S(1)}, f32[128]{0:T(128)}, u32[]{:S(2)}) copy-start(f32[128]{0:T(128)} %param.24) | copy-start | bytes 1540
  54.3 3.5 %collective-permute-start.11 = (f32[2,128,256]{2,1,0:T(8,128)S(1)}, f32[2,128,256]{2,1,0:T(8,128)S(1)}, u32[]{:S(2)}, u32[]{:S(2)}) collective-permute-start(f32[2,128,256]{2,1,0:T(8,128)S(1)} %state_steps.13.refs_3_), channel_id=1, source_target_pairs={{4,8},{5,9},{6,10},{7,11},{20,24},{21,25},{22,26},{23,27}} | collective-permute-start | bytes 786440 | tf_op jit(solution)/shard_map/ppermute | solution.py:512
  55.0 4.4 %collective-permute-start.3 = (f32[2,128,256]{2,1,0:T(8,128)S(1)}, f32[2,128,256]{2,1,0:T(8,128)S(1)}, u32[]{:S(2)}, u32[]{:S(2)}) collective-permute-start(f32[2,128,256]{2,1,0:T(8,128)S(1)} %get-tuple-element.33.refs_0_), channel_id=1, source_target_pairs={{8,12},{9,13},{10,14},{11,15},{24,28},{25,29},{26,30},{27,31}} | collective-permute-start | bytes 786440 | tf_op jit(solution)/shard_map/ppermute | solution.py:526
  55.7 4.4 %collective-permute-start.15 = (f32[2,128,256]{2,1,0:T(8,128)S(1)}, f32[2,128,256]{2,1,0:T(8,128)S(1)}, u32[]{:S(2)}, u32[]{:S(2)}) collective-permute-start(f32[2,128,256]{2,1,0:T(8,128)S(1)} %get-tuple-element.44.refs_14_), channel_id=1, source_target_pairs={{8,4},{9,5},{10,6},{11,7},{24,20},{25,21},{26,22},{27,23}} | collective-permute-start | bytes 786440 | tf_op jit(solution)/shard_map/ppermute | solution.py:522
  56.4 5.0 %collective-permute-start.6 = (f32[2,128,256]{2,1,0:T(8,128)S(1)}, f32[2,128,256]{2,1,0:T(8,128)S(1)}, u32[]{:S(2)}, u32[]{:S(2)}) collective-permute-start(f32[2,128,256]{2,1,0:T(8,128)S(1)} %get-tuple-element.36.refs_2_), channel_id=1, source_target_pairs={{8,12},{9,13},{10,14},{11,15},{24,28},{25,29},{26,30},{27,31}} | collective-permute-start | bytes 786440 | tf_op jit(solution)/shard_map/ppermute | solution.py:526
  57.1 14.4 %collective-permute-start.10 = (f32[2,128,256]{2,1,0:T(8,128)S(1)}, f32[2,128,256]{2,1,0:T(8,128)S(1)}, u32[]{:S(2)}, u32[]{:S(2)}) collective-permute-start(f32[2,128,256]{2,1,0:T(8,128)S(1)} %get-tuple-element.39.refs_3_), channel_id=1, source_target_pairs={{8,12},{9,13},{10,14},{11,15},{24,28},{25,29},{26,30},{27,31}} | collective-permute-start | bytes 786440 | tf_op jit(solution)/shard_map/ppermute | solution.py:526
  57.8 13.7 %collective-permute-start.16 = (f32[2,128,256]{2,1,0:T(8,128)S(1)}, f32[2,128,256]{2,1,0:T(8,128)S(1)}, u32[]{:S(2)}, u32[]{:S(2)}) collective-permute-start(f32[2,128,256]{2,1,0:T(8,128)S(1)} %collective-permute-done.12.refs_4_.refs_8_), channel_id=1, source_target_pairs={{4,0},{5,1},{6,2},{7,3},{20,16},{21,17},{22,18},{23,19}} | collective-permute-start | bytes 786440 | tf_op jit(solution)/shard_map/ppermute | solution.py:522
  59.4 16.8 %collective-permute-start.14 = (f32[2,128,256]{2,1,0:T(8,128)S(1)}, f32[2,128,256]{2,1,0:T(8,128)S(1)}, u32[]{:S(2)}, u32[]{:S(2)}) collective-permute-start(f32[2,128,256]{2,1,0:T(8,128)S(1)} %get-tuple-element.41.refs_17_), channel_id=1, source_target_pairs={{8,12},{9,13},{10,14},{11,15},{24,28},{25,29},{26,30},{27,31}} | collective-permute-start | bytes 786440 | tf_op jit(solution)/shard_map/ppermute | solution.py:526
  60.1 16.1 %collective-permute-start.18 = (f32[2,128,256]{2,1,0:T(8,128)S(1)}, f32[2,128,256]{2,1,0:T(8,128)S(1)}, u32[]{:S(2)}, u32[]{:S(2)}) collective-permute-start(f32[2,128,256]{2,1,0:T(8,128)S(1)} %collective-permute-done.15.refs_18_.refs_13_), channel_id=1, source_target_pairs={{4,0},{5,1},{6,2},{7,3},{20,16},{21,17},{22,18},{23,19}} | collective-permute-start | bytes 786440 | tf_op jit(solution)/shard_map/ppermute | solution.py:522
  61.4 14.8 %collective-permute-start.17 = (f32[2,128,256]{2,1,0:T(8,128)S(1)}, f32[2,128,256]{2,1,0:T(8,128)S(1)}, u32[]{:S(2)}, u32[]{:S(2)}) collective-permute-start(f32[2,128,256]{2,1,0:T(8,128)S(1)} %get-tuple-element.45.refs_4_), channel_id=1, source_target_pairs={{8,4},{9,5},{10,6},{11,7},{24,20},{25,21},{26,22},{27,23}} | collective-permute-start | bytes 786440 | tf_op jit(solution)/shard_map/ppermute | solution.py:522
  77.7 2.5 %copy-start.6 = (s32[16]{0:T(128)S(1)}, s32[16]{0:T(128)}, u32[]{:S(2)}) copy-start(s32[16]{0:T(128)} %refs_0_.7) | copy-start | bytes 196
  77.7 2.5 %copy-start.7 = (s32[16]{0:T(128)S(1)}, s32[16]{0:T(128)}, u32[]{:S(2)}) copy-start(s32[16]{0:T(128)} %refs_1_.7) | copy-start | bytes 196
  77.7 2.5 %copy-start.8 = (s32[16]{0:T(128)S(1)}, s32[16]{0:T(128)}, u32[]{:S(2)}) copy-start(s32[16]{0:T(128)} %refs_2_.7) | copy-start | bytes 196
  77.8 2.4 %collective-permute-start.20 = (f32[6,128,256]{2,1,0:T(8,128)S(1)}, f32[6,128,256]{2,1,0:T(8,128)S(1)}, u32[]{:S(2)}, u32[]{:S(2)}) collective-permute-start(f32[6,128,256]{2,1,0:T(8,128)S(1)} %settle.2.refs_3_), channel_id=1, source_target_pairs={{0,1},{1,0},{2,3},{3,2},{4,5},{5,4},{6,7},{7,6},{8,9},{9,8},{10,11... | collective-permute-start | bytes 2359304 | tf_op jit(solution)/shard_map/ppermute | solution.py:541
  77.8 11.2 %collective-permute-start.19 = (f32[2,128,256]{2,1,0:T(8,128)S(1)}, f32[2,128,256]{2,1,0:T(8,128)S(1)}, u32[]{:S(2)}, u32[]{:S(2)}) collective-permute-start(f32[2,128,256]{2,1,0:T(8,128)S(1)} %collective-permute-done.17.refs_20_.refs_3_), channel_id=1, source_target_pairs={{4,0},{5,1},{6,2},{7,3},{20,16},{21,17},{22,18},{23,19}} | collective-permute-start | bytes 786440 | tf_op jit(solution)/shard_map/ppermute | solution.py:522
  89.1 1.6 %collective-permute-start.21 = (f32[2,128,256]{2,1,0:T(8,128)S(1)}, f32[2,128,256]{2,1,0:T(8,128)S(1)}, u32[]{:S(2)}, u32[]{:S(2)}) collective-permute-start(f32[2,128,256]{2,1,0:T(8,128)S(1)} %settle.3.refs_3_), channel_id=1, source_target_pairs={{0,1},{1,0},{2,3},{3,2},{4,5},{5,4},{6,7},{7,6},{8,9},{9,8},{10,11... | collective-permute-start | bytes 786440 | tf_op jit(solution)/shard_map/ppermute | solution.py:541

commit v3 on v2

v3 whole, which is shorter than its diff:
```python
import functools
import math

import jax
import jax.numpy as jnp
from jax import lax
from jax.experimental import pallas as pl
from jax.experimental.pallas import tpu as pltpu
from jax.sharding import PartitionSpec as P

DK = 128
DV = 128
CH = 128
W2 = 2 * DV
EPS_NORM = 1e-06
HIGH = lax.Precision.HIGHEST
SCOPED = 24 * 1024 * 1024


def mm(left, right):
    return lax.dot_general(left, right, (((1,), (0,)), ((), ())), preferred_element_type=jnp.float32)


def diag2(pair):
    zero = jnp.zeros((pair.shape[0], DV), pair.dtype)
    top = jnp.concatenate([pair[:, :DV], zero], axis=1)
    low = jnp.concatenate([zero, pair[:, DV:]], axis=1)
    return jnp.concatenate([top, low], axis=0)


def low16(value):
    return value.astype(jnp.bfloat16)


def halves(value):
    high = low16(value)
    return high, low16(value - high.astype(jnp.float32))


def lanes2(col_a, col_b):
    shape = (col_a.shape[0], DV)
    return jnp.concatenate(
        [jnp.broadcast_to(col_a, shape), jnp.broadcast_to(col_b, shape)], axis=1
    )


def unit_rows(vectors):
    wide = vectors.astype(jnp.float32)
    factor = lax.rsqrt(jnp.sum(wide * wide, axis=-1, keepdims=True) + EPS_NORM)
    return low16(wide * factor)


def apply_pair(transfer, state, offset):
    t_hi, t_lo = halves(transfer)
    s_hi, s_lo = halves(state)
    hi = diag2(s_hi)
    return mm(t_hi, hi) + mm(t_lo, hi) + mm(t_hi, diag2(s_lo)) + offset


def gate_tables(decay):
    rows = lax.broadcasted_iota(jnp.int32, (CH, CH), 0)
    cols = lax.broadcasted_iota(jnp.int32, (CH, CH), 1)
    upper = jnp.where(rows <= cols, 1.0, 0.0).astype(jnp.float32)
    cum = lax.dot_general(
        decay, upper, (((1,), (0,)), ((), ())), precision=HIGH, preferred_element_type=jnp.float32
    )
    return cum, cum.T


def chunk_terms(chains):
    rows = lax.broadcasted_iota(jnp.int32, (CH, W2), 0)
    cols = jnp.bitwise_and(lax.broadcasted_iota(jnp.int32, (CH, W2), 1), CH - 1)
    causal = rows >= cols
    eye = jnp.where(rows == cols, 1.0, 0.0).astype(jnp.float32)
    eye16 = low16(eye)
    apart = jnp.bitwise_xor(rows, cols)
    strict = rows > cols
    masks = [
        low16(jnp.where(strict & (apart >= low) & (apart < high), -1.0, 0.0))
        for low, high in ((1, 8), (8, 32), (32, CH))
    ]

    heads = []
    for q, k, v, beta, cum_r, cum_c, ends in chains:
        qn = unit_rows(q)
        kn = unit_rows(k)
        heads.append((qn, kn, low16(kn.astype(jnp.float32).T)))
    grams = []
    for one, two in zip(heads[::2], heads[1::2]):
        rows_of = jnp.concatenate(
            [jnp.concatenate(one[1::-1], axis=0), jnp.concatenate(two[1::-1], axis=0)], axis=1
        )
        both = mm(rows_of, diag2(jnp.concatenate([one[2], two[2]], axis=1)))
        grams += [both[:, :DK], both[:, DK:]]
    if len(heads) % 2:
        qn, kn, kt = heads[-1]
        grams.append(mm(jnp.concatenate([kn, qn], axis=0), kt))
    lows, lefts, grows = [], [], []
    for (q, k, v, beta, cum_r, cum_c, ends), (qn, kn, kt), gram in zip(chains, heads, grams):
        kk = gram[:CH]
        qk = gram[CH:]
        bcast = lanes2(cum_c[:, 0:1], cum_c[:, 1:2])
        row = jnp.concatenate([cum_r[0:1], cum_r[1:2]], axis=1)
        gate = jnp.concatenate([beta[0:1], beta[1:2]], axis=1)
        scaled = jnp.exp(jnp.where(causal, bcast - row, -1e30)) * gate
        lows.append(low16(scaled * jnp.concatenate([kk, kk], axis=1)))
        attn = scaled * jnp.concatenate([qk, qk], axis=1)
        last = jnp.concatenate([cum_r[0:1, CH - 1 :], cum_r[1:2, CH - 1 :]], axis=0)
        last = jnp.concatenate(
            [jnp.broadcast_to(last[0:1], (1, DV)), jnp.broadcast_to(last[1:2], (1, DV))], axis=1
        )
        tail = jnp.exp(last - row) * gate
        ktf = kt.astype(jnp.float32)
        if ends:
            lefts.append(halves(attn))
        else:
            tail_k = jnp.concatenate([ktf, ktf], axis=1) * tail
            lefts.append(halves(jnp.concatenate([attn, tail_k], axis=0)))
        grows.append((jnp.exp(bcast), jnp.exp(row), jnp.exp(last)))
    nil = [low * masks[0] for low in lows]
    sq = [low16(mm(n, diag2(n))) for n in nil]
    fourth = [low16(mm(s, diag2(s))) for s in sq]
    inv = [low16(mm(eye16 + n, diag2(eye16 + s))) for n, s in zip(nil, sq)]
    inv = [low16(mm(i, diag2(eye16 + f))) for i, f in zip(inv, fourth)]
    for mask in masks[1:]:
        x = [low16(mm(i, diag2(low * mask))) for i, low in zip(inv, lows)]
        y = [low16(mm(eye16 + t, diag2(i))) for t, i in zip(x, inv)]
        z = [low16(mm(t, diag2(t))) for t in x]
        full = [mm(eye16 + t, diag2(i)) for t, i in zip(z, y)]
        inv = [low16(f) for f in full]
    ws = [
        low16(mm(low16(f * grow[1]), diag2(jnp.concatenate([kn, kn], axis=1))))
        for f, grow, (qn, kn, kt) in zip(full, grows, heads)
    ]
    us = [halves(mm(i, diag2(chain[2]))) for i, chain in zip(inv, chains)]
    by_w = [mm(left, diag2(w)) for (left, rest), w in zip(lefts, ws)]
    by_u = []
    for (left, rest), (u_hi, u_lo) in zip(lefts, us):
        hi = diag2(u_hi)
        by_u.append(mm(left, hi) + mm(rest, hi) + mm(left, diag2(u_lo)))
    out = []
    for (qn, kn, kt), grow, bw, bu in zip(heads, grows, by_w, by_u):
        qf = qn.astype(jnp.float32)
        a = jnp.concatenate([qf, qf], axis=1) * grow[0] - bw[:CH]
        if bw.shape[0] == CH:
            out.append((a, bu, None, None))
        else:
            out.append((a, bu[:CH], eye * grow[2] - bw[CH:], bu[CH:]))
    return out


def read_chains(pairs, heads, at, q_ref, k_ref, v_ref, beta_ref, decay_ref, slot, skip=0, ends=False):
    beta = beta_ref[slot, heads, at]
    cum_r, cum_c = gate_tables(decay_ref[slot, heads, at])
    return [
        (
            q_ref[slot, at, (skip + p) * DK : (skip + p + 1) * DK],
            k_ref[slot, at, (skip + p) * DK : (skip + p + 1) * DK],
            v_ref[slot, at, (skip + p) * W2 : (skip + p + 1) * W2],
            beta[2 * p : 2 * p + 2],
            cum_r[2 * p : 2 * p + 2],
            cum_c[:, 2 * p : 2 * p + 2],
            ends,
        )
        for p in range(pairs)
    ]


def window(first, pairs):
    return math.gcd(first, pairs) if first else pairs


def lane_specs(arrays, first, pairs, width):
    wide = window(first, pairs)
    specs, args = [], []
    for part in range(first, first + pairs, wide):
        specs.append(
            pl.BlockSpec(arrays.shape[:2] + (wide * width,), lambda i, at=part // wide: (0, 0, at))
        )
        args.append(arrays)
    return specs, args, wide


ANY = pl.BlockSpec(memory_space=pl.ANY)
WHOLE = pl.BlockSpec(memory_space=pltpu.VMEM)


SHORT = pl.CostEstimate(flops=1, transcendentals=0, bytes_accessed=1)


def near(value):
    return pltpu.with_memory_space_constraint(value, pltpu.VMEM)


def away(value):
    return pltpu.with_memory_space_constraint(value, pltpu.HBM)


class Spans:
    def __init__(self, refs, wide, width):
        self.refs, self.size, self.width = refs, wide * width, width

    def __getitem__(self, key):
        lanes = key[-1]
        part, at = divmod(lanes.start, self.size)
        return self.refs[part][key[:-1] + (slice(at, at + lanes.stop - lanes.start),)]


def places_of(sizes):
    return [(run, at) for run, size in enumerate(sizes) for at in range(size)]


def prompt_kernel(first, sizes, wide, count, *refs):
    pairs = sum(sizes)
    q_ref = Spans(refs[:count], wide, DK)
    k_ref = Spans(refs[count : 2 * count], wide, DK)
    v_ref = Spans(refs[2 * count : 3 * count], wide, W2)
    beta_ref, decay_ref = refs[3 * count : 3 * count + 2]
    *both, a_ref, b_ref = refs[len(refs) - 2 - len(sizes) :]
    heads = slice(2 * first, 2 * (first + pairs))
    chains = read_chains(
        pairs, heads, slice(0, CH), q_ref, k_ref, v_ref, beta_ref, decay_ref, 0
    )
    places = places_of(sizes)
    for p, (a, b, transfer, offset) in enumerate(chunk_terms(chains)):
        a_ref[:, p * W2 : (p + 1) * W2] = low16(a)
        b_ref[:, p * W2 : (p + 1) * W2] = low16(b)
        run, at = places[p]
        both[run][0, at] = transfer
        both[run][1, at] = offset


def prompt_terms(first, sizes, q, k, v, beta, decay, after=()):
    pairs = sum(sizes)
    q_specs, q_args, wide = lane_specs(q, first, pairs, DK)
    k_specs, k_args, wide = lane_specs(k, first, pairs, DK)
    v_specs, v_args, wide = lane_specs(v, first, pairs, W2)
    *boths, a, b = pl.pallas_call(
        functools.partial(prompt_kernel, first, sizes, wide, len(q_args)),
        grid=(1,),
        in_specs=q_specs
        + k_specs
        + v_specs
        + [
            pl.BlockSpec(beta.shape, lambda i: (0, 0, 0)),
            pl.BlockSpec(decay.shape, lambda i: (0, 0, 0)),
        ]
        + [ANY] * len(after),
        out_specs=[WHOLE] * (len(sizes) + 2),
        out_shape=[pltpu.VMEM((2, size, DK, W2), jnp.float32) for size in sizes]
        + [pltpu.VMEM((CH, pairs * W2), jnp.bfloat16)] * 2,
        compiler_params=pltpu.CompilerParams(vmem_limit_bytes=SCOPED),
        cost_estimate=SHORT,
        name="prompt_terms",
    )(*[away(value) for value in (*q_args, *k_args, *v_args, beta, decay)], *after)
    return boths, a, b


def suffix_kernel(first, unit, q_ref, k_ref, v_ref, beta_ref, decay_ref, *refs):
    a_ref, b_ref = refs[-2:]
    slots, tokens = q_ref.shape[:2]
    spans = tokens // CH
    heads = slice(2 * first, 2 * (first + unit))
    chains = []
    for slot in range(slots):
        for s in range(spans):
            at = slice(s * CH, (s + 1) * CH)
            chains += read_chains(
                unit, heads, at, q_ref, k_ref, v_ref, beta_ref, decay_ref, slot, first, s + 1 == spans
            )
    terms = chunk_terms(chains)
    for slot in range(slots):
        for p in range(unit):
            lanes = slice(p * W2, (p + 1) * W2)
            a, b, transfer, offset = terms[slot * spans * unit + p]
            a_ref[slot, 0:CH, lanes] = low16(a)
            b_ref[slot, 0:CH, lanes] = low16(b)
            for s in range(1, spans):
                a, b, t_next, o_next = terms[(slot * spans + s) * unit + p]
                a16 = low16(a)
                at = slice(s * CH, (s + 1) * CH)
                d_t = diag2(low16(transfer))
                d_o = diag2(low16(offset))
                a_ref[slot, at, lanes] = low16(mm(a16, d_t))
                b_ref[slot, at, lanes] = low16(mm(a16, d_o) + b)
                if s + 1 < spans:
                    t16 = low16(t_next)
                    transfer, offset = mm(t16, d_t), mm(t16, d_o) + o_next


def suffix_terms(first, unit, q, k, v, beta, decay, after=()):
    slots, tokens = q.shape[0], q.shape[1]
    return pl.pallas_call(
        functools.partial(suffix_kernel, first, unit),
        in_specs=[WHOLE] * 5 + [ANY] * len(after),
        out_specs=[WHOLE] * 2,
        out_shape=[pltpu.VMEM((slots, tokens, unit * W2), jnp.bfloat16)] * 2,
        compiler_params=pltpu.CompilerParams(vmem_limit_bytes=SCOPED),
        cost_estimate=SHORT,
        name="suffix_terms",
    )(near(q), near(k), near(v), near(beta), near(decay), *after)


def call_near(kernel, shapes, name, args, after=(), scratch=()):
    out = pl.pallas_call(
        kernel,
        in_specs=[WHOLE] * len(args) + [ANY] * len(after),
        out_specs=[WHOLE] * len(shapes),
        out_shape=[pltpu.VMEM(shape, jnp.float32) for shape in shapes],
        scratch_shapes=scratch,
        compiler_params=pltpu.CompilerParams(vmem_limit_bytes=SCOPED),
        cost_estimate=SHORT,
        name=name,
    )(*[near(value) for value in args], *after)
    return list(out)


def pair_at(ref, index):
    if len(ref.shape) == 3:
        return ref[index]
    return ref[index // ref.shape[1], index % ref.shape[1]]


def pack_kernel(half, sizes, *refs):
    both_ref, out_ref = refs[len(sizes)], refs[-1]
    here = lax.axis_index("seq")

    @pl.when(here < half)
    def _():
        for p, (run, at) in enumerate(places_of(sizes)):
            out_ref[p // out_ref.shape[1], p % out_ref.shape[1]] = refs[run][1, at]

    @pl.when(here >= half)
    def _():
        out_ref[...] = both_ref[...]


def pack(half, boths, both, after):
    sizes = [other.shape[1] for other in boths]
    (out,) = call_near(
        functools.partial(pack_kernel, half, sizes), [both.shape], "pack", [*boths, both], after
    )
    return out


def part_kernel(half, skips, left_ref, state_ref, *refs):
    out_ref = refs[-1]
    here = lax.axis_index("seq")

    @pl.when(here < half)
    def _():
        out_ref[...] = left_ref[skips[0] : skips[0] + out_ref.shape[0]]

    @pl.when(here >= half)
    def _():
        out_ref[...] = state_ref[skips[1] : skips[1] + out_ref.shape[0]]


def part(half, size, left, right, after):
    (out,) = call_near(
        functools.partial(part_kernel, half, (left[1], right[1])),
        [(size, DK, W2)],
        "part",
        [left[0], right[0]],
        after,
    )
    return out


def step_kernel(user, sizes, skip, *refs):
    state_ref, out_ref = refs[len(sizes)], refs[-1]

    @pl.when(lax.axis_index("seq") == user)
    def _():
        for p, (run, at) in enumerate(places_of(sizes)):
            out_ref[p] = apply_pair(refs[run][0, at], pair_at(state_ref, skip + p), refs[run][1, at])


def step(user, boths, state, after, skip=0):
    sizes = [both.shape[1] for both in boths]
    (out,) = call_near(
        functools.partial(step_kernel, user, sizes, skip),
        [(sum(sizes), DK, W2)],
        "state_step",
        [*boths, state],
        after,
    )
    return out


def meet_kernel(user, skip, far_ref, state_ref, *refs):
    out_ref = refs[-1]

    @pl.when(lax.axis_index("seq") == user)
    def _():
        for p in range(out_ref.shape[0]):
            out_ref[p] = apply_pair(far_ref[0, p], state_ref[skip + p], far_ref[1, p])


def meet(user, far, skip, state, after):
    (out,) = call_near(
        functools.partial(meet_kernel, user, skip),
        [far.shape[1:]],
        "final_state",
        [far, state],
        after,
    )
    return out


def settle_kernel(sizes, skips, *refs):
    here = lax.axis_index("seq")
    out_ref = refs[-1]
    wide = len(skips[0])
    at = 0
    for run, size in enumerate(sizes):
        for d, skip in enumerate(skips[run]):

            @pl.when(here == d)
            def _(at=at, size=size, skip=skip, source=refs[run * wide + d]):
                out_ref[at : at + size] = source[skip : skip + size]

        at += size


def settle(runs, after):
    sizes = [size for held, size in runs]
    (out,) = call_near(
        functools.partial(settle_kernel, sizes, [[skip for x, skip in held] for held, size in runs]),
        [(sum(sizes), DK, W2)],
        "settle",
        [x for held, size in runs for x, skip in held],
        after,
    )
    return out


def slot_rows_kernel(slots, n_prompt, sb_ref, bl_ref, bp_ref, *refs):
    out_ref = refs[-1]
    me = lax.axis_index("prompt")
    rank = lax.axis_index("seq") * n_prompt + me
    for slot in range(slots):
        branch = sb_ref[rank * slots + slot]
        mine = jnp.where(bp_ref[branch] == me, 1, 0)
        out_ref[slot, 0:8] = jnp.full((8, W2), bl_ref[branch], jnp.int32)
        out_ref[slot, 8:16] = jnp.full((8, W2), mine, jnp.int32)


def slot_rows(slots, tables, after):
    return pl.pallas_call(
        functools.partial(slot_rows_kernel, slots, lax.axis_size("prompt")),
        in_specs=[pl.BlockSpec(memory_space=pltpu.SMEM)] * 3 + [ANY] * len(after),
        out_specs=WHOLE,
        out_shape=pltpu.VMEM((slots, 16, W2), jnp.int32),
        compiler_params=pltpu.CompilerParams(vmem_limit_bytes=SCOPED),
        cost_estimate=SHORT,
        name="slot_rows",
    )(*tables, *after)


def finish(a, state, b, gain2):
    raw = mm(a, diag2(low16(state))) + b.astype(jnp.float32)
    share = diag2(jnp.full((DV, W2), 1.0 / DV, jnp.bfloat16))
    return raw * lax.rsqrt(mm(low16(raw * raw), share) + EPS_NORM) * gain2


def suffix_out_kernel(sizes, *refs):
    rows_ref, own_ref, other_ref, gain_ref = refs[:4]
    out_ref = refs[-1]
    slot = pl.program_id(0)
    mine = rows_ref[slot, 8:9] == 1
    gain = gain_ref[...]
    gain2 = jnp.concatenate([gain, gain], axis=1)
    tokens = out_ref.shape[1]
    live = lax.broadcasted_iota(jnp.int32, (tokens, W2), 0) < rows_ref[slot, 0:1]
    for p, (run, at) in enumerate(places_of(sizes)):
        source = slice(at * W2, (at + 1) * W2)
        a_ref, b_ref = refs[4 + 2 * run : 6 + 2 * run]
        state = jnp.where(mine, own_ref[p], other_ref[p])
        out = finish(a_ref[slot, :, source], state, b_ref[slot, :, source], gain2)
        out_ref[0, :, p * W2 : (p + 1) * W2] = low16(jnp.where(live, out, 0.0))


def suffix_outputs(first, rows, own, other, terms, gain, so_far, width, after=()):
    slots, tokens, _ = terms[0][0].shape
    sizes = [a.shape[2] // W2 for a, b in terms]
    pairs = sum(sizes)
    at = first // pairs
    args = [rows, own, other, gain] + [x for pair in terms for x in pair]
    in_specs = [WHOLE] * len(args)
    args = [near(value) for value in args]
    aliases = {}
    if so_far is not None:
        aliases = {len(args): 0}
        in_specs.append(ANY)
        args.append(away(so_far))
    return pl.pallas_call(
        functools.partial(suffix_out_kernel, sizes),
        grid=(slots,),
        in_specs=in_specs + [ANY] * len(after),
        out_specs=pl.BlockSpec((1, tokens, pairs * W2), lambda i: (i, 0, at)),
        out_shape=pltpu.HBM((slots, tokens, width), jnp.bfloat16),
        input_output_aliases=aliases,
        compiler_params=pltpu.CompilerParams(vmem_limit_bytes=SCOPED),
        cost_estimate=SHORT,
        name="suffix_out",
    )(*args, *after)


def prompt_out_kernel(calls, hops, *refs):
    here = lax.axis_index("seq")
    refs, out_ref, state_ref = list(refs[:-2]), refs[-2], refs[-1]
    for j, sizes in enumerate(hops):
        arrived = [refs.pop(0) for _ in sizes]

        @pl.when((here == j + 1) | ((here == 0) & (j == 0)))
        def _(sizes=sizes, arrived=arrived):
            for p, (run, at) in enumerate(places_of(sizes)):
                state_ref[p] = pair_at(arrived[run], at)

    terms = [(refs.pop(0), refs.pop(0)) for _ in calls]
    gain = refs[0][...]
    gain2 = jnp.concatenate([gain, gain], axis=1)
    for p, (call, at) in enumerate(places_of(calls)):
        source = slice(at * W2, (at + 1) * W2)
        a_ref, b_ref = terms[call]
        out = finish(a_ref[:, source], state_ref[p], b_ref[:, source], gain2)
        out_ref[0, :, p * W2 : (p + 1) * W2] = low16(out)


def prompt_outputs(arrived, terms, gain, width, after=()):
    pairs = width // W2
    calls = [a.shape[1] // W2 for a, b in terms]
    hops = [[size for x, size in hop] for hop in arrived]
    args = [x for hop in arrived for x, size in hop] + [x for pair in terms for x in pair] + [gain]
    return pl.pallas_call(
        functools.partial(prompt_out_kernel, calls, hops),
        grid=(1,),
        in_specs=[WHOLE] * len(args) + [ANY] * len(after),
        out_specs=pl.BlockSpec((1, CH, width), lambda i: (0, 0, 0)),
        out_shape=pltpu.HBM((1, CH, width), jnp.bfloat16),
        scratch_shapes=[pltpu.VMEM((pairs, DK, W2), jnp.float32)],
        compiler_params=pltpu.CompilerParams(vmem_limit_bytes=SCOPED),
        cost_estimate=SHORT,
        name="prompt_out",
    )(*[near(value) for value in args], *after)


def pair_product(left, right):
    pairs = left.shape[0]
    left = left.reshape(pairs, DK, 2, DK)
    right = right.reshape(pairs, DK, 2, DV)
    return jnp.einsum("pihj,pjhv->pihv", left, right, precision=HIGH).reshape(pairs, DK, W2)


def send(value, source, target):
    return lax.ppermute(value, "seq", [(source, target)])


class Forward:
    def __init__(self, boths, arrived, skip):
        self.boths, self.size = boths, sum(both.shape[1] for both in boths)
        self.skip = skip
        self.arrived, self.states = [arrived], []

    def advance(self, after):
        hop = len(self.states)
        state = step(hop + 1, self.boths, self.arrived[-1], after, 0 if hop else self.skip)
        self.states.append(state)
        count = lax.axis_size("seq")
        if hop + 2 < count and not (count == 4 and hop == 1):
            self.arrived.append(send(state, hop + 1, hop + 2))
        return (near(state),)


class Backward:
    def __init__(self, both, arrived, direct):
        self.both, self.size, self.direct, self.right = both, both.shape[1], direct, None
        count = lax.axis_size("seq")
        self.half = count // 2
        here = lax.axis_index("seq")
        self.far = arrived
        for source in range(count - 2, self.half, -1):
            sending = jnp.stack(
                [
                    pair_product(arrived[0], both[0]),
                    pair_product(arrived[0], both[1]) + arrived[1],
                ]
            )
            arrived = send(sending, source, source - 1)
            self.far = jnp.where(here == source - 1, arrived, self.far)

    def meet(self, after):
        half = self.half
        state = self.run.states[half - 1]
        self.mid = meet(half, self.far, self.skip, state, after)
        self.lefts = [send(self.mid, half, half - 1)]
        if self.direct:
            self.lefts = [send(self.mid, half, d) for d in range(half - 1)] + self.lefts
        elif half > 2:
            for d in range(half - 2, -1, -1):
                self.lefts.insert(0, send(self.lefts[0], d + 1, d))
        return (near(self.mid),)

    def pass_on(self, after):
        right = (self.run.states[self.half - 1], self.skip)
        left = right if self.direct else (self.lefts[0], 0)
        out = part(self.half, self.size, left, right, after)
        if self.direct:
            self.right = send(out, self.half, self.half + 1)
        else:
            self.right = lax.ppermute(out, "seq", [(1, 0), (2, 3)])
            self.lefts.insert(0, self.right)
        return (near(out),)

    def reach_end(self, after):
        if self.half == 2:
            self.end = step(3, [self.both], self.right, after)
            return (near(self.end),)
        while len(self.run.states) < lax.axis_size("seq") - 1:
            after = self.run.advance(after)
        return after

    def held(self):
        if self.half == 2:
            ends = [(self.end, 0)]
        else:
            ends = [(state, self.skip) for state in self.run.states[self.half :]]
        return [(left, 0) for left in self.lefts] + [(self.mid, 0)] + ends


def settle_runs(backs, after):
    half, count, here = backs[0].half, lax.axis_size("seq"), lax.axis_index("seq")
    final = settle([(back.held(), back.size) for back in backs], after)
    if half > 2:
        inner = (here > half) & (here < count - 1)
        far = jnp.concatenate([back.far for back in backs], axis=1)
        final = jnp.where(inner, pair_product(far[0], final) + far[1], final)
    prompts = lax.axis_size("prompt")
    other = lax.ppermute(final, "prompt", [(i, (i + 1) % prompts) for i in range(prompts)])
    return final, other


def plan_of(pairs):
    if pairs % 8:
        return [[1]] * pairs, [[1]] * pairs, [1] * pairs, [(pairs, pairs)], 0
    u = pairs // 4
    return [[u, u], [u, u // 2, u // 2]], [[2], [2], [1]], [u] * 4, [(2, 2), (3, 2)], 1


FIVE = (
    ("forward", 0),
    ("make", 0),
    ("make", 0),
    ("forward", 1),
    ("forward", 0),
    ("meet", 0),
    ("meet", 1),
    ("pass", 0),
    ("forward", 2),
    ("forward", 1),
    ("meet", 2),
    ("pass", 1),
    ("meet", 3),
    ("end", 0),
    ("forward", 2),
    ("pass", 4),
    ("meet", 4),
    ("pass", 2),
    ("end", 1),
    ("pass", 3),
    ("settle", 0),
    ("make", 0),
    ("land", 4),
    ("end", 2),
    ("end", 3),
    ("end", 4),
    ("settle", 1),
    ("prompt", 0),
    ("out", 0),
    ("out", 1),
)


def order_of(joins, half, makes, groups):
    if half == 2 and joins == [[2], [2], [1]]:
        return FIVE
    forwards, runs = sum(len(join) for join in joins), sum(sum(join) for join in joins)
    order = [("forward", k) for j in range(half) for k in range(forwards)]
    order += [("meet", k) for k in range(runs)]
    order += [("pass", k) for k in range(runs) if half == 2]
    order += [("make", k) for k in range(makes)]
    order += [("end", k) for k in range(runs)]
    order += [("settle", k) for k in range(groups)] + [("prompt", 0)]
    return order + [("out", k) for k in range(groups)]


def local(
    prompt_queries,
    prompt_keys,
    prompt_values,
    prompt_beta,
    prompt_decay,
    suffix_queries,
    suffix_keys,
    suffix_values,
    suffix_beta,
    suffix_decay,
    norm_gain,
    slot_branch,
    branch_length,
    branch_prompt,
):
    gain = norm_gain.reshape(1, DV)
    tables = (slot_branch, branch_length, branch_prompt)
    width = prompt_values.shape[2]
    prompt_in = (prompt_queries, prompt_keys, prompt_values, prompt_beta, prompt_decay)
    suffix_in = (suffix_queries, suffix_keys, suffix_values, suffix_beta, suffix_decay)
    half = lax.axis_size("seq") // 2

    calls, joins, units, groups, direct = plan_of(width // W2)
    total = sum(len(sizes) for sizes in calls)
    boths, terms, packed = [], [], []
    heads_of = [(k, size) for k, join in enumerate(joins) for size in join]
    bounds = [sum(size for k, size in heads_of[:i]) for i in range(len(heads_of) + 1)]

    def pack_up(after):
        while len(packed) < len(boths):
            k = len(packed)
            start = sum(sum(join) for join in joins[:k])
            stop = sum(sum(join) for join in joins[: k + 1])
            if len(boths) < stop:
                break
            packed.append(pack(half, boths[start:stop], boths[k], after))
            after = (near(packed[-1]),)
        return after

    made = []

    def make(after):
        if len(made) == len(units):
            return after
        unit = units[len(made)]
        made.append(suffix_terms(sum(units[: len(made)]), unit, *suffix_in, after=after))
        return (near(made[-1][0]),)

    first, last = 0, ()
    for call, sizes in enumerate(calls):
        new, a, b = prompt_terms(first, sizes, *prompt_in, after=last)
        boths += new
        terms.append((a, b))
        last = pack_up((near(a),))
        if call == 0:
            last = make(last)
        first += sum(sizes)
    opened = [
        lax.ppermute(out, "seq", [(0, 1), (2 * half - 1, 2 * half - 2)]) for out in packed
    ]
    forwards = []
    for i, (k, size) in enumerate(heads_of):
        start = sum(sum(join) for join in joins[:k])
        skip = sum(x.shape[1] for x in boths[start : bounds[i]])
        forwards.append(Forward(boths[bounds[i] : bounds[i + 1]], opened[k], skip))
    backwards = []
    for k, both in enumerate(boths):
        back = Backward(both, opened[k], k + direct >= total)
        f = [i for i in range(len(heads_of)) if bounds[i] <= k][-1]
        back.run = forwards[f]
        back.skip = sum(x.shape[1] for x in boths[bounds[f] : k])
        back.first = sum(x.shape[1] for x in boths[:k])
        backwards.append(back)
    rows = slot_rows(suffix_queries.shape[0], tables, last)
    last = (near(rows),)
    settled = {}
    edges = [sum(runs for runs, count in groups[:i]) for i in range(len(groups) + 1)]
    prompt_out, suffix_out = None, None
    for what, k in order_of(joins, half, len(units), len(groups)):
        if what == "make":
            last = make(last)
        elif what == "forward":
            last = forwards[k].advance(last)
        elif what == "meet":
            last = backwards[k].meet(last)
        elif what == "pass":
            last = backwards[k].pass_on(last)
        elif what == "land":
            last = last + tuple(near(left) for left in backwards[k].lefts)
        elif what == "end":
            last = backwards[k].reach_end(last)
        elif what == "settle":
            settled[k] = settle_runs(backwards[edges[k] : edges[k + 1]], last)
            last = (near(settled[k][0]),)
        elif what == "out":
            done = sum(count for runs, count in groups[:k])
            suffix_out = suffix_outputs(
                backwards[edges[k]].first,
                rows,
                *settled[k],
                made[done : done + groups[k][1]],
                gain,
                suffix_out,
                width,
                last if k == 0 else (),
            )
            last = (away(suffix_out),)
        else:
            lots = [sum(f.size for f, (i, n) in zip(forwards, heads_of) if i == k) for k in range(len(joins))]
            came = [list(zip(opened, lots))]
            for j in range(1, len(forwards[0].arrived)):
                came.append([(f.arrived[j], f.size) for f in forwards])
            if half == 2:
                came.append([(back.right, back.size) for back in backwards])
            prompt_out = prompt_outputs(came, terms, gain, width, last)
            last = (away(prompt_out),)
    return (prompt_out, suffix_out)


def solution(mesh):
    return jax.shard_map(
        local,
        mesh=mesh,
        in_specs=(
            P(("groups", "prompt"), "seq", "head"),
            P(("groups", "prompt"), "seq", "head"),
            P(("groups", "prompt"), "seq", "head"),
            P(("groups", "prompt"), "head", "seq"),
            P(("groups", "prompt"), "head", "seq"),
            P(("groups", "seq", "prompt"), None, "head"),
            P(("groups", "seq", "prompt"), None, "head"),
            P(("groups", "seq", "prompt"), None, "head"),
            P(("groups", "seq", "prompt"), "head", None),
            P(("groups", "seq", "prompt"), "head", None),
            P(),
            P("groups"),
            P("groups"),
            P("groups"),
        ),
        out_specs=(
            P(("groups", "prompt"), "seq", "head"),
            P(("groups", "seq", "prompt"), None, "head"),
        ),
        check_vma=False,
    )
```

time: 93.3 us -> 81.5 us (0.87)
  waiting for transfers between devices: 31.7 us -> 7.28 us
  starting transfers between devices: 25.2 us -> 38.5 us
  Pallas kernels: 34.7 us -> 32.4 us
  local copies, waits for them, and re-layouts: 0.04 us -> 1.27 us
    ppermute x20 -> x19, waiting for transfers between devices: 29.3 us -> 7.27 us  [the longest x4 6.41 us: pass_on(): self.right = lax.ppermute(out, 'seq', [(1, 0), (2, 3)])]
    ppermute x20 -> x19, starting transfers between devices: 25.1 us -> 38.1 us  [the longest x5 25.3 us: local(): lax.ppermute(out, 'seq', [(0, 1), (2 * half - 1, 2 * half - 2)])]
    ppermute x2, waiting for transfers between devices: 2.49 us -> 0.01 us  [settle_runs(): lax.ppermute(final, 'prompt', [(i, (i + 1) % prompts) for i in range(prom...]
    pallas_call x13 -> x32, Pallas kernels: 8.27 us -> 6.68 us  [the longest x2 4.11 us: suffix_outputs(): pl.pallas_call(functools.partial(suffix_out_kernel, sizes), grid=(slots,)...]
    unnamed x18 -> x20, local copies, waits for them, and re-layouts: 0.04 us -> 1.27 us
    pallas_call x4, Pallas kernels: 18.1 us -> 17.2 us  [suffix_terms(): pl.pallas_call(functools.partial(suffix_kernel, first, unit), in_specs=[W...]
  transfers between devices with their start and end apart: 22 -> 21, of which waited for: 7 -> 4; matrix products, arithmetic and copies ran while one was open for 0% -> 0% of each run, Pallas kernels for 30% -> 32%
where the time goes in v3:
time: 81.5 us; the launch traced here: 80.7 us
  starting transfers between devices  38.5 us (47%)
  Pallas kernels  32.4 us (40%)
  waiting for transfers between devices  7.28 us (9%)
  local copies, waits for them, and re-layouts  1.27 us (2%)
  between operations  1.25 us (2%)
    ppermute x5, starting transfers between devices, local(): lax.ppermute(out, 'seq', [(0, 1), (2 * half - 1, 2 * half - 2)])  25.3 us
    pallas_call x4, Pallas kernels, suffix_terms(): pl.pallas_call(functools.partial(suffix_kernel, first, unit), in_specs=[W...  17.2 us
    pallas_call x2, Pallas kernels, prompt_terms(): pl.pallas_call(functools.partial(prompt_kernel, first, sizes, wide, len(q...  8.49 us
    ppermute x10, starting transfers between devices, send(): return lax.ppermute(value, 'seq', [(source, target)])  7.6 us
    ppermute x4, waiting for transfers between devices, pass_on(): self.right = lax.ppermute(out, 'seq', [(1, 0), (2, 3)])  6.41 us
    ppermute x4, starting transfers between devices, pass_on(): self.right = lax.ppermute(out, 'seq', [(1, 0), (2, 3)])  5.17 us
    pallas_call x2, Pallas kernels, suffix_outputs(): pl.pallas_call(functools.partial(suffix_out_kernel, sizes), grid=(slots,)...  4.11 us
  transfers between devices with their start and end apart: 21, of which 4 were waited for; matrix products, arithmetic and copies ran while one was open for 0% of the time, Pallas kernels for 32%

profile of v3, /device:TPU:0, one launch (start us, length us, event | category | flops | bytes accessed | tf_op | source)
XLA Modules:
  0.0 80.7 jit_solution(4326464459281659958)
XLA Ops:
  0.7 4.3 %prompt_terms.2 = (f32[2,2,128,256]{3,2,1,0:T(8,128)S(1)}, f32[2,2,128,256]{3,2,1,0:T(8,128)S(1)}, bf16[128,1024]{1,0:T(8,128)(2,1)S(1)}, bf16[128,1024]{1,0:T(8,128)(2,1)S(1)}) custom-call(bf16[1,128,1024]{2,1,0:T(8,128)(2,1)} %refs_0_.3, bf16[1,128,1024]{2,1,0:T(8,128)(2,1)} %refs_1_.3, bf16[1,128,2048]{2,1,0:T(8,128)(2,1)} %refs_2_.3, ...), custom_call_target="tpu_custom_call" | custom-call | flops 1 | bytes 1 | tf_op jit(solution)/shard_map/prompt_terms/pallas_call | solution.py:238
  5.0 0.1 pack.5.refs_0_
  5.1 5.0 %collective-permute-start = (f32[2,2,128,256]{3,2,1,0:T(8,128)S(1)}, f32[2,2,128,256]{3,2,1,0:T(8,128)S(1)}, u32[]{:S(2)}, u32[]{:S(2)}) collective-permute-start(f32[2,2,128,256]{3,2,1,0:T(8,128)S(1)} %pack.5.refs_0_), channel_id=1, source_target_pairs={{0,4},{12,8},{1,5},{13,9},{2,6},{14,10},{3,7},{15,11},{16,20},{28,... | collective-permute-start | bytes 1572872 | tf_op jit(solution)/shard_map/ppermute | solution.py:757
  10.1 0.0 copy-start.2
  10.1 1.2 %copy-done.2 = bf16[2,256,1024]{2,1,0:T(8,128)(2,1)S(1)} copy-done((bf16[2,256,1024]{2,1,0:T(8,128)(2,1)S(1)}, bf16[2,256,1024]{2,1,0:T(8,128)(2,1)}, u32[]{:S(2)}) %copy-start.2) | copy-done | bytes 1048600
  11.3 4.3 %suffix_terms.4 = (bf16[2,256,512]{2,1,0:T(8,128)(2,1)S(1)}, bf16[2,256,512]{2,1,0:T(8,128)(2,1)S(1)}) custom-call(bf16[2,256,1024]{2,1,0:T(8,128)(2,1)S(1)} %copy-done.1, bf16[2,256,1024]{2,1,0:T(8,128)(2,1)S(1)} %copy-done.2, bf16[2,256,2048]{2,1,0:T(8,128)(2,1)S(1)} %copy-done, f32[2,16,256]{2,1,0:T(8,128)S(1)} %copy-done.4, f32[2,16,256]{2,1,0:T(8,128)S(1)} %copy-done.5, ...), custom_call_target="tpu_custom_call" | custom-call | flops 1 | bytes 1 | tf_op jit(solution)/shard_map/suffix_terms/pallas_call | solution.py:293
  15.6 4.2 %prompt_terms.3 = (f32[2,2,128,256]{3,2,1,0:T(8,128)S(1)}, f32[2,1,128,256]{3,2,1,0:T(8,128)S(1)}, f32[2,1,128,256]{3,2,1,0:T(8,128)S(1)}, bf16[128,1024]{1,0:T(8,128)(2,1)S(1)}, bf16[128,1024]{1,0:T(8,128)(2,1)S(1)}) custom-call(bf16[1,128,1024]{2,1,0:T(8,128)(2,1)} %refs_0_.3, bf16[1,128,1024]{2,1,0:T(8,128)(2,1)} %refs_1_.3, ...), custom_call_target="tpu_custom_call" | custom-call | flops 1 | bytes 1 | tf_op jit(solution)/shard_map/prompt_terms/pallas_call | solution.py:238
  19.8 0.0 copy-start.7
  19.8 0.0 copy-start.8
  19.8 0.0 copy-start.9
  19.9 1.5 %collective-permute-start.1 = (f32[2,2,128,256]{3,2,1,0:T(8,128)S(1)}, f32[2,2,128,256]{3,2,1,0:T(8,128)S(1)}, u32[]{:S(2)}, u32[]{:S(2)}) collective-permute-start(f32[2,2,128,256]{3,2,1,0:T(8,128)S(1)} %pack.6.refs_2_), channel_id=1, source_target_pairs={{0,4},{12,8},{1,5},{13,9},{2,6},{14,10},{3,7},{15,11},{16,20},{28,... | collective-permute-start | bytes 1572872 | tf_op jit(solution)/shard_map/ppermute | solution.py:757
  21.4 0.0 copy-start.3
  21.4 0.0 copy-done.7
  21.4 0.0 copy-done.8
  21.4 0.6 slot_rows.1.refs_3_.refs_0_
  22.0 0.0 collective-permute-done.refs_2_.far_ref.refs_0_
  22.1 0.7 collective-permute-start.3
  22.8 6.5 %collective-permute-start.2 = (f32[2,2,128,256]{3,2,1,0:T(8,128)S(1)}, f32[2,2,128,256]{3,2,1,0:T(8,128)S(1)}, u32[]{:S(2)}, u32[]{:S(2)}) collective-permute-start(f32[2,2,128,256]{3,2,1,0:T(8,128)S(1)} %pack.7.refs_1_), channel_id=1, source_target_pairs={{0,4},{12,8},{1,5},{13,9},{2,6},{14,10},{3,7},{15,11},{16,20},{28,... | collective-permute-start | bytes 1572872 | tf_op jit(solution)/shard_map/ppermute | solution.py:757
  29.3 4.3 %suffix_terms.5 = (bf16[2,256,512]{2,1,0:T(8,128)(2,1)S(1)}, bf16[2,256,512]{2,1,0:T(8,128)(2,1)S(1)}) custom-call(bf16[2,256,1024]{2,1,0:T(8,128)(2,1)S(1)} %copy-done.1, bf16[2,256,1024]{2,1,0:T(8,128)(2,1)S(1)} %copy-done.3, bf16[2,256,2048]{2,1,0:T(8,128)(2,1)S(1)} %copy-done, f32[2,16,256]{2,1,0:T(8,128)S(1)} %copy-done.4, f32[2,16,256]{2,1,0:T(8,128)S(1)} %copy-done.5, ...), custom_call_target="tpu_custom_call" | custom-call | flops 1 | bytes 1 | tf_op jit(solution)/shard_map/suffix_terms/pallas_call | solution.py:293
  33.6 4.3 %suffix_terms.6 = (bf16[2,256,512]{2,1,0:T(8,128)(2,1)S(1)}, bf16[2,256,512]{2,1,0:T(8,128)(2,1)S(1)}) custom-call(bf16[2,256,1024]{2,1,0:T(8,128)(2,1)S(1)} %copy-done.1, bf16[2,256,1024]{2,1,0:T(8,128)(2,1)S(1)} %copy-done.3, bf16[2,256,2048]{2,1,0:T(8,128)(2,1)S(1)} %copy-done, f32[2,16,256]{2,1,0:T(8,128)S(1)} %copy-done.4, f32[2,16,256]{2,1,0:T(8,128)S(1)} %copy-done.5, ...), custom_call_target="tpu_custom_call" | custom-call | flops 1 | bytes 1 | tf_op jit(solution)/shard_map/suffix_terms/pallas_call | solution.py:293
  37.9 0.0 collective-permute-done.1.refs_2_.far_ref.refs_1_
  37.9 0.7 collective-permute-start.4
  38.6 0.0 collective-permute-done.3.refs_2_.refs_3_
  38.7 0.7 collective-permute-start.5
  39.4 0.7 collective-permute-start.8
  40.1 4.1 %collective-permute-start.12 = (f32[2,1,128,256]{3,2,1,0:T(8,128)S(1)}, f32[2,1,128,256]{3,2,1,0:T(8,128)S(1)}, u32[]{:S(2)}, u32[]{:S(2)}) collective-permute-start(f32[2,1,128,256]{3,2,1,0:T(8,128)S(1)} %pack.8.refs_1_), channel_id=1, source_target_pairs={{0,4},{12,8},{1,5},{13,9},{2,6},{14,10},{3,7},{15,11},{16,20},{28,... | collective-permute-start | bytes 786440 | tf_op jit(solution)/shard_map/ppermute | solution.py:757
  44.2 0.0 collective-permute-done.5.left_ref.refs_1_
  44.3 1.3 %collective-permute-start.7 = (f32[2,128,256]{2,1,0:T(8,128)S(1)}, f32[2,128,256]{2,1,0:T(8,128)S(1)}, u32[]{:S(2)}, u32[]{:S(2)}) collective-permute-start(f32[2,128,256]{2,1,0:T(8,128)S(1)} %part.5.refs_2_), channel_id=1, source_target_pairs={{4,0},{8,12},{5,1},{9,13},{6,2},{10,14},{7,3},{11,15},{20,16},{24,... | collective-permute-start | bytes 786440 | tf_op jit(solution)/shard_map/ppermute | solution.py:612
  45.6 0.0 collective-permute-done.2.refs_1_.far_ref.refs_2_
  45.6 8.3 %collective-permute-start.11 = (f32[2,1,128,256]{3,2,1,0:T(8,128)S(1)}, f32[2,1,128,256]{3,2,1,0:T(8,128)S(1)}, u32[]{:S(2)}, u32[]{:S(2)}) collective-permute-start(f32[2,1,128,256]{3,2,1,0:T(8,128)S(1)} %pack.9.refs_0_), channel_id=1, source_target_pairs={{0,4},{12,8},{1,5},{13,9},{2,6},{14,10},{3,7},{15,11},{16,20},{28,... | collective-permute-start | bytes 786440 | tf_op jit(solution)/shard_map/ppermute | solution.py:757
  53.9 0.0 collective-permute-done.4.refs_2_.refs_4_
  53.9 0.7 collective-permute-start.10
  54.6 0.0 collective-permute-done.8.left_ref.refs_5_
  54.6 0.7 collective-permute-start.6
  55.4 0.0 collective-permute-done.12.far_ref
  55.4 1.3 %collective-permute-start.9 = (f32[2,128,256]{2,1,0:T(8,128)S(1)}, f32[2,128,256]{2,1,0:T(8,128)S(1)}, u32[]{:S(2)}, u32[]{:S(2)}) collective-permute-start(f32[2,128,256]{2,1,0:T(8,128)S(1)} %part.6.refs_0_), channel_id=1, source_target_pairs={{4,0},{8,12},{5,1},{9,13},{6,2},{10,14},{7,3},{11,15},{20,16},{24,... | collective-permute-start | bytes 786440 | tf_op jit(solution)/shard_map/ppermute | solution.py:612
  56.7 0.2 collective-permute-done.7.refs_1_.refs_0_.refs_6_
  56.9 0.0 collective-permute-done.6.refs_1_.refs_5_
  56.9 0.8 %collective-permute-done.11.far_ref = f32[2,1,128,256]{3,2,1,0:T(8,128)S(1)} collective-permute-done((f32[2,1,128,256]{3,2,1,0:T(8,128)S(1)}, f32[2,1,128,256]{3,2,1,0:T(8,128)S(1)}, u32[]{:S(2)}, u32[]{:S(2)}) %collective-permute-start.11) | collective-permute-done | bytes 262176 | tf_op jit(solution)/shard_map/ppermute | solution.py:757
  57.7 0.0 collective-permute-done.10.left_ref.refs_1_
  57.8 1.3 %collective-permute-start.13 = (f32[2,128,256]{2,1,0:T(8,128)S(1)}, f32[2,128,256]{2,1,0:T(8,128)S(1)}, u32[]{:S(2)}, u32[]{:S(2)}) collective-permute-start(f32[2,128,256]{2,1,0:T(8,128)S(1)} %part.8.refs_2_), channel_id=1, source_target_pairs={{4,0},{8,12},{5,1},{9,13},{6,2},{10,14},{7,3},{11,15},{20,16},{24,... | collective-permute-start | bytes 786440 | tf_op jit(solution)/shard_map/ppermute | solution.py:612
  59.1 0.7 collective-permute-start.14
  59.7 1.3 %collective-permute-start.17 = (f32[1,128,256]{2,1,0:T(8,128)S(1)}, f32[1,128,256]{2,1,0:T(8,128)S(1)}, u32[]{:S(2)}, u32[]{:S(2)}) collective-permute-start(f32[1,128,256]{2,1,0:T(8,128)S(1)} %final_state.9.refs_0_.refs_10_), channel_id=1, source_target_pairs={{8,0},{9,1},{10,2},{11,3},{24,16},{25,17},{26,18},{27,19}} | collective-permute-start | bytes 393224 | tf_op jit(solution)/shard_map/ppermute | solution.py:557
  61.0 0.7 collective-permute-start.18
  61.7 6.0 %collective-permute-done.9.refs_1_.refs_4_.refs_7_ = f32[2,128,256]{2,1,0:T(8,128)S(1)} collective-permute-done((f32[2,128,256]{2,1,0:T(8,128)S(1)}, f32[2,128,256]{2,1,0:T(8,128)S(1)}, u32[]{:S(2)}, u32[]{:S(2)}) %collective-permute-start.9) | collective-permute-done | bytes 262176 | tf_op jit(solution)/shard_map/ppermute | solution.py:612
  67.7 0.0 collective-permute-done.14.left_ref.refs_5_
  67.7 1.3 %collective-permute-start.15 = (f32[1,128,256]{2,1,0:T(8,128)S(1)}, f32[1,128,256]{2,1,0:T(8,128)S(1)}, u32[]{:S(2)}, u32[]{:S(2)}) collective-permute-start(f32[1,128,256]{2,1,0:T(8,128)S(1)} %part.9.refs_8_), channel_id=1, source_target_pairs={{4,0},{8,12},{5,1},{9,13},{6,2},{10,14},{7,3},{11,15},{20,16},{24,... | collective-permute-start | bytes 393224 | tf_op jit(solution)/shard_map/ppermute | solution.py:612
  69.0 0.9 %collective-permute-start.16 = (f32[1,128,256]{2,1,0:T(8,128)S(1)}, f32[1,128,256]{2,1,0:T(8,128)S(1)}, u32[]{:S(2)}, u32[]{:S(2)}) collective-permute-start(f32[1,128,256]{2,1,0:T(8,128)S(1)} %part.7.refs_0_), channel_id=1, source_target_pairs={{8,12},{9,13},{10,14},{11,15},{24,28},{25,29},{26,30},{27,31}} | collective-permute-start | bytes 393224 | tf_op jit(solution)/shard_map/ppermute | solution.py:557
  69.9 0.1 settle.2.refs_0_.refs_1_
  70.0 4.3 %suffix_terms.7 = (bf16[2,256,512]{2,1,0:T(8,128)(2,1)S(1)}, bf16[2,256,512]{2,1,0:T(8,128)(2,1)S(1)}) custom-call(bf16[2,256,1024]{2,1,0:T(8,128)(2,1)S(1)} %copy-done.1, bf16[2,256,1024]{2,1,0:T(8,128)(2,1)S(1)} %copy-done.3, bf16[2,256,2048]{2,1,0:T(8,128)(2,1)S(1)} %copy-done, f32[2,16,256]{2,1,0:T(8,128)S(1)} %copy-done.4, f32[2,16,256]{2,1,0:T(8,128)S(1)} %copy-done.5, ...), custom_call_target="tpu_custom_call" | custom-call | flops 1 | bytes 1 | tf_op jit(solution)/shard_map/suffix_terms/pallas_call | solution.py:293
  74.3 0.0 collective-permute-done.17.refs_3_.refs_8_
  74.3 0.1 collective-permute-start.20
  74.4 0.0 collective-permute-done.18.refs_4_.refs_9_
  74.4 0.0 collective-permute-done.13.refs_1_.refs_0_.refs_8_
  74.4 0.0 copy-start.6
  74.4 0.2 collective-permute-done.15.refs_1_.refs_4_.refs_9_
  74.7 0.0 collective-permute-done.16.refs_1_.refs_10_
  74.7 0.1 settle.3.refs_16_.refs_1_
  74.8 0.4 collective-permute-start.19
  75.1 1.4 %prompt_out.1.refs_8_ = bf16[1,128,2048]{2,1,0:T(8,128)(2,1)} custom-call(f32[2,2,128,256]{3,2,1,0:T(8,128)S(1)} %collective-permute-done.refs_2_.far_ref.refs_0_, f32[2,2,128,256]{3,2,1,0:T(8,128)S(1)} %collective-permute-done.1.refs_2_.far_ref.refs_1_, f32[2,2,128,256]{3,2,1,0:T(8,128)S(1)} %collective-permute-done.2.refs_1_.far_ref.refs_2_, ...), custom_call_target="tpu_custom_call" | custom-call | flops 1 | bytes 1 | tf_op jit(solution)/shard_map/prompt_out/pallas_call | solution.py:536
  76.6 0.0 collective-permute-done.20.refs_2_
  76.6 2.1 %suffix_out.2.refs_8_ = bf16[2,256,2048]{2,1,0:T(8,128)(2,1)} custom-call(s32[2,16,256]{2,1,0:T(8,128)S(1)} %slot_rows.1.refs_3_.refs_0_, f32[4,128,256]{2,1,0:T(8,128)S(1)} %settle.2.refs_0_.refs_1_, f32[4,128,256]{2,1,0:T(8,128)S(1)} %collective-permute-done.20.refs_2_, f32[1,128]{1,0:T(1,128)S(1)} %bitcast.2, ...), custom_call_target="tpu_custom_call" | custom-call | flops 1 | bytes 1 | tf_op jit(solution)/shard_map/suffix_out/pallas_call | solution.py:497
  78.6 0.0 collective-permute-done.19.refs_2_
  78.6 2.0 %suffix_out.3 = bf16[2,256,2048]{2,1,0:T(8,128)(2,1)} custom-call(s32[2,16,256]{2,1,0:T(8,128)S(1)} %slot_rows.1.refs_3_.refs_0_, f32[4,128,256]{2,1,0:T(8,128)S(1)} %settle.3.refs_16_.refs_1_, f32[4,128,256]{2,1,0:T(8,128)S(1)} %collective-permute-done.19.refs_2_, f32[1,128]{1,0:T(1,128)S(1)} %bitcast.3, ...), custom_call_target="tpu_custom_call", output_to_operand_aliasing={{}: (8, {})} | custom-call | flops 1 | bytes 1 | tf_op jit(solution)/shard_map/suffix_out/pallas_call | solution.py:497
  (36 shorter events, 0.4 us)
Async XLA Ops:
  0.6 9.4 %copy-start.1 = (bf16[2,256,1024]{2,1,0:T(8,128)(2,1)S(1)}, bf16[2,256,1024]{2,1,0:T(8,128)(2,1)}, u32[]{:S(2)}) copy-start(bf16[2,256,1024]{2,1,0:T(8,128)(2,1)} %q_ref.7) | copy-start | bytes 3145732
  0.6 9.4 %copy-start = (bf16[2,256,2048]{2,1,0:T(8,128)(2,1)S(1)}, bf16[2,256,2048]{2,1,0:T(8,128)(2,1)}, u32[]{:S(2)}) copy-start(bf16[2,256,2048]{2,1,0:T(8,128)(2,1)} %v_ref.7) | copy-start | bytes 6291460
  0.7 9.4 %copy-start.4 = (f32[2,16,256]{2,1,0:T(8,128)S(1)}, f32[2,16,256]{2,1,0:T(8,128)}, u32[]{:S(2)}) copy-start(f32[2,16,256]{2,1,0:T(8,128)} %beta_ref.7) | copy-start | bytes 98308
  0.7 9.4 %copy-start.5 = (f32[2,16,256]{2,1,0:T(8,128)S(1)}, f32[2,16,256]{2,1,0:T(8,128)}, u32[]{:S(2)}) copy-start(f32[2,16,256]{2,1,0:T(8,128)} %decay_ref.7) | copy-start | bytes 98308
  5.1 17.0 %collective-permute-start = (f32[2,2,128,256]{3,2,1,0:T(8,128)S(1)}, f32[2,2,128,256]{3,2,1,0:T(8,128)S(1)}, u32[]{:S(2)}, u32[]{:S(2)}) collective-permute-start(f32[2,2,128,256]{3,2,1,0:T(8,128)S(1)} %pack.5.refs_0_), channel_id=1, source_target_pairs={{0,4},{12,8},{1,5},{13,9},{2,6},{14,10},{3,7},{15,11},{16,20},{28,... | collective-permute-start | bytes 1572872 | tf_op jit(solution)/shard_map/ppermute | solution.py:757
  10.1 1.2 %copy-start.2 = (bf16[2,256,1024]{2,1,0:T(8,128)(2,1)S(1)}, bf16[2,256,1024]{2,1,0:T(8,128)(2,1)}, u32[]{:S(2)}) copy-start(bf16[2,256,1024]{2,1,0:T(8,128)(2,1)} %k_ref.7) | copy-start | bytes 3145732
  19.8 1.6 %copy-start.7 = (s32[16]{0:T(128)S(1)}, s32[16]{0:T(128)}, u32[]{:S(2)}) copy-start(s32[16]{0:T(128)} %sb_ref.1) | copy-start | bytes 196
  19.8 1.6 %copy-start.8 = (s32[16]{0:T(128)S(1)}, s32[16]{0:T(128)}, u32[]{:S(2)}) copy-start(s32[16]{0:T(128)} %bl_ref.1) | copy-start | bytes 196
  19.8 1.6 %copy-start.9 = (s32[16]{0:T(128)S(1)}, s32[16]{0:T(128)}, u32[]{:S(2)}) copy-start(s32[16]{0:T(128)} %bp_ref.1) | copy-start | bytes 196
  19.9 18.0 %collective-permute-start.1 = (f32[2,2,128,256]{3,2,1,0:T(8,128)S(1)}, f32[2,2,128,256]{3,2,1,0:T(8,128)S(1)}, u32[]{:S(2)}, u32[]{:S(2)}) collective-permute-start(f32[2,2,128,256]{3,2,1,0:T(8,128)S(1)} %pack.6.refs_2_), channel_id=1, source_target_pairs={{0,4},{12,8},{1,5},{13,9},{2,6},{14,10},{3,7},{15,11},{16,20},{28,... | collective-permute-start | bytes 1572872 | tf_op jit(solution)/shard_map/ppermute | solution.py:757
  21.4 7.9 %copy-start.3 = (bf16[2,256,1024]{2,1,0:T(8,128)(2,1)S(1)}, bf16[2,256,1024]{2,1,0:T(8,128)(2,1)}, u32[]{:S(2)}) copy-start(bf16[2,256,1024]{2,1,0:T(8,128)(2,1)} %k_ref.7) | copy-start | bytes 3145732
  22.1 16.5 %collective-permute-start.3 = (f32[4,128,256]{2,1,0:T(8,128)S(1)}, f32[4,128,256]{2,1,0:T(8,128)S(1)}, u32[]{:S(2)}, u32[]{:S(2)}) collective-permute-start(f32[4,128,256]{2,1,0:T(8,128)S(1)} %state_step.11.refs_0_), channel_id=1, source_target_pairs={{4,8},{5,9},{6,10},{7,11},{20,24},{21,25},{22,26},{23,27}} | collective-permute-start | bytes 1572872 | tf_op jit(solution)/shard_map/ppermute | solution.py:557
  22.8 22.8 %collective-permute-start.2 = (f32[2,2,128,256]{3,2,1,0:T(8,128)S(1)}, f32[2,2,128,256]{3,2,1,0:T(8,128)S(1)}, u32[]{:S(2)}, u32[]{:S(2)}) collective-permute-start(f32[2,2,128,256]{3,2,1,0:T(8,128)S(1)} %pack.7.refs_1_), channel_id=1, source_target_pairs={{0,4},{12,8},{1,5},{13,9},{2,6},{14,10},{3,7},{15,11},{16,20},{28,... | collective-permute-start | bytes 1572872 | tf_op jit(solution)/shard_map/ppermute | solution.py:757
  37.9 16.0 %collective-permute-start.4 = (f32[3,128,256]{2,1,0:T(8,128)S(1)}, f32[3,128,256]{2,1,0:T(8,128)S(1)}, u32[]{:S(2)}, u32[]{:S(2)}) collective-permute-start(f32[3,128,256]{2,1,0:T(8,128)S(1)} %state_step.12.refs_3_), channel_id=1, source_target_pairs={{4,8},{5,9},{6,10},{7,11},{20,24},{21,25},{22,26},{23,27}} | collective-permute-start | bytes 1179656 | tf_op jit(solution)/shard_map/ppermute | solution.py:557
  38.7 5.5 %collective-permute-start.5 = (f32[2,128,256]{2,1,0:T(8,128)S(1)}, f32[2,128,256]{2,1,0:T(8,128)S(1)}, u32[]{:S(2)}, u32[]{:S(2)}) collective-permute-start(f32[2,128,256]{2,1,0:T(8,128)S(1)} %final_state.5.refs_0_.refs_2_), channel_id=1, source_target_pairs={{8,4},{9,5},{10,6},{11,7},{24,20},{25,21},{26,22},{27,23}} | collective-permute-start | bytes 786440 | tf_op jit(solution)/shard_map/ppermute | solution.py:557
  39.4 15.3 %collective-permute-start.8 = (f32[2,128,256]{2,1,0:T(8,128)S(1)}, f32[2,128,256]{2,1,0:T(8,128)S(1)}, u32[]{:S(2)}, u32[]{:S(2)}) collective-permute-start(f32[2,128,256]{2,1,0:T(8,128)S(1)} %final_state.6.refs_0_.refs_6_), channel_id=1, source_target_pairs={{8,4},{9,5},{10,6},{11,7},{24,20},{25,21},{26,22},{27,23}} | collective-permute-start | bytes 786440 | tf_op jit(solution)/shard_map/ppermute | solution.py:557
  40.1 15.3 %collective-permute-start.12 = (f32[2,1,128,256]{3,2,1,0:T(8,128)S(1)}, f32[2,1,128,256]{3,2,1,0:T(8,128)S(1)}, u32[]{:S(2)}, u32[]{:S(2)}) collective-permute-start(f32[2,1,128,256]{3,2,1,0:T(8,128)S(1)} %pack.8.refs_1_), channel_id=1, source_target_pairs={{0,4},{12,8},{1,5},{13,9},{2,6},{14,10},{3,7},{15,11},{16,20},{28,... | collective-permute-start | bytes 786440 | tf_op jit(solution)/shard_map/ppermute | solution.py:757
  44.3 12.6 %collective-permute-start.7 = (f32[2,128,256]{2,1,0:T(8,128)S(1)}, f32[2,128,256]{2,1,0:T(8,128)S(1)}, u32[]{:S(2)}, u32[]{:S(2)}) collective-permute-start(f32[2,128,256]{2,1,0:T(8,128)S(1)} %part.5.refs_2_), channel_id=1, source_target_pairs={{4,0},{8,12},{5,1},{9,13},{6,2},{10,14},{7,3},{11,15},{20,16},{24,... | collective-permute-start | bytes 786440 | tf_op jit(solution)/shard_map/ppermute | solution.py:612
  45.6 12.1 %collective-permute-start.11 = (f32[2,1,128,256]{3,2,1,0:T(8,128)S(1)}, f32[2,1,128,256]{3,2,1,0:T(8,128)S(1)}, u32[]{:S(2)}, u32[]{:S(2)}) collective-permute-start(f32[2,1,128,256]{3,2,1,0:T(8,128)S(1)} %pack.9.refs_0_), channel_id=1, source_target_pairs={{0,4},{12,8},{1,5},{13,9},{2,6},{14,10},{3,7},{15,11},{16,20},{28,... | collective-permute-start | bytes 786440 | tf_op jit(solution)/shard_map/ppermute | solution.py:757
  53.9 3.8 %collective-permute-start.10 = (f32[2,128,256]{2,1,0:T(8,128)S(1)}, f32[2,128,256]{2,1,0:T(8,128)S(1)}, u32[]{:S(2)}, u32[]{:S(2)}) collective-permute-start(f32[2,128,256]{2,1,0:T(8,128)S(1)} %final_state.7.refs_0_.refs_2_), channel_id=1, source_target_pairs={{8,4},{9,5},{10,6},{11,7},{24,20},{25,21},{26,22},{27,23}} | collective-permute-start | bytes 786440 | tf_op jit(solution)/shard_map/ppermute | solution.py:557
  54.6 2.2 %collective-permute-start.6 = (f32[1,128,256]{2,1,0:T(8,128)S(1)}, f32[1,128,256]{2,1,0:T(8,128)S(1)}, u32[]{:S(2)}, u32[]{:S(2)}) collective-permute-start(f32[1,128,256]{2,1,0:T(8,128)S(1)} %state_step.14.refs_3_), channel_id=1, source_target_pairs={{4,8},{5,9},{6,10},{7,11},{20,24},{21,25},{22,26},{23,27}} | collective-permute-start | bytes 393224 | tf_op jit(solution)/shard_map/ppermute | solution.py:557
  55.4 12.3 %collective-permute-start.9 = (f32[2,128,256]{2,1,0:T(8,128)S(1)}, f32[2,128,256]{2,1,0:T(8,128)S(1)}, u32[]{:S(2)}, u32[]{:S(2)}) collective-permute-start(f32[2,128,256]{2,1,0:T(8,128)S(1)} %part.6.refs_0_), channel_id=1, source_target_pairs={{4,0},{8,12},{5,1},{9,13},{6,2},{10,14},{7,3},{11,15},{20,16},{24,... | collective-permute-start | bytes 786440 | tf_op jit(solution)/shard_map/ppermute | solution.py:612
  57.8 16.7 %collective-permute-start.13 = (f32[2,128,256]{2,1,0:T(8,128)S(1)}, f32[2,128,256]{2,1,0:T(8,128)S(1)}, u32[]{:S(2)}, u32[]{:S(2)}) collective-permute-start(f32[2,128,256]{2,1,0:T(8,128)S(1)} %part.8.refs_2_), channel_id=1, source_target_pairs={{4,0},{8,12},{5,1},{9,13},{6,2},{10,14},{7,3},{11,15},{20,16},{24,... | collective-permute-start | bytes 786440 | tf_op jit(solution)/shard_map/ppermute | solution.py:612
  59.1 8.7 %collective-permute-start.14 = (f32[1,128,256]{2,1,0:T(8,128)S(1)}, f32[1,128,256]{2,1,0:T(8,128)S(1)}, u32[]{:S(2)}, u32[]{:S(2)}) collective-permute-start(f32[1,128,256]{2,1,0:T(8,128)S(1)} %final_state.8.refs_2_.refs_6_), channel_id=1, source_target_pairs={{8,4},{9,5},{10,6},{11,7},{24,20},{25,21},{26,22},{27,23}} | collective-permute-start | bytes 393224 | tf_op jit(solution)/shard_map/ppermute | solution.py:557
  59.7 14.6 %collective-permute-start.17 = (f32[1,128,256]{2,1,0:T(8,128)S(1)}, f32[1,128,256]{2,1,0:T(8,128)S(1)}, u32[]{:S(2)}, u32[]{:S(2)}) collective-permute-start(f32[1,128,256]{2,1,0:T(8,128)S(1)} %final_state.9.refs_0_.refs_10_), channel_id=1, source_target_pairs={{8,0},{9,1},{10,2},{11,3},{24,16},{25,17},{26,18},{27,19}} | collective-permute-start | bytes 393224 | tf_op jit(solution)/shard_map/ppermute | solution.py:557
  61.0 13.4 %collective-permute-start.18 = (f32[1,128,256]{2,1,0:T(8,128)S(1)}, f32[1,128,256]{2,1,0:T(8,128)S(1)}, u32[]{:S(2)}, u32[]{:S(2)}) collective-permute-start(f32[1,128,256]{2,1,0:T(8,128)S(1)} %final_state.9.refs_0_.refs_10_), channel_id=1, source_target_pairs={{8,4},{9,5},{10,6},{11,7},{24,20},{25,21},{26,22},{27,23}} | collective-permute-start | bytes 393224 | tf_op jit(solution)/shard_map/ppermute | solution.py:557
  67.7 7.0 %collective-permute-start.15 = (f32[1,128,256]{2,1,0:T(8,128)S(1)}, f32[1,128,256]{2,1,0:T(8,128)S(1)}, u32[]{:S(2)}, u32[]{:S(2)}) collective-permute-start(f32[1,128,256]{2,1,0:T(8,128)S(1)} %part.9.refs_8_), channel_id=1, source_target_pairs={{4,0},{8,12},{5,1},{9,13},{6,2},{10,14},{7,3},{11,15},{20,16},{24,... | collective-permute-start | bytes 393224 | tf_op jit(solution)/shard_map/ppermute | solution.py:612
  69.0 5.7 %collective-permute-start.16 = (f32[1,128,256]{2,1,0:T(8,128)S(1)}, f32[1,128,256]{2,1,0:T(8,128)S(1)}, u32[]{:S(2)}, u32[]{:S(2)}) collective-permute-start(f32[1,128,256]{2,1,0:T(8,128)S(1)} %part.7.refs_0_), channel_id=1, source_target_pairs={{8,12},{9,13},{10,14},{11,15},{24,28},{25,29},{26,30},{27,31}} | collective-permute-start | bytes 393224 | tf_op jit(solution)/shard_map/ppermute | solution.py:557
  74.3 2.3 %collective-permute-start.20 = (f32[4,128,256]{2,1,0:T(8,128)S(1)}, f32[4,128,256]{2,1,0:T(8,128)S(1)}, u32[]{:S(2)}, u32[]{:S(2)}) collective-permute-start(f32[4,128,256]{2,1,0:T(8,128)S(1)} %settle.2.refs_0_.refs_1_), channel_id=1, source_target_pairs={{0,1},{1,0},{2,3},{3,2},{4,5},{5,4},{6,7},{7,6},{8,9},{9,8},{10,11... | collective-permute-start | bytes 1572872 | tf_op jit(solution)/shard_map/ppermute | solution.py:640
  74.4 0.7 copy-start.6
  74.8 3.9 %collective-permute-start.19 = (f32[4,128,256]{2,1,0:T(8,128)S(1)}, f32[4,128,256]{2,1,0:T(8,128)S(1)}, u32[]{:S(2)}, u32[]{:S(2)}) collective-permute-start(f32[4,128,256]{2,1,0:T(8,128)S(1)} %settle.3.refs_16_.refs_1_), channel_id=1, source_target_pairs={{0,1},{1,0},{2,3},{3,2},{4,5},{5,4},{6,7},{7,6},{8,9},{9,8},{10,11... | collective-permute-start | bytes 1572872 | tf_op jit(solution)/shard_map/ppermute | solution.py:640

commit v4 on v3

--- a/solution.py
+++ b/solution.py
@@ -667,10 +667,10 @@
     ("pass", 4),
     ("meet", 4),
     ("pass", 2),
+    ("pass", 3),
+    ("make", 0),
     ("end", 1),
-    ("pass", 3),
     ("settle", 0),
-    ("make", 0),
     ("land", 4),
     ("end", 2),
     ("end", 3),

time: 81.5 us -> 80.3 us (0.985)
  waiting for transfers between devices: 7.28 us -> 6.07 us
  transfers between devices with their start and end apart: 21 -> 21, of which waited for: 4 -> 4; matrix products, arithmetic and copies ran while one was open for 0% -> 0% of each run, Pallas kernels for 32% -> 33%
where the time goes in v4:
time: 80.3 us; the launch traced here: 79.5 us
  starting transfers between devices  38.4 us (48%)
  Pallas kernels  32.4 us (40%)
  waiting for transfers between devices  6.07 us (8%)
  local copies, waits for them, and re-layouts  1.27 us (2%)
  between operations  1.27 us (2%)
    ppermute x5, starting transfers between devices, local(): lax.ppermute(out, 'seq', [(0, 1), (2 * half - 1, 2 * half - 2)])  25.3 us
    pallas_call x4, Pallas kernels, suffix_terms(): pl.pallas_call(functools.partial(suffix_kernel, first, unit), in_specs=[W...  17.2 us
    pallas_call x2, Pallas kernels, prompt_terms(): pl.pallas_call(functools.partial(prompt_kernel, first, sizes, wide, len(q...  8.49 us
    ppermute x10, starting transfers between devices, send(): return lax.ppermute(value, 'seq', [(source, target)])  7.58 us
    ppermute x4, waiting for transfers between devices, pass_on(): self.right = lax.ppermute(out, 'seq', [(1, 0), (2, 3)])  5.89 us
    ppermute x4, starting transfers between devices, pass_on(): self.right = lax.ppermute(out, 'seq', [(1, 0), (2, 3)])  5.17 us
    pallas_call x2, Pallas kernels, suffix_outputs(): pl.pallas_call(functools.partial(suffix_out_kernel, sizes), grid=(slots,)...  4.13 us
  transfers between devices with their start and end apart: 21, of which 4 were waited for; matrix products, arithmetic and copies ran while one was open for 0% of the time, Pallas kernels for 33%

profile of v4, /device:TPU:0, one launch (start us, length us, event | category | flops | bytes accessed | tf_op | source)
XLA Modules:
  0.0 79.5 jit_solution(11814578204878218109)
XLA Ops:
  0.7 4.3 %prompt_terms.2 = (f32[2,2,128,256]{3,2,1,0:T(8,128)S(1)}, f32[2,2,128,256]{3,2,1,0:T(8,128)S(1)}, bf16[128,1024]{1,0:T(8,128)(2,1)S(1)}, bf16[128,1024]{1,0:T(8,128)(2,1)S(1)}) custom-call(bf16[1,128,1024]{2,1,0:T(8,128)(2,1)} %refs_0_.3, bf16[1,128,1024]{2,1,0:T(8,128)(2,1)} %refs_1_.3, bf16[1,128,2048]{2,1,0:T(8,128)(2,1)} %refs_2_.3, ...), custom_call_target="tpu_custom_call" | custom-call | flops 1 | bytes 1 | tf_op jit(solution)/shard_map/prompt_terms/pallas_call | solution.py:238
  5.0 0.1 pack.5.refs_0_
  5.1 5.0 %collective-permute-start = (f32[2,2,128,256]{3,2,1,0:T(8,128)S(1)}, f32[2,2,128,256]{3,2,1,0:T(8,128)S(1)}, u32[]{:S(2)}, u32[]{:S(2)}) collective-permute-start(f32[2,2,128,256]{3,2,1,0:T(8,128)S(1)} %pack.5.refs_0_), channel_id=1, source_target_pairs={{0,4},{12,8},{1,5},{13,9},{2,6},{14,10},{3,7},{15,11},{16,20},{28,... | collective-permute-start | bytes 1572872 | tf_op jit(solution)/shard_map/ppermute | solution.py:757
  10.1 0.0 copy-start.2
  10.1 1.2 %copy-done.2 = bf16[2,256,1024]{2,1,0:T(8,128)(2,1)S(1)} copy-done((bf16[2,256,1024]{2,1,0:T(8,128)(2,1)S(1)}, bf16[2,256,1024]{2,1,0:T(8,128)(2,1)}, u32[]{:S(2)}) %copy-start.2) | copy-done | bytes 1048600
  11.3 4.3 %suffix_terms.4 = (bf16[2,256,512]{2,1,0:T(8,128)(2,1)S(1)}, bf16[2,256,512]{2,1,0:T(8,128)(2,1)S(1)}) custom-call(bf16[2,256,1024]{2,1,0:T(8,128)(2,1)S(1)} %copy-done.1, bf16[2,256,1024]{2,1,0:T(8,128)(2,1)S(1)} %copy-done.2, bf16[2,256,2048]{2,1,0:T(8,128)(2,1)S(1)} %copy-done, f32[2,16,256]{2,1,0:T(8,128)S(1)} %copy-done.4, f32[2,16,256]{2,1,0:T(8,128)S(1)} %copy-done.5, ...), custom_call_target="tpu_custom_call" | custom-call | flops 1 | bytes 1 | tf_op jit(solution)/shard_map/suffix_terms/pallas_call | solution.py:293
  15.6 4.2 %prompt_terms.3 = (f32[2,2,128,256]{3,2,1,0:T(8,128)S(1)}, f32[2,1,128,256]{3,2,1,0:T(8,128)S(1)}, f32[2,1,128,256]{3,2,1,0:T(8,128)S(1)}, bf16[128,1024]{1,0:T(8,128)(2,1)S(1)}, bf16[128,1024]{1,0:T(8,128)(2,1)S(1)}) custom-call(bf16[1,128,1024]{2,1,0:T(8,128)(2,1)} %refs_0_.3, bf16[1,128,1024]{2,1,0:T(8,128)(2,1)} %refs_1_.3, ...), custom_call_target="tpu_custom_call" | custom-call | flops 1 | bytes 1 | tf_op jit(solution)/shard_map/prompt_terms/pallas_call | solution.py:238
  19.8 0.0 copy-start.7
  19.8 0.0 copy-start.8
  19.8 0.0 copy-start.9
  19.9 1.5 %collective-permute-start.1 = (f32[2,2,128,256]{3,2,1,0:T(8,128)S(1)}, f32[2,2,128,256]{3,2,1,0:T(8,128)S(1)}, u32[]{:S(2)}, u32[]{:S(2)}) collective-permute-start(f32[2,2,128,256]{3,2,1,0:T(8,128)S(1)} %pack.6.refs_2_), channel_id=1, source_target_pairs={{0,4},{12,8},{1,5},{13,9},{2,6},{14,10},{3,7},{15,11},{16,20},{28,... | collective-permute-start | bytes 1572872 | tf_op jit(solution)/shard_map/ppermute | solution.py:757
  21.4 0.0 copy-start.3
  21.4 0.0 copy-done.7
  21.4 0.0 copy-done.8
  21.4 0.6 slot_rows.1.refs_3_.refs_0_
  22.0 0.0 collective-permute-done.refs_2_.far_ref.refs_0_
  22.1 0.7 collective-permute-start.3
  22.8 6.5 %collective-permute-start.2 = (f32[2,2,128,256]{3,2,1,0:T(8,128)S(1)}, f32[2,2,128,256]{3,2,1,0:T(8,128)S(1)}, u32[]{:S(2)}, u32[]{:S(2)}) collective-permute-start(f32[2,2,128,256]{3,2,1,0:T(8,128)S(1)} %pack.7.refs_1_), channel_id=1, source_target_pairs={{0,4},{12,8},{1,5},{13,9},{2,6},{14,10},{3,7},{15,11},{16,20},{28,... | collective-permute-start | bytes 1572872 | tf_op jit(solution)/shard_map/ppermute | solution.py:757
  29.3 4.3 %suffix_terms.5 = (bf16[2,256,512]{2,1,0:T(8,128)(2,1)S(1)}, bf16[2,256,512]{2,1,0:T(8,128)(2,1)S(1)}) custom-call(bf16[2,256,1024]{2,1,0:T(8,128)(2,1)S(1)} %copy-done.1, bf16[2,256,1024]{2,1,0:T(8,128)(2,1)S(1)} %copy-done.3, bf16[2,256,2048]{2,1,0:T(8,128)(2,1)S(1)} %copy-done, f32[2,16,256]{2,1,0:T(8,128)S(1)} %copy-done.4, f32[2,16,256]{2,1,0:T(8,128)S(1)} %copy-done.5, ...), custom_call_target="tpu_custom_call" | custom-call | flops 1 | bytes 1 | tf_op jit(solution)/shard_map/suffix_terms/pallas_call | solution.py:293
  33.6 4.3 %suffix_terms.6 = (bf16[2,256,512]{2,1,0:T(8,128)(2,1)S(1)}, bf16[2,256,512]{2,1,0:T(8,128)(2,1)S(1)}) custom-call(bf16[2,256,1024]{2,1,0:T(8,128)(2,1)S(1)} %copy-done.1, bf16[2,256,1024]{2,1,0:T(8,128)(2,1)S(1)} %copy-done.3, bf16[2,256,2048]{2,1,0:T(8,128)(2,1)S(1)} %copy-done, f32[2,16,256]{2,1,0:T(8,128)S(1)} %copy-done.4, f32[2,16,256]{2,1,0:T(8,128)S(1)} %copy-done.5, ...), custom_call_target="tpu_custom_call" | custom-call | flops 1 | bytes 1 | tf_op jit(solution)/shard_map/suffix_terms/pallas_call | solution.py:293
  37.9 0.0 collective-permute-done.1.refs_2_.far_ref.refs_1_
  37.9 0.7 collective-permute-start.4
  38.6 0.0 collective-permute-done.3.refs_2_.refs_3_
  38.7 0.7 collective-permute-start.5
  39.4 0.7 collective-permute-start.8
  40.1 4.1 %collective-permute-start.12 = (f32[2,1,128,256]{3,2,1,0:T(8,128)S(1)}, f32[2,1,128,256]{3,2,1,0:T(8,128)S(1)}, u32[]{:S(2)}, u32[]{:S(2)}) collective-permute-start(f32[2,1,128,256]{3,2,1,0:T(8,128)S(1)} %pack.8.refs_1_), channel_id=1, source_target_pairs={{0,4},{12,8},{1,5},{13,9},{2,6},{14,10},{3,7},{15,11},{16,20},{28,... | collective-permute-start | bytes 786440 | tf_op jit(solution)/shard_map/ppermute | solution.py:757
  44.2 0.0 collective-permute-done.5.left_ref.refs_1_
  44.3 1.3 %collective-permute-start.7 = (f32[2,128,256]{2,1,0:T(8,128)S(1)}, f32[2,128,256]{2,1,0:T(8,128)S(1)}, u32[]{:S(2)}, u32[]{:S(2)}) collective-permute-start(f32[2,128,256]{2,1,0:T(8,128)S(1)} %part.5.refs_2_), channel_id=1, source_target_pairs={{4,0},{8,12},{5,1},{9,13},{6,2},{10,14},{7,3},{11,15},{20,16},{24,... | collective-permute-start | bytes 786440 | tf_op jit(solution)/shard_map/ppermute | solution.py:612
  45.6 0.0 collective-permute-done.2.refs_1_.far_ref.refs_2_
  45.6 8.3 %collective-permute-start.11 = (f32[2,1,128,256]{3,2,1,0:T(8,128)S(1)}, f32[2,1,128,256]{3,2,1,0:T(8,128)S(1)}, u32[]{:S(2)}, u32[]{:S(2)}) collective-permute-start(f32[2,1,128,256]{3,2,1,0:T(8,128)S(1)} %pack.9.refs_0_), channel_id=1, source_target_pairs={{0,4},{12,8},{1,5},{13,9},{2,6},{14,10},{3,7},{15,11},{16,20},{28,... | collective-permute-start | bytes 786440 | tf_op jit(solution)/shard_map/ppermute | solution.py:757
  53.9 0.0 collective-permute-done.4.refs_2_.refs_4_
  53.9 0.7 collective-permute-start.10
  54.6 0.0 collective-permute-done.8.left_ref.refs_5_
  54.6 0.7 collective-permute-start.6
  55.4 0.0 collective-permute-done.12.far_ref
  55.4 1.3 %collective-permute-start.9 = (f32[2,128,256]{2,1,0:T(8,128)S(1)}, f32[2,128,256]{2,1,0:T(8,128)S(1)}, u32[]{:S(2)}, u32[]{:S(2)}) collective-permute-start(f32[2,128,256]{2,1,0:T(8,128)S(1)} %part.6.refs_0_), channel_id=1, source_target_pairs={{4,0},{8,12},{5,1},{9,13},{6,2},{10,14},{7,3},{11,15},{20,16},{24,... | collective-permute-start | bytes 786440 | tf_op jit(solution)/shard_map/ppermute | solution.py:612
  56.7 0.2 collective-permute-done.7.refs_1_.refs_0_.refs_6_
  56.9 0.0 collective-permute-done.6.refs_1_.refs_5_
  56.9 0.7 collective-permute-start.14
  57.6 0.1 collective-permute-done.11.far_ref
  57.7 0.0 collective-permute-done.10.left_ref.refs_1_
  57.8 1.3 %collective-permute-start.13 = (f32[2,128,256]{2,1,0:T(8,128)S(1)}, f32[2,128,256]{2,1,0:T(8,128)S(1)}, u32[]{:S(2)}, u32[]{:S(2)}) collective-permute-start(f32[2,128,256]{2,1,0:T(8,128)S(1)} %part.8.refs_0_), channel_id=1, source_target_pairs={{4,0},{8,12},{5,1},{9,13},{6,2},{10,14},{7,3},{11,15},{20,16},{24,... | collective-permute-start | bytes 786440 | tf_op jit(solution)/shard_map/ppermute | solution.py:612
  59.1 1.3 %collective-permute-start.17 = (f32[1,128,256]{2,1,0:T(8,128)S(1)}, f32[1,128,256]{2,1,0:T(8,128)S(1)}, u32[]{:S(2)}, u32[]{:S(2)}) collective-permute-start(f32[1,128,256]{2,1,0:T(8,128)S(1)} %final_state.9.refs_0_.refs_10_), channel_id=1, source_target_pairs={{8,0},{9,1},{10,2},{11,3},{24,16},{25,17},{26,18},{27,19}} | collective-permute-start | bytes 393224 | tf_op jit(solution)/shard_map/ppermute | solution.py:557
  60.4 0.7 collective-permute-start.18
  61.0 0.0 collective-permute-done.14.left_ref.refs_5_
  61.1 1.3 %collective-permute-start.15 = (f32[1,128,256]{2,1,0:T(8,128)S(1)}, f32[1,128,256]{2,1,0:T(8,128)S(1)}, u32[]{:S(2)}, u32[]{:S(2)}) collective-permute-start(f32[1,128,256]{2,1,0:T(8,128)S(1)} %part.9.refs_0_), channel_id=1, source_target_pairs={{4,0},{8,12},{5,1},{9,13},{6,2},{10,14},{7,3},{11,15},{20,16},{24,... | collective-permute-start | bytes 393224 | tf_op jit(solution)/shard_map/ppermute | solution.py:612
  62.4 5.4 %collective-permute-done.9.refs_1_.refs_4_.refs_7_ = f32[2,128,256]{2,1,0:T(8,128)S(1)} collective-permute-done((f32[2,128,256]{2,1,0:T(8,128)S(1)}, f32[2,128,256]{2,1,0:T(8,128)S(1)}, u32[]{:S(2)}, u32[]{:S(2)}) %collective-permute-start.9) | collective-permute-done | bytes 262176 | tf_op jit(solution)/shard_map/ppermute | solution.py:612
  67.8 0.9 %collective-permute-start.16 = (f32[1,128,256]{2,1,0:T(8,128)S(1)}, f32[1,128,256]{2,1,0:T(8,128)S(1)}, u32[]{:S(2)}, u32[]{:S(2)}) collective-permute-start(f32[1,128,256]{2,1,0:T(8,128)S(1)} %part.7.refs_0_), channel_id=1, source_target_pairs={{8,12},{9,13},{10,14},{11,15},{24,28},{25,29},{26,30},{27,31}} | collective-permute-start | bytes 393224 | tf_op jit(solution)/shard_map/ppermute | solution.py:557
  68.7 4.3 %suffix_terms.7 = (bf16[2,256,512]{2,1,0:T(8,128)(2,1)S(1)}, bf16[2,256,512]{2,1,0:T(8,128)(2,1)S(1)}) custom-call(bf16[2,256,1024]{2,1,0:T(8,128)(2,1)S(1)} %copy-done.1, bf16[2,256,1024]{2,1,0:T(8,128)(2,1)S(1)} %copy-done.3, bf16[2,256,2048]{2,1,0:T(8,128)(2,1)S(1)} %copy-done, f32[2,16,256]{2,1,0:T(8,128)S(1)} %copy-done.4, f32[2,16,256]{2,1,0:T(8,128)S(1)} %copy-done.5, ...), custom_call_target="tpu_custom_call" | custom-call | flops 1 | bytes 1 | tf_op jit(solution)/shard_map/suffix_terms/pallas_call | solution.py:293
  73.0 0.1 settle.2.refs_2_.refs_1_
  73.1 0.0 collective-permute-done.17.refs_3_.refs_8_
  73.1 0.1 collective-permute-start.20
  73.2 0.0 collective-permute-done.18.refs_4_.refs_9_
  73.2 0.0 collective-permute-done.13.refs_1_.refs_0_.refs_8_
  73.2 0.0 copy-start.6
  73.2 0.3 collective-permute-done.15.refs_1_.refs_4_.refs_9_
  73.5 0.0 collective-permute-done.16.refs_1_.refs_10_
  73.5 0.1 settle.3.refs_16_.refs_1_
  73.6 0.3 collective-permute-start.19
  73.9 1.4 %prompt_out.1.refs_8_ = bf16[1,128,2048]{2,1,0:T(8,128)(2,1)} custom-call(f32[2,2,128,256]{3,2,1,0:T(8,128)S(1)} %collective-permute-done.refs_2_.far_ref.refs_0_, f32[2,2,128,256]{3,2,1,0:T(8,128)S(1)} %collective-permute-done.1.refs_2_.far_ref.refs_1_, f32[2,2,128,256]{3,2,1,0:T(8,128)S(1)} %collective-permute-done.2.refs_1_.far_ref.refs_2_, ...), custom_call_target="tpu_custom_call" | custom-call | flops 1 | bytes 1 | tf_op jit(solution)/shard_map/prompt_out/pallas_call | solution.py:536
  75.3 0.0 collective-permute-done.20.refs_2_
  75.3 2.1 %suffix_out.2.refs_8_ = bf16[2,256,2048]{2,1,0:T(8,128)(2,1)} custom-call(s32[2,16,256]{2,1,0:T(8,128)S(1)} %slot_rows.1.refs_3_.refs_0_, f32[4,128,256]{2,1,0:T(8,128)S(1)} %settle.2.refs_2_.refs_1_, f32[4,128,256]{2,1,0:T(8,128)S(1)} %collective-permute-done.20.refs_2_, f32[1,128]{1,0:T(1,128)S(1)} %bitcast.2, ...), custom_call_target="tpu_custom_call" | custom-call | flops 1 | bytes 1 | tf_op jit(solution)/shard_map/suffix_out/pallas_call | solution.py:497
  77.4 0.0 collective-permute-done.19.refs_2_
  77.4 2.1 %suffix_out.3 = bf16[2,256,2048]{2,1,0:T(8,128)(2,1)} custom-call(s32[2,16,256]{2,1,0:T(8,128)S(1)} %slot_rows.1.refs_3_.refs_0_, f32[4,128,256]{2,1,0:T(8,128)S(1)} %settle.3.refs_16_.refs_1_, f32[4,128,256]{2,1,0:T(8,128)S(1)} %collective-permute-done.19.refs_2_, f32[1,128]{1,0:T(1,128)S(1)} %bitcast.3, ...), custom_call_target="tpu_custom_call", output_to_operand_aliasing={{}: (8, {})} | custom-call | flops 1 | bytes 1 | tf_op jit(solution)/shard_map/suffix_out/pallas_call | solution.py:497
  (36 shorter events, 0.4 us)
Async XLA Ops:
  0.6 9.4 %copy-start.1 = (bf16[2,256,1024]{2,1,0:T(8,128)(2,1)S(1)}, bf16[2,256,1024]{2,1,0:T(8,128)(2,1)}, u32[]{:S(2)}) copy-start(bf16[2,256,1024]{2,1,0:T(8,128)(2,1)} %q_ref.7) | copy-start | bytes 3145732
  0.6 9.4 %copy-start = (bf16[2,256,2048]{2,1,0:T(8,128)(2,1)S(1)}, bf16[2,256,2048]{2,1,0:T(8,128)(2,1)}, u32[]{:S(2)}) copy-start(bf16[2,256,2048]{2,1,0:T(8,128)(2,1)} %v_ref.7) | copy-start | bytes 6291460
  0.7 9.4 %copy-start.4 = (f32[2,16,256]{2,1,0:T(8,128)S(1)}, f32[2,16,256]{2,1,0:T(8,128)}, u32[]{:S(2)}) copy-start(f32[2,16,256]{2,1,0:T(8,128)} %beta_ref.7) | copy-start | bytes 98308
  0.7 9.4 %copy-start.5 = (f32[2,16,256]{2,1,0:T(8,128)S(1)}, f32[2,16,256]{2,1,0:T(8,128)}, u32[]{:S(2)}) copy-start(f32[2,16,256]{2,1,0:T(8,128)} %decay_ref.7) | copy-start | bytes 98308
  5.1 17.0 %collective-permute-start = (f32[2,2,128,256]{3,2,1,0:T(8,128)S(1)}, f32[2,2,128,256]{3,2,1,0:T(8,128)S(1)}, u32[]{:S(2)}, u32[]{:S(2)}) collective-permute-start(f32[2,2,128,256]{3,2,1,0:T(8,128)S(1)} %pack.5.refs_0_), channel_id=1, source_target_pairs={{0,4},{12,8},{1,5},{13,9},{2,6},{14,10},{3,7},{15,11},{16,20},{28,... | collective-permute-start | bytes 1572872 | tf_op jit(solution)/shard_map/ppermute | solution.py:757
  10.1 1.2 %copy-start.2 = (bf16[2,256,1024]{2,1,0:T(8,128)(2,1)S(1)}, bf16[2,256,1024]{2,1,0:T(8,128)(2,1)}, u32[]{:S(2)}) copy-start(bf16[2,256,1024]{2,1,0:T(8,128)(2,1)} %k_ref.7) | copy-start | bytes 3145732
  19.8 1.6 %copy-start.7 = (s32[16]{0:T(128)S(1)}, s32[16]{0:T(128)}, u32[]{:S(2)}) copy-start(s32[16]{0:T(128)} %sb_ref.1) | copy-start | bytes 196
  19.8 1.6 %copy-start.8 = (s32[16]{0:T(128)S(1)}, s32[16]{0:T(128)}, u32[]{:S(2)}) copy-start(s32[16]{0:T(128)} %bl_ref.1) | copy-start | bytes 196
  19.8 1.6 %copy-start.9 = (s32[16]{0:T(128)S(1)}, s32[16]{0:T(128)}, u32[]{:S(2)}) copy-start(s32[16]{0:T(128)} %bp_ref.1) | copy-start | bytes 196
  19.9 18.0 %collective-permute-start.1 = (f32[2,2,128,256]{3,2,1,0:T(8,128)S(1)}, f32[2,2,128,256]{3,2,1,0:T(8,128)S(1)}, u32[]{:S(2)}, u32[]{:S(2)}) collective-permute-start(f32[2,2,128,256]{3,2,1,0:T(8,128)S(1)} %pack.6.refs_2_), channel_id=1, source_target_pairs={{0,4},{12,8},{1,5},{13,9},{2,6},{14,10},{3,7},{15,11},{16,20},{28,... | collective-permute-start | bytes 1572872 | tf_op jit(solution)/shard_map/ppermute | solution.py:757
  21.4 7.9 %copy-start.3 = (bf16[2,256,1024]{2,1,0:T(8,128)(2,1)S(1)}, bf16[2,256,1024]{2,1,0:T(8,128)(2,1)}, u32[]{:S(2)}) copy-start(bf16[2,256,1024]{2,1,0:T(8,128)(2,1)} %k_ref.7) | copy-start | bytes 3145732
  22.1 16.5 %collective-permute-start.3 = (f32[4,128,256]{2,1,0:T(8,128)S(1)}, f32[4,128,256]{2,1,0:T(8,128)S(1)}, u32[]{:S(2)}, u32[]{:S(2)}) collective-permute-start(f32[4,128,256]{2,1,0:T(8,128)S(1)} %state_step.11.refs_0_), channel_id=1, source_target_pairs={{4,8},{5,9},{6,10},{7,11},{20,24},{21,25},{22,26},{23,27}} | collective-permute-start | bytes 1572872 | tf_op jit(solution)/shard_map/ppermute | solution.py:557
  22.8 22.8 %collective-permute-start.2 = (f32[2,2,128,256]{3,2,1,0:T(8,128)S(1)}, f32[2,2,128,256]{3,2,1,0:T(8,128)S(1)}, u32[]{:S(2)}, u32[]{:S(2)}) collective-permute-start(f32[2,2,128,256]{3,2,1,0:T(8,128)S(1)} %pack.7.refs_1_), channel_id=1, source_target_pairs={{0,4},{12,8},{1,5},{13,9},{2,6},{14,10},{3,7},{15,11},{16,20},{28,... | collective-permute-start | bytes 1572872 | tf_op jit(solution)/shard_map/ppermute | solution.py:757
  37.9 16.0 %collective-permute-start.4 = (f32[3,128,256]{2,1,0:T(8,128)S(1)}, f32[3,128,256]{2,1,0:T(8,128)S(1)}, u32[]{:S(2)}, u32[]{:S(2)}) collective-permute-start(f32[3,128,256]{2,1,0:T(8,128)S(1)} %state_step.12.refs_3_), channel_id=1, source_target_pairs={{4,8},{5,9},{6,10},{7,11},{20,24},{21,25},{22,26},{23,27}} | collective-permute-start | bytes 1179656 | tf_op jit(solution)/shard_map/ppermute | solution.py:557
  38.7 5.5 %collective-permute-start.5 = (f32[2,128,256]{2,1,0:T(8,128)S(1)}, f32[2,128,256]{2,1,0:T(8,128)S(1)}, u32[]{:S(2)}, u32[]{:S(2)}) collective-permute-start(f32[2,128,256]{2,1,0:T(8,128)S(1)} %final_state.5.refs_0_.refs_2_), channel_id=1, source_target_pairs={{8,4},{9,5},{10,6},{11,7},{24,20},{25,21},{26,22},{27,23}} | collective-permute-start | bytes 786440 | tf_op jit(solution)/shard_map/ppermute | solution.py:557
  39.4 15.3 %collective-permute-start.8 = (f32[2,128,256]{2,1,0:T(8,128)S(1)}, f32[2,128,256]{2,1,0:T(8,128)S(1)}, u32[]{:S(2)}, u32[]{:S(2)}) collective-permute-start(f32[2,128,256]{2,1,0:T(8,128)S(1)} %final_state.6.refs_0_.refs_6_), channel_id=1, source_target_pairs={{8,4},{9,5},{10,6},{11,7},{24,20},{25,21},{26,22},{27,23}} | collective-permute-start | bytes 786440 | tf_op jit(solution)/shard_map/ppermute | solution.py:557
  40.1 15.3 %collective-permute-start.12 = (f32[2,1,128,256]{3,2,1,0:T(8,128)S(1)}, f32[2,1,128,256]{3,2,1,0:T(8,128)S(1)}, u32[]{:S(2)}, u32[]{:S(2)}) collective-permute-start(f32[2,1,128,256]{3,2,1,0:T(8,128)S(1)} %pack.8.refs_1_), channel_id=1, source_target_pairs={{0,4},{12,8},{1,5},{13,9},{2,6},{14,10},{3,7},{15,11},{16,20},{28,... | collective-permute-start | bytes 786440 | tf_op jit(solution)/shard_map/ppermute | solution.py:757
  44.3 12.6 %collective-permute-start.7 = (f32[2,128,256]{2,1,0:T(8,128)S(1)}, f32[2,128,256]{2,1,0:T(8,128)S(1)}, u32[]{:S(2)}, u32[]{:S(2)}) collective-permute-start(f32[2,128,256]{2,1,0:T(8,128)S(1)} %part.5.refs_2_), channel_id=1, source_target_pairs={{4,0},{8,12},{5,1},{9,13},{6,2},{10,14},{7,3},{11,15},{20,16},{24,... | collective-permute-start | bytes 786440 | tf_op jit(solution)/shard_map/ppermute | solution.py:612
  45.6 12.1 %collective-permute-start.11 = (f32[2,1,128,256]{3,2,1,0:T(8,128)S(1)}, f32[2,1,128,256]{3,2,1,0:T(8,128)S(1)}, u32[]{:S(2)}, u32[]{:S(2)}) collective-permute-start(f32[2,1,128,256]{3,2,1,0:T(8,128)S(1)} %pack.9.refs_0_), channel_id=1, source_target_pairs={{0,4},{12,8},{1,5},{13,9},{2,6},{14,10},{3,7},{15,11},{16,20},{28,... | collective-permute-start | bytes 786440 | tf_op jit(solution)/shard_map/ppermute | solution.py:757
  53.9 3.8 %collective-permute-start.10 = (f32[2,128,256]{2,1,0:T(8,128)S(1)}, f32[2,128,256]{2,1,0:T(8,128)S(1)}, u32[]{:S(2)}, u32[]{:S(2)}) collective-permute-start(f32[2,128,256]{2,1,0:T(8,128)S(1)} %final_state.7.refs_0_.refs_2_), channel_id=1, source_target_pairs={{8,4},{9,5},{10,6},{11,7},{24,20},{25,21},{26,22},{27,23}} | collective-permute-start | bytes 786440 | tf_op jit(solution)/shard_map/ppermute | solution.py:557
  54.6 2.2 %collective-permute-start.6 = (f32[1,128,256]{2,1,0:T(8,128)S(1)}, f32[1,128,256]{2,1,0:T(8,128)S(1)}, u32[]{:S(2)}, u32[]{:S(2)}) collective-permute-start(f32[1,128,256]{2,1,0:T(8,128)S(1)} %state_step.14.refs_3_), channel_id=1, source_target_pairs={{4,8},{5,9},{6,10},{7,11},{20,24},{21,25},{22,26},{23,27}} | collective-permute-start | bytes 393224 | tf_op jit(solution)/shard_map/ppermute | solution.py:557
  55.4 12.4 %collective-permute-start.9 = (f32[2,128,256]{2,1,0:T(8,128)S(1)}, f32[2,128,256]{2,1,0:T(8,128)S(1)}, u32[]{:S(2)}, u32[]{:S(2)}) collective-permute-start(f32[2,128,256]{2,1,0:T(8,128)S(1)} %part.6.refs_0_), channel_id=1, source_target_pairs={{4,0},{8,12},{5,1},{9,13},{6,2},{10,14},{7,3},{11,15},{20,16},{24,... | collective-permute-start | bytes 786440 | tf_op jit(solution)/shard_map/ppermute | solution.py:612
  56.9 4.2 %collective-permute-start.14 = (f32[1,128,256]{2,1,0:T(8,128)S(1)}, f32[1,128,256]{2,1,0:T(8,128)S(1)}, u32[]{:S(2)}, u32[]{:S(2)}) collective-permute-start(f32[1,128,256]{2,1,0:T(8,128)S(1)} %final_state.8.refs_2_.refs_6_), channel_id=1, source_target_pairs={{8,4},{9,5},{10,6},{11,7},{24,20},{25,21},{26,22},{27,23}} | collective-permute-start | bytes 393224 | tf_op jit(solution)/shard_map/ppermute | solution.py:557
  57.8 15.4 %collective-permute-start.13 = (f32[2,128,256]{2,1,0:T(8,128)S(1)}, f32[2,128,256]{2,1,0:T(8,128)S(1)}, u32[]{:S(2)}, u32[]{:S(2)}) collective-permute-start(f32[2,128,256]{2,1,0:T(8,128)S(1)} %part.8.refs_0_), channel_id=1, source_target_pairs={{4,0},{8,12},{5,1},{9,13},{6,2},{10,14},{7,3},{11,15},{20,16},{24,... | collective-permute-start | bytes 786440 | tf_op jit(solution)/shard_map/ppermute | solution.py:612
  59.1 14.0 %collective-permute-start.17 = (f32[1,128,256]{2,1,0:T(8,128)S(1)}, f32[1,128,256]{2,1,0:T(8,128)S(1)}, u32[]{:S(2)}, u32[]{:S(2)}) collective-permute-start(f32[1,128,256]{2,1,0:T(8,128)S(1)} %final_state.9.refs_0_.refs_10_), channel_id=1, source_target_pairs={{8,0},{9,1},{10,2},{11,3},{24,16},{25,17},{26,18},{27,19}} | collective-permute-start | bytes 393224 | tf_op jit(solution)/shard_map/ppermute | solution.py:557
  60.4 12.8 %collective-permute-start.18 = (f32[1,128,256]{2,1,0:T(8,128)S(1)}, f32[1,128,256]{2,1,0:T(8,128)S(1)}, u32[]{:S(2)}, u32[]{:S(2)}) collective-permute-start(f32[1,128,256]{2,1,0:T(8,128)S(1)} %final_state.9.refs_0_.refs_10_), channel_id=1, source_target_pairs={{8,4},{9,5},{10,6},{11,7},{24,20},{25,21},{26,22},{27,23}} | collective-permute-start | bytes 393224 | tf_op jit(solution)/shard_map/ppermute | solution.py:557
  61.1 12.4 %collective-permute-start.15 = (f32[1,128,256]{2,1,0:T(8,128)S(1)}, f32[1,128,256]{2,1,0:T(8,128)S(1)}, u32[]{:S(2)}, u32[]{:S(2)}) collective-permute-start(f32[1,128,256]{2,1,0:T(8,128)S(1)} %part.9.refs_0_), channel_id=1, source_target_pairs={{4,0},{8,12},{5,1},{9,13},{6,2},{10,14},{7,3},{11,15},{20,16},{24,... | collective-permute-start | bytes 393224 | tf_op jit(solution)/shard_map/ppermute | solution.py:612
  67.8 5.7 %collective-permute-start.16 = (f32[1,128,256]{2,1,0:T(8,128)S(1)}, f32[1,128,256]{2,1,0:T(8,128)S(1)}, u32[]{:S(2)}, u32[]{:S(2)}) collective-permute-start(f32[1,128,256]{2,1,0:T(8,128)S(1)} %part.7.refs_0_), channel_id=1, source_target_pairs={{8,12},{9,13},{10,14},{11,15},{24,28},{25,29},{26,30},{27,31}} | collective-permute-start | bytes 393224 | tf_op jit(solution)/shard_map/ppermute | solution.py:557
  73.1 2.3 %collective-permute-start.20 = (f32[4,128,256]{2,1,0:T(8,128)S(1)}, f32[4,128,256]{2,1,0:T(8,128)S(1)}, u32[]{:S(2)}, u32[]{:S(2)}) collective-permute-start(f32[4,128,256]{2,1,0:T(8,128)S(1)} %settle.2.refs_2_.refs_1_), channel_id=1, source_target_pairs={{0,1},{1,0},{2,3},{3,2},{4,5},{5,4},{6,7},{7,6},{8,9},{9,8},{10,11... | collective-permute-start | bytes 1572872 | tf_op jit(solution)/shard_map/ppermute | solution.py:640
  73.2 0.7 copy-start.6
  73.6 3.8 %collective-permute-start.19 = (f32[4,128,256]{2,1,0:T(8,128)S(1)}, f32[4,128,256]{2,1,0:T(8,128)S(1)}, u32[]{:S(2)}, u32[]{:S(2)}) collective-permute-start(f32[4,128,256]{2,1,0:T(8,128)S(1)} %settle.3.refs_16_.refs_1_), channel_id=1, source_target_pairs={{0,1},{1,0},{2,3},{3,2},{4,5},{5,4},{6,7},{7,6},{8,9},{9,8},{10,11... | collective-permute-start | bytes 1572872 | tf_op jit(solution)/shard_map/ppermute | solution.py:640

commit v5 on v4

--- a/solution.py
+++ b/solution.py
@@ -528,21 +528,42 @@
         out_ref[0, :, p * W2 : (p + 1) * W2] = low16(out)
 
 
-def prompt_outputs(arrived, terms, gain, width, after=()):
+def first_out_kernel(calls, hops, count, sizes, *refs):
+    prompt_ref, suffix_ref, state_ref = refs[-3:]
+
+    @pl.when(pl.program_id(0) == 0)
+    def _():
+        prompt_out_kernel(calls, hops, *refs[:count], prompt_ref, state_ref)
+
+    stop = count + 4 + 2 * len(sizes)
+    suffix_out_kernel(sizes, *refs[count:stop], suffix_ref)
+
+
+def first_outputs(arrived, terms, rows, own, other, made, gain, width, after):
     pairs = width // W2
+    slots, tokens, _ = made[0][0].shape
     calls = [a.shape[1] // W2 for a, b in terms]
     hops = [[size for x, size in hop] for hop in arrived]
+    sizes = [a.shape[2] // W2 for a, b in made]
     args = [x for hop in arrived for x, size in hop] + [x for pair in terms for x in pair] + [gain]
+    count = len(args)
+    args += [rows, own, other, gain] + [x for pair in made for x in pair]
     return pl.pallas_call(
-        functools.partial(prompt_out_kernel, calls, hops),
-        grid=(1,),
+        functools.partial(first_out_kernel, calls, hops, count, sizes),
+        grid=(slots,),
         in_specs=[WHOLE] * len(args) + [ANY] * len(after),
-        out_specs=pl.BlockSpec((1, CH, width), lambda i: (0, 0, 0)),
-        out_shape=pltpu.HBM((1, CH, width), jnp.bfloat16),
+        out_specs=[
+            pl.BlockSpec((1, CH, width), lambda i: (0, 0, 0)),
+            pl.BlockSpec((1, tokens, sum(sizes) * W2), lambda i: (i, 0, 0)),
+        ],
+        out_shape=[
+            pltpu.HBM((1, CH, width), jnp.bfloat16),
+            pltpu.HBM((slots, tokens, width), jnp.bfloat16),
+        ],
         scratch_shapes=[pltpu.VMEM((pairs, DK, W2), jnp.float32)],
         compiler_params=pltpu.CompilerParams(vmem_limit_bytes=SCOPED),
         cost_estimate=SHORT,
-        name="prompt_out",
+        name="first_out",
     )(*[near(value) for value in args], *after)
 
 
@@ -677,7 +698,6 @@
     ("end", 4),
     ("settle", 1),
     ("prompt", 0),
-    ("out", 0),
     ("out", 1),
 )
 
@@ -692,7 +712,7 @@
     order += [("make", k) for k in range(makes)]
     order += [("end", k) for k in range(runs)]
     order += [("settle", k) for k in range(groups)] + [("prompt", 0)]
-    return order + [("out", k) for k in range(groups)]
+    return order + [("out", k) for k in range(1, groups)]
 
 
 def local(
@@ -810,7 +830,10 @@
                 came.append([(f.arrived[j], f.size) for f in forwards])
             if half == 2:
                 came.append([(back.right, back.size) for back in backwards])
-            prompt_out = prompt_outputs(came, terms, gain, width, last)
+            done = groups[0][1]
+            prompt_out, suffix_out = first_outputs(
+                came, terms, rows, *settled[0], made[:done], gain, width, last
+            )
             last = (away(prompt_out),)
     return (prompt_out, suffix_out)
 

time: 80.3 us -> 80.3 us (level)
  waiting for transfers between devices: 6.07 us -> 7.22 us
    pallas_call x2 -> x1, Pallas kernels: 4.13 us -> 2.04 us  [suffix_outputs(): pl.pallas_call(functools.partial(suffix_out_kernel, sizes), grid=(slots,)...]
    pallas_call x1, Pallas kernels: 1.43 us -> 2.68 us  [first_outputs(): pl.pallas_call(functools.partial(first_out_kernel, calls, hops, count, si...]
    ppermute x2, waiting for transfers between devices: 0.01 us -> 1.16 us  [settle_runs(): lax.ppermute(final, 'prompt', [(i, (i + 1) % prompts) for i in range(prom...]
  transfers between devices with their start and end apart: 21 -> 21, of which waited for: 4 -> 5; matrix products, arithmetic and copies ran while one was open for 0% -> 0% of each run, Pallas kernels for 33% -> 32%
where the time goes in v5:
time: 80.3 us; the launch traced here: 79.8 us
  starting transfers between devices  38.4 us (48%)
  Pallas kernels  31.6 us (39%)
  waiting for transfers between devices  7.22 us (9%)
  local copies, waits for them, and re-layouts  1.27 us (2%)
  between operations  1.27 us (2%)
    ppermute x5, starting transfers between devices, local(): lax.ppermute(out, 'seq', [(0, 1), (2 * half - 1, 2 * half - 2)])  25.3 us
    pallas_call x4, Pallas kernels, suffix_terms(): pl.pallas_call(functools.partial(suffix_kernel, first, unit), in_specs=[W...  17.2 us
    pallas_call x2, Pallas kernels, prompt_terms(): pl.pallas_call(functools.partial(prompt_kernel, first, sizes, wide, len(q...  8.49 us
    ppermute x10, starting transfers between devices, send(): return lax.ppermute(value, 'seq', [(source, target)])  7.58 us
    ppermute x4, waiting for transfers between devices, pass_on(): self.right = lax.ppermute(out, 'seq', [(1, 0), (2, 3)])  5.89 us
    ppermute x4, starting transfers between devices, pass_on(): self.right = lax.ppermute(out, 'seq', [(1, 0), (2, 3)])  5.17 us
    pallas_call x1, Pallas kernels, first_outputs(): pl.pallas_call(functools.partial(first_out_kernel, calls, hops, count, si...  2.68 us
    pallas_call x1, Pallas kernels, suffix_outputs(): pl.pallas_call(functools.partial(suffix_out_kernel, sizes), grid=(slots,)...  2.04 us
  transfers between devices with their start and end apart: 21, of which 5 were waited for; matrix products, arithmetic and copies ran while one was open for 0% of the time, Pallas kernels for 32%

profile of v5, /device:TPU:0, one launch (start us, length us, event | category | flops | bytes accessed | tf_op | source)
XLA Modules:
  0.0 79.8 jit_solution(14688645378994214608)
XLA Ops:
  0.7 4.3 %prompt_terms.2 = (f32[2,2,128,256]{3,2,1,0:T(8,128)S(1)}, f32[2,2,128,256]{3,2,1,0:T(8,128)S(1)}, bf16[128,1024]{1,0:T(8,128)(2,1)S(1)}, bf16[128,1024]{1,0:T(8,128)(2,1)S(1)}) custom-call(bf16[1,128,1024]{2,1,0:T(8,128)(2,1)} %refs_0_.3, bf16[1,128,1024]{2,1,0:T(8,128)(2,1)} %refs_1_.3, bf16[1,128,2048]{2,1,0:T(8,128)(2,1)} %refs_2_.3, ...), custom_call_target="tpu_custom_call" | custom-call | flops 1 | bytes 1 | tf_op jit(solution)/shard_map/prompt_terms/pallas_call | solution.py:238
  5.0 0.1 pack.5.refs_0_
  5.1 5.0 %collective-permute-start = (f32[2,2,128,256]{3,2,1,0:T(8,128)S(1)}, f32[2,2,128,256]{3,2,1,0:T(8,128)S(1)}, u32[]{:S(2)}, u32[]{:S(2)}) collective-permute-start(f32[2,2,128,256]{3,2,1,0:T(8,128)S(1)} %pack.5.refs_0_), channel_id=1, source_target_pairs={{0,4},{12,8},{1,5},{13,9},{2,6},{14,10},{3,7},{15,11},{16,20},{28,... | collective-permute-start | bytes 1572872 | tf_op jit(solution)/shard_map/ppermute | solution.py:777
  10.1 0.0 copy-start.2
  10.1 1.2 %copy-done.2 = bf16[2,256,1024]{2,1,0:T(8,128)(2,1)S(1)} copy-done((bf16[2,256,1024]{2,1,0:T(8,128)(2,1)S(1)}, bf16[2,256,1024]{2,1,0:T(8,128)(2,1)}, u32[]{:S(2)}) %copy-start.2) | copy-done | bytes 1048600
  11.3 4.3 %suffix_terms.4 = (bf16[2,256,512]{2,1,0:T(8,128)(2,1)S(1)}, bf16[2,256,512]{2,1,0:T(8,128)(2,1)S(1)}) custom-call(bf16[2,256,1024]{2,1,0:T(8,128)(2,1)S(1)} %copy-done.1, bf16[2,256,1024]{2,1,0:T(8,128)(2,1)S(1)} %copy-done.2, bf16[2,256,2048]{2,1,0:T(8,128)(2,1)S(1)} %copy-done, f32[2,16,256]{2,1,0:T(8,128)S(1)} %copy-done.4, f32[2,16,256]{2,1,0:T(8,128)S(1)} %copy-done.5, ...), custom_call_target="tpu_custom_call" | custom-call | flops 1 | bytes 1 | tf_op jit(solution)/shard_map/suffix_terms/pallas_call | solution.py:293
  15.6 4.2 %prompt_terms.3 = (f32[2,2,128,256]{3,2,1,0:T(8,128)S(1)}, f32[2,1,128,256]{3,2,1,0:T(8,128)S(1)}, f32[2,1,128,256]{3,2,1,0:T(8,128)S(1)}, bf16[128,1024]{1,0:T(8,128)(2,1)S(1)}, bf16[128,1024]{1,0:T(8,128)(2,1)S(1)}) custom-call(bf16[1,128,1024]{2,1,0:T(8,128)(2,1)} %refs_0_.3, bf16[1,128,1024]{2,1,0:T(8,128)(2,1)} %refs_1_.3, ...), custom_call_target="tpu_custom_call" | custom-call | flops 1 | bytes 1 | tf_op jit(solution)/shard_map/prompt_terms/pallas_call | solution.py:238
  19.8 0.0 copy-start.7
  19.8 0.0 copy-start.8
  19.9 0.0 copy-start.9
  19.9 1.5 %collective-permute-start.1 = (f32[2,2,128,256]{3,2,1,0:T(8,128)S(1)}, f32[2,2,128,256]{3,2,1,0:T(8,128)S(1)}, u32[]{:S(2)}, u32[]{:S(2)}) collective-permute-start(f32[2,2,128,256]{3,2,1,0:T(8,128)S(1)} %pack.6.refs_2_), channel_id=1, source_target_pairs={{0,4},{12,8},{1,5},{13,9},{2,6},{14,10},{3,7},{15,11},{16,20},{28,... | collective-permute-start | bytes 1572872 | tf_op jit(solution)/shard_map/ppermute | solution.py:777
  21.4 0.0 copy-start.3
  21.4 0.0 copy-done.7
  21.4 0.0 copy-done.8
  21.4 0.0 copy-done.9
  21.5 0.6 slot_rows.1.refs_3_.refs_16_.refs_0_
  22.0 0.0 collective-permute-done.refs_2_.far_ref.refs_0_
  22.1 0.7 collective-permute-start.3
  22.8 6.5 %collective-permute-start.2 = (f32[2,2,128,256]{3,2,1,0:T(8,128)S(1)}, f32[2,2,128,256]{3,2,1,0:T(8,128)S(1)}, u32[]{:S(2)}, u32[]{:S(2)}) collective-permute-start(f32[2,2,128,256]{3,2,1,0:T(8,128)S(1)} %pack.7.refs_1_), channel_id=1, source_target_pairs={{0,4},{12,8},{1,5},{13,9},{2,6},{14,10},{3,7},{15,11},{16,20},{28,... | collective-permute-start | bytes 1572872 | tf_op jit(solution)/shard_map/ppermute | solution.py:777
  29.3 4.3 %suffix_terms.5 = (bf16[2,256,512]{2,1,0:T(8,128)(2,1)S(1)}, bf16[2,256,512]{2,1,0:T(8,128)(2,1)S(1)}) custom-call(bf16[2,256,1024]{2,1,0:T(8,128)(2,1)S(1)} %copy-done.1, bf16[2,256,1024]{2,1,0:T(8,128)(2,1)S(1)} %copy-done.3, bf16[2,256,2048]{2,1,0:T(8,128)(2,1)S(1)} %copy-done, f32[2,16,256]{2,1,0:T(8,128)S(1)} %copy-done.4, f32[2,16,256]{2,1,0:T(8,128)S(1)} %copy-done.5, ...), custom_call_target="tpu_custom_call" | custom-call | flops 1 | bytes 1 | tf_op jit(solution)/shard_map/suffix_terms/pallas_call | solution.py:293
  33.6 4.3 %suffix_terms.6 = (bf16[2,256,512]{2,1,0:T(8,128)(2,1)S(1)}, bf16[2,256,512]{2,1,0:T(8,128)(2,1)S(1)}) custom-call(bf16[2,256,1024]{2,1,0:T(8,128)(2,1)S(1)} %copy-done.1, bf16[2,256,1024]{2,1,0:T(8,128)(2,1)S(1)} %copy-done.3, bf16[2,256,2048]{2,1,0:T(8,128)(2,1)S(1)} %copy-done, f32[2,16,256]{2,1,0:T(8,128)S(1)} %copy-done.4, f32[2,16,256]{2,1,0:T(8,128)S(1)} %copy-done.5, ...), custom_call_target="tpu_custom_call" | custom-call | flops 1 | bytes 1 | tf_op jit(solution)/shard_map/suffix_terms/pallas_call | solution.py:293
  37.9 0.0 collective-permute-done.1.refs_2_.far_ref.refs_1_
  37.9 0.7 collective-permute-start.4
  38.6 0.0 collective-permute-done.3.refs_2_.refs_3_
  38.7 0.7 collective-permute-start.5
  39.4 0.7 collective-permute-start.8
  40.1 4.1 %collective-permute-start.12 = (f32[2,1,128,256]{3,2,1,0:T(8,128)S(1)}, f32[2,1,128,256]{3,2,1,0:T(8,128)S(1)}, u32[]{:S(2)}, u32[]{:S(2)}) collective-permute-start(f32[2,1,128,256]{3,2,1,0:T(8,128)S(1)} %pack.8.refs_1_), channel_id=1, source_target_pairs={{0,4},{12,8},{1,5},{13,9},{2,6},{14,10},{3,7},{15,11},{16,20},{28,... | collective-permute-start | bytes 786440 | tf_op jit(solution)/shard_map/ppermute | solution.py:777
  44.2 0.0 collective-permute-done.5.left_ref.refs_1_
  44.3 1.3 %collective-permute-start.7 = (f32[2,128,256]{2,1,0:T(8,128)S(1)}, f32[2,128,256]{2,1,0:T(8,128)S(1)}, u32[]{:S(2)}, u32[]{:S(2)}) collective-permute-start(f32[2,128,256]{2,1,0:T(8,128)S(1)} %part.5.refs_2_), channel_id=1, source_target_pairs={{4,0},{8,12},{5,1},{9,13},{6,2},{10,14},{7,3},{11,15},{20,16},{24,... | collective-permute-start | bytes 786440 | tf_op jit(solution)/shard_map/ppermute | solution.py:633
  45.6 0.0 collective-permute-done.2.refs_1_.far_ref.refs_2_
  45.6 8.2 %collective-permute-start.11 = (f32[2,1,128,256]{3,2,1,0:T(8,128)S(1)}, f32[2,1,128,256]{3,2,1,0:T(8,128)S(1)}, u32[]{:S(2)}, u32[]{:S(2)}) collective-permute-start(f32[2,1,128,256]{3,2,1,0:T(8,128)S(1)} %pack.9.refs_0_), channel_id=1, source_target_pairs={{0,4},{12,8},{1,5},{13,9},{2,6},{14,10},{3,7},{15,11},{16,20},{28,... | collective-permute-start | bytes 786440 | tf_op jit(solution)/shard_map/ppermute | solution.py:777
  53.9 0.0 collective-permute-done.4.refs_2_.refs_4_
  53.9 0.7 collective-permute-start.10
  54.6 0.0 collective-permute-done.8.left_ref.refs_5_
  54.6 0.7 collective-permute-start.6
  55.3 0.0 collective-permute-done.12.far_ref
  55.3 1.3 %collective-permute-start.9 = (f32[2,128,256]{2,1,0:T(8,128)S(1)}, f32[2,128,256]{2,1,0:T(8,128)S(1)}, u32[]{:S(2)}, u32[]{:S(2)}) collective-permute-start(f32[2,128,256]{2,1,0:T(8,128)S(1)} %part.6.refs_0_), channel_id=1, source_target_pairs={{4,0},{8,12},{5,1},{9,13},{6,2},{10,14},{7,3},{11,15},{20,16},{24,... | collective-permute-start | bytes 786440 | tf_op jit(solution)/shard_map/ppermute | solution.py:633
  56.7 0.2 collective-permute-done.7.refs_1_.refs_0_.refs_6_
  56.9 0.0 collective-permute-done.6.refs_1_.refs_5_
  56.9 0.7 collective-permute-start.14
  57.6 0.1 collective-permute-done.11.far_ref
  57.7 0.0 collective-permute-done.10.left_ref.refs_1_
  57.7 1.3 %collective-permute-start.13 = (f32[2,128,256]{2,1,0:T(8,128)S(1)}, f32[2,128,256]{2,1,0:T(8,128)S(1)}, u32[]{:S(2)}, u32[]{:S(2)}) collective-permute-start(f32[2,128,256]{2,1,0:T(8,128)S(1)} %part.8.refs_0_), channel_id=1, source_target_pairs={{4,0},{8,12},{5,1},{9,13},{6,2},{10,14},{7,3},{11,15},{20,16},{24,... | collective-permute-start | bytes 786440 | tf_op jit(solution)/shard_map/ppermute | solution.py:633
  59.0 1.3 %collective-permute-start.18 = (f32[1,128,256]{2,1,0:T(8,128)S(1)}, f32[1,128,256]{2,1,0:T(8,128)S(1)}, u32[]{:S(2)}, u32[]{:S(2)}) collective-permute-start(f32[1,128,256]{2,1,0:T(8,128)S(1)} %final_state.9.refs_0_.refs_10_), channel_id=1, source_target_pairs={{8,0},{9,1},{10,2},{11,3},{24,16},{25,17},{26,18},{27,19}} | collective-permute-start | bytes 393224 | tf_op jit(solution)/shard_map/ppermute | solution.py:578
  60.3 0.7 collective-permute-start.19
  61.0 0.0 collective-permute-done.14.left_ref.refs_5_
  61.0 1.3 %collective-permute-start.15 = (f32[1,128,256]{2,1,0:T(8,128)S(1)}, f32[1,128,256]{2,1,0:T(8,128)S(1)}, u32[]{:S(2)}, u32[]{:S(2)}) collective-permute-start(f32[1,128,256]{2,1,0:T(8,128)S(1)} %part.9.refs_0_), channel_id=1, source_target_pairs={{4,0},{8,12},{5,1},{9,13},{6,2},{10,14},{7,3},{11,15},{20,16},{24,... | collective-permute-start | bytes 393224 | tf_op jit(solution)/shard_map/ppermute | solution.py:633
  62.3 5.4 %collective-permute-done.9.refs_1_.refs_4_.refs_7_ = f32[2,128,256]{2,1,0:T(8,128)S(1)} collective-permute-done((f32[2,128,256]{2,1,0:T(8,128)S(1)}, f32[2,128,256]{2,1,0:T(8,128)S(1)}, u32[]{:S(2)}, u32[]{:S(2)}) %collective-permute-start.9) | collective-permute-done | bytes 262176 | tf_op jit(solution)/shard_map/ppermute | solution.py:633
  67.8 0.9 %collective-permute-start.16 = (f32[1,128,256]{2,1,0:T(8,128)S(1)}, f32[1,128,256]{2,1,0:T(8,128)S(1)}, u32[]{:S(2)}, u32[]{:S(2)}) collective-permute-start(f32[1,128,256]{2,1,0:T(8,128)S(1)} %part.7.refs_0_), channel_id=1, source_target_pairs={{8,12},{9,13},{10,14},{11,15},{24,28},{25,29},{26,30},{27,31}} | collective-permute-start | bytes 393224 | tf_op jit(solution)/shard_map/ppermute | solution.py:578
  68.6 4.3 %suffix_terms.7 = (bf16[2,256,512]{2,1,0:T(8,128)(2,1)S(1)}, bf16[2,256,512]{2,1,0:T(8,128)(2,1)S(1)}) custom-call(bf16[2,256,1024]{2,1,0:T(8,128)(2,1)S(1)} %copy-done.1, bf16[2,256,1024]{2,1,0:T(8,128)(2,1)S(1)} %copy-done.3, bf16[2,256,2048]{2,1,0:T(8,128)(2,1)S(1)} %copy-done, f32[2,16,256]{2,1,0:T(8,128)S(1)} %copy-done.4, f32[2,16,256]{2,1,0:T(8,128)S(1)} %copy-done.5, ...), custom_call_target="tpu_custom_call" | custom-call | flops 1 | bytes 1 | tf_op jit(solution)/shard_map/suffix_terms/pallas_call | solution.py:293
  73.0 0.1 settle.2.refs_2_.refs_17_
  73.0 0.0 collective-permute-done.18.refs_3_.refs_8_
  73.0 0.1 collective-permute-start.17
  73.1 0.0 collective-permute-done.19.refs_4_.refs_9_
  73.1 0.0 collective-permute-done.13.refs_1_.refs_0_.refs_8_
  73.2 0.0 copy-start.6
  73.2 0.3 collective-permute-done.15.refs_1_.refs_4_.refs_9_
  73.5 0.0 collective-permute-done.16.refs_1_.refs_10_
  73.5 0.1 settle.3.refs_24_.refs_1_
  73.6 0.3 collective-permute-start.20
  73.9 1.2 %collective-permute-done.17.refs_18_ = f32[4,128,256]{2,1,0:T(8,128)S(1)} collective-permute-done((f32[4,128,256]{2,1,0:T(8,128)S(1)}, f32[4,128,256]{2,1,0:T(8,128)S(1)}, u32[]{:S(2)}, u32[]{:S(2)}) %collective-permute-start.17) | collective-permute-done | bytes 524320 | tf_op jit(solution)/shard_map/ppermute | solution.py:661
  75.0 2.7 %first_out.1 = (bf16[1,128,2048]{2,1,0:T(8,128)(2,1)}, bf16[2,256,2048]{2,1,0:T(8,128)(2,1)}) custom-call(f32[2,2,128,256]{3,2,1,0:T(8,128)S(1)} %collective-permute-done.refs_2_.far_ref.refs_0_, f32[2,2,128,256]{3,2,1,0:T(8,128)S(1)} %collective-permute-done.1.refs_2_.far_ref.refs_1_, f32[2,2,128,256]{3,2,1,0:T(8,128)S(1)} %collective-permute-done.2.refs_1_.far_ref.refs_2_, ...), custom_call_target="tpu_custom_call" | custom-call | flops 1 | bytes 1 | tf_op jit(solution)/shard_map/first_out/pallas_call | solution.py:551
  77.7 0.0 collective-permute-done.20.refs_2_
  77.7 2.0 %suffix_out.1 = bf16[2,256,2048]{2,1,0:T(8,128)(2,1)} custom-call(s32[2,16,256]{2,1,0:T(8,128)S(1)} %slot_rows.1.refs_3_.refs_16_.refs_0_, f32[4,128,256]{2,1,0:T(8,128)S(1)} %settle.3.refs_24_.refs_1_, f32[4,128,256]{2,1,0:T(8,128)S(1)} %collective-permute-done.20.refs_2_, f32[1,128]{1,0:T(1,128)S(1)} %bitcast.3, ...), custom_call_target="tpu_custom_call", output_to_operand_aliasing={{}: (8, {})} | custom-call | flops 1 | bytes 1 | tf_op jit(solution)/shard_map/suffix_out/pallas_call | solution.py:497
  (35 shorter events, 0.4 us)
Async XLA Ops:
  0.6 9.4 %copy-start.1 = (bf16[2,256,1024]{2,1,0:T(8,128)(2,1)S(1)}, bf16[2,256,1024]{2,1,0:T(8,128)(2,1)}, u32[]{:S(2)}) copy-start(bf16[2,256,1024]{2,1,0:T(8,128)(2,1)} %q_ref.7) | copy-start | bytes 3145732
  0.6 9.4 %copy-start = (bf16[2,256,2048]{2,1,0:T(8,128)(2,1)S(1)}, bf16[2,256,2048]{2,1,0:T(8,128)(2,1)}, u32[]{:S(2)}) copy-start(bf16[2,256,2048]{2,1,0:T(8,128)(2,1)} %v_ref.7) | copy-start | bytes 6291460
  0.7 9.4 %copy-start.4 = (f32[2,16,256]{2,1,0:T(8,128)S(1)}, f32[2,16,256]{2,1,0:T(8,128)}, u32[]{:S(2)}) copy-start(f32[2,16,256]{2,1,0:T(8,128)} %beta_ref.7) | copy-start | bytes 98308
  0.7 9.4 %copy-start.5 = (f32[2,16,256]{2,1,0:T(8,128)S(1)}, f32[2,16,256]{2,1,0:T(8,128)}, u32[]{:S(2)}) copy-start(f32[2,16,256]{2,1,0:T(8,128)} %decay_ref.7) | copy-start | bytes 98308
  5.1 17.0 %collective-permute-start = (f32[2,2,128,256]{3,2,1,0:T(8,128)S(1)}, f32[2,2,128,256]{3,2,1,0:T(8,128)S(1)}, u32[]{:S(2)}, u32[]{:S(2)}) collective-permute-start(f32[2,2,128,256]{3,2,1,0:T(8,128)S(1)} %pack.5.refs_0_), channel_id=1, source_target_pairs={{0,4},{12,8},{1,5},{13,9},{2,6},{14,10},{3,7},{15,11},{16,20},{28,... | collective-permute-start | bytes 1572872 | tf_op jit(solution)/shard_map/ppermute | solution.py:777
  10.1 1.2 %copy-start.2 = (bf16[2,256,1024]{2,1,0:T(8,128)(2,1)S(1)}, bf16[2,256,1024]{2,1,0:T(8,128)(2,1)}, u32[]{:S(2)}) copy-start(bf16[2,256,1024]{2,1,0:T(8,128)(2,1)} %k_ref.7) | copy-start | bytes 3145732
  19.8 1.6 %copy-start.7 = (s32[16]{0:T(128)S(1)}, s32[16]{0:T(128)}, u32[]{:S(2)}) copy-start(s32[16]{0:T(128)} %sb_ref.1) | copy-start | bytes 196
  19.8 1.6 %copy-start.8 = (s32[16]{0:T(128)S(1)}, s32[16]{0:T(128)}, u32[]{:S(2)}) copy-start(s32[16]{0:T(128)} %bl_ref.1) | copy-start | bytes 196
  19.9 1.6 %copy-start.9 = (s32[16]{0:T(128)S(1)}, s32[16]{0:T(128)}, u32[]{:S(2)}) copy-start(s32[16]{0:T(128)} %bp_ref.1) | copy-start | bytes 196
  19.9 18.0 %collective-permute-start.1 = (f32[2,2,128,256]{3,2,1,0:T(8,128)S(1)}, f32[2,2,128,256]{3,2,1,0:T(8,128)S(1)}, u32[]{:S(2)}, u32[]{:S(2)}) collective-permute-start(f32[2,2,128,256]{3,2,1,0:T(8,128)S(1)} %pack.6.refs_2_), channel_id=1, source_target_pairs={{0,4},{12,8},{1,5},{13,9},{2,6},{14,10},{3,7},{15,11},{16,20},{28,... | collective-permute-start | bytes 1572872 | tf_op jit(solution)/shard_map/ppermute | solution.py:777
  21.4 7.9 %copy-start.3 = (bf16[2,256,1024]{2,1,0:T(8,128)(2,1)S(1)}, bf16[2,256,1024]{2,1,0:T(8,128)(2,1)}, u32[]{:S(2)}) copy-start(bf16[2,256,1024]{2,1,0:T(8,128)(2,1)} %k_ref.7) | copy-start | bytes 3145732
  22.1 16.5 %collective-permute-start.3 = (f32[4,128,256]{2,1,0:T(8,128)S(1)}, f32[4,128,256]{2,1,0:T(8,128)S(1)}, u32[]{:S(2)}, u32[]{:S(2)}) collective-permute-start(f32[4,128,256]{2,1,0:T(8,128)S(1)} %state_step.11.refs_0_), channel_id=1, source_target_pairs={{4,8},{5,9},{6,10},{7,11},{20,24},{21,25},{22,26},{23,27}} | collective-permute-start | bytes 1572872 | tf_op jit(solution)/shard_map/ppermute | solution.py:578
  22.8 22.8 %collective-permute-start.2 = (f32[2,2,128,256]{3,2,1,0:T(8,128)S(1)}, f32[2,2,128,256]{3,2,1,0:T(8,128)S(1)}, u32[]{:S(2)}, u32[]{:S(2)}) collective-permute-start(f32[2,2,128,256]{3,2,1,0:T(8,128)S(1)} %pack.7.refs_1_), channel_id=1, source_target_pairs={{0,4},{12,8},{1,5},{13,9},{2,6},{14,10},{3,7},{15,11},{16,20},{28,... | collective-permute-start | bytes 1572872 | tf_op jit(solution)/shard_map/ppermute | solution.py:777
  37.9 15.9 %collective-permute-start.4 = (f32[3,128,256]{2,1,0:T(8,128)S(1)}, f32[3,128,256]{2,1,0:T(8,128)S(1)}, u32[]{:S(2)}, u32[]{:S(2)}) collective-permute-start(f32[3,128,256]{2,1,0:T(8,128)S(1)} %state_step.12.refs_3_), channel_id=1, source_target_pairs={{4,8},{5,9},{6,10},{7,11},{20,24},{21,25},{22,26},{23,27}} | collective-permute-start | bytes 1179656 | tf_op jit(solution)/shard_map/ppermute | solution.py:578
  38.7 5.6 %collective-permute-start.5 = (f32[2,128,256]{2,1,0:T(8,128)S(1)}, f32[2,128,256]{2,1,0:T(8,128)S(1)}, u32[]{:S(2)}, u32[]{:S(2)}) collective-permute-start(f32[2,128,256]{2,1,0:T(8,128)S(1)} %final_state.5.refs_0_.refs_2_), channel_id=1, source_target_pairs={{8,4},{9,5},{10,6},{11,7},{24,20},{25,21},{26,22},{27,23}} | collective-permute-start | bytes 786440 | tf_op jit(solution)/shard_map/ppermute | solution.py:578
  39.4 15.2 %collective-permute-start.8 = (f32[2,128,256]{2,1,0:T(8,128)S(1)}, f32[2,128,256]{2,1,0:T(8,128)S(1)}, u32[]{:S(2)}, u32[]{:S(2)}) collective-permute-start(f32[2,128,256]{2,1,0:T(8,128)S(1)} %final_state.6.refs_0_.refs_6_), channel_id=1, source_target_pairs={{8,4},{9,5},{10,6},{11,7},{24,20},{25,21},{26,22},{27,23}} | collective-permute-start | bytes 786440 | tf_op jit(solution)/shard_map/ppermute | solution.py:578
  40.1 15.3 %collective-permute-start.12 = (f32[2,1,128,256]{3,2,1,0:T(8,128)S(1)}, f32[2,1,128,256]{3,2,1,0:T(8,128)S(1)}, u32[]{:S(2)}, u32[]{:S(2)}) collective-permute-start(f32[2,1,128,256]{3,2,1,0:T(8,128)S(1)} %pack.8.refs_1_), channel_id=1, source_target_pairs={{0,4},{12,8},{1,5},{13,9},{2,6},{14,10},{3,7},{15,11},{16,20},{28,... | collective-permute-start | bytes 786440 | tf_op jit(solution)/shard_map/ppermute | solution.py:777
  44.3 12.6 %collective-permute-start.7 = (f32[2,128,256]{2,1,0:T(8,128)S(1)}, f32[2,128,256]{2,1,0:T(8,128)S(1)}, u32[]{:S(2)}, u32[]{:S(2)}) collective-permute-start(f32[2,128,256]{2,1,0:T(8,128)S(1)} %part.5.refs_2_), channel_id=1, source_target_pairs={{4,0},{8,12},{5,1},{9,13},{6,2},{10,14},{7,3},{11,15},{20,16},{24,... | collective-permute-start | bytes 786440 | tf_op jit(solution)/shard_map/ppermute | solution.py:633
  45.6 12.1 %collective-permute-start.11 = (f32[2,1,128,256]{3,2,1,0:T(8,128)S(1)}, f32[2,1,128,256]{3,2,1,0:T(8,128)S(1)}, u32[]{:S(2)}, u32[]{:S(2)}) collective-permute-start(f32[2,1,128,256]{3,2,1,0:T(8,128)S(1)} %pack.9.refs_0_), channel_id=1, source_target_pairs={{0,4},{12,8},{1,5},{13,9},{2,6},{14,10},{3,7},{15,11},{16,20},{28,... | collective-permute-start | bytes 786440 | tf_op jit(solution)/shard_map/ppermute | solution.py:777
  53.9 3.8 %collective-permute-start.10 = (f32[2,128,256]{2,1,0:T(8,128)S(1)}, f32[2,128,256]{2,1,0:T(8,128)S(1)}, u32[]{:S(2)}, u32[]{:S(2)}) collective-permute-start(f32[2,128,256]{2,1,0:T(8,128)S(1)} %final_state.7.refs_0_.refs_2_), channel_id=1, source_target_pairs={{8,4},{9,5},{10,6},{11,7},{24,20},{25,21},{26,22},{27,23}} | collective-permute-start | bytes 786440 | tf_op jit(solution)/shard_map/ppermute | solution.py:578
  54.6 2.2 %collective-permute-start.6 = (f32[1,128,256]{2,1,0:T(8,128)S(1)}, f32[1,128,256]{2,1,0:T(8,128)S(1)}, u32[]{:S(2)}, u32[]{:S(2)}) collective-permute-start(f32[1,128,256]{2,1,0:T(8,128)S(1)} %state_step.14.refs_3_), channel_id=1, source_target_pairs={{4,8},{5,9},{6,10},{7,11},{20,24},{21,25},{22,26},{23,27}} | collective-permute-start | bytes 393224 | tf_op jit(solution)/shard_map/ppermute | solution.py:578
  55.3 12.4 %collective-permute-start.9 = (f32[2,128,256]{2,1,0:T(8,128)S(1)}, f32[2,128,256]{2,1,0:T(8,128)S(1)}, u32[]{:S(2)}, u32[]{:S(2)}) collective-permute-start(f32[2,128,256]{2,1,0:T(8,128)S(1)} %part.6.refs_0_), channel_id=1, source_target_pairs={{4,0},{8,12},{5,1},{9,13},{6,2},{10,14},{7,3},{11,15},{20,16},{24,... | collective-permute-start | bytes 786440 | tf_op jit(solution)/shard_map/ppermute | solution.py:633
  56.9 4.2 %collective-permute-start.14 = (f32[1,128,256]{2,1,0:T(8,128)S(1)}, f32[1,128,256]{2,1,0:T(8,128)S(1)}, u32[]{:S(2)}, u32[]{:S(2)}) collective-permute-start(f32[1,128,256]{2,1,0:T(8,128)S(1)} %final_state.8.refs_2_.refs_6_), channel_id=1, source_target_pairs={{8,4},{9,5},{10,6},{11,7},{24,20},{25,21},{26,22},{27,23}} | collective-permute-start | bytes 393224 | tf_op jit(solution)/shard_map/ppermute | solution.py:578
  57.7 15.4 %collective-permute-start.13 = (f32[2,128,256]{2,1,0:T(8,128)S(1)}, f32[2,128,256]{2,1,0:T(8,128)S(1)}, u32[]{:S(2)}, u32[]{:S(2)}) collective-permute-start(f32[2,128,256]{2,1,0:T(8,128)S(1)} %part.8.refs_0_), channel_id=1, source_target_pairs={{4,0},{8,12},{5,1},{9,13},{6,2},{10,14},{7,3},{11,15},{20,16},{24,... | collective-permute-start | bytes 786440 | tf_op jit(solution)/shard_map/ppermute | solution.py:633
  59.0 14.0 %collective-permute-start.18 = (f32[1,128,256]{2,1,0:T(8,128)S(1)}, f32[1,128,256]{2,1,0:T(8,128)S(1)}, u32[]{:S(2)}, u32[]{:S(2)}) collective-permute-start(f32[1,128,256]{2,1,0:T(8,128)S(1)} %final_state.9.refs_0_.refs_10_), channel_id=1, source_target_pairs={{8,0},{9,1},{10,2},{11,3},{24,16},{25,17},{26,18},{27,19}} | collective-permute-start | bytes 393224 | tf_op jit(solution)/shard_map/ppermute | solution.py:578
  60.3 12.8 %collective-permute-start.19 = (f32[1,128,256]{2,1,0:T(8,128)S(1)}, f32[1,128,256]{2,1,0:T(8,128)S(1)}, u32[]{:S(2)}, u32[]{:S(2)}) collective-permute-start(f32[1,128,256]{2,1,0:T(8,128)S(1)} %final_state.9.refs_0_.refs_10_), channel_id=1, source_target_pairs={{8,4},{9,5},{10,6},{11,7},{24,20},{25,21},{26,22},{27,23}} | collective-permute-start | bytes 393224 | tf_op jit(solution)/shard_map/ppermute | solution.py:578
  61.0 12.4 %collective-permute-start.15 = (f32[1,128,256]{2,1,0:T(8,128)S(1)}, f32[1,128,256]{2,1,0:T(8,128)S(1)}, u32[]{:S(2)}, u32[]{:S(2)}) collective-permute-start(f32[1,128,256]{2,1,0:T(8,128)S(1)} %part.9.refs_0_), channel_id=1, source_target_pairs={{4,0},{8,12},{5,1},{9,13},{6,2},{10,14},{7,3},{11,15},{20,16},{24,... | collective-permute-start | bytes 393224 | tf_op jit(solution)/shard_map/ppermute | solution.py:633
  67.8 5.7 %collective-permute-start.16 = (f32[1,128,256]{2,1,0:T(8,128)S(1)}, f32[1,128,256]{2,1,0:T(8,128)S(1)}, u32[]{:S(2)}, u32[]{:S(2)}) collective-permute-start(f32[1,128,256]{2,1,0:T(8,128)S(1)} %part.7.refs_0_), channel_id=1, source_target_pairs={{8,12},{9,13},{10,14},{11,15},{24,28},{25,29},{26,30},{27,31}} | collective-permute-start | bytes 393224 | tf_op jit(solution)/shard_map/ppermute | solution.py:578
  73.0 2.0 %collective-permute-start.17 = (f32[4,128,256]{2,1,0:T(8,128)S(1)}, f32[4,128,256]{2,1,0:T(8,128)S(1)}, u32[]{:S(2)}, u32[]{:S(2)}) collective-permute-start(f32[4,128,256]{2,1,0:T(8,128)S(1)} %settle.2.refs_2_.refs_17_), channel_id=1, source_target_pairs={{0,1},{1,0},{2,3},{3,2},{4,5},{5,4},{6,7},{7,6},{8,9},{9,8},{10,11... | collective-permute-start | bytes 1572872 | tf_op jit(solution)/shard_map/ppermute | solution.py:661
  73.2 1.9 %copy-start.6 = (f32[128]{0:T(128)S(1)}, f32[128]{0:T(128)}, u32[]{:S(2)}) copy-start(f32[128]{0:T(128)} %param.24) | copy-start | bytes 1540
  73.6 4.1 %collective-permute-start.20 = (f32[4,128,256]{2,1,0:T(8,128)S(1)}, f32[4,128,256]{2,1,0:T(8,128)S(1)}, u32[]{:S(2)}, u32[]{:S(2)}) collective-permute-start(f32[4,128,256]{2,1,0:T(8,128)S(1)} %settle.3.refs_24_.refs_1_), channel_id=1, source_target_pairs={{0,1},{1,0},{2,3},{3,2},{4,5},{5,4},{6,7},{7,6},{8,9},{9,8},{10,11... | collective-permute-start | bytes 1572872 | tf_op jit(solution)/shard_map/ppermute | solution.py:661
